TPU v7x, 32 devices: a whole 2x2x4 slice. The times are simulated.
32 devices in a mesh: ctx: 8 (over y, x, core), fsdp: 4 (over z).
Axes of the slice: x: 2, y: 2, z: 4, core: 2. Of those that a mesh axis runs over, the one named last changes fastest.
Arguments:
- tokens: float32 [8, 2048, 1024], P('fsdp', 'ctx'), may hold values from -6 to 6
- segments: int32 [8, 2048], P('fsdp', 'ctx'), may hold values from 0 to 2047, as said below
- query_weight: float32 [1024, 1024], P('fsdp'), may hold values from -0.1875 to 0.1875
- query_bias: float32 [1024], P('fsdp'), may hold values from -1.75 to 1.75
- key_weight: float32 [1024, 1024], P('fsdp'), may hold values from -0.1875 to 0.1875
- value_weight: float32 [1024, 1024], P('fsdp'), may hold values from -0.1875 to 0.1875
- value_bias: float32 [1024], P('fsdp'), may hold values from -0.3125 to 0.3125
- output_weight: float32 [1024, 1024], P('fsdp'), may hold values from -2 to 2
- output_bias: float32 [1024], P('fsdp'), may hold values from -1.75 to 1.75
- first_gain: float32 [1024], P('fsdp'), may hold values from 0.5 to 1.5
- first_shift: float32 [1024], P('fsdp'), may hold values from -1.75 to 1.75
- expand_weight: float32 [1024, 4096], P('fsdp'), may hold values from -0.1875 to 0.1875
- expand_bias: float32 [4096], P('fsdp'), may hold values from -1.75 to 1.75
- reduce_weight: float32 [4096, 1024], P('fsdp'), may hold values from -0.09375 to 0.09375
- reduce_bias: float32 [1024], P('fsdp'), may hold values from -1.75 to 1.75
- second_gain: float32 [1024], P('fsdp'), may hold values from 0.5 to 1.5
- second_shift: float32 [1024], P('fsdp'), may hold values from -1.75 to 1.75
- cotangent: float32 [8, 2048, 1024], P('fsdp', 'ctx'), may hold values from -6 to 6
Outputs:
- layer_output: float32 [8, 2048, 1024], P('fsdp', 'ctx')
- grad_tokens: float32 [8, 2048, 1024], P('fsdp', 'ctx')
- grad_query_weight: float32 [1024, 1024], P('fsdp')
- grad_query_bias: float32 [1024], P('fsdp')
- grad_key_weight: float32 [1024, 1024], P('fsdp')
- grad_value_weight: float32 [1024, 1024], P('fsdp')
- grad_value_bias: float32 [1024], P('fsdp')
- grad_output_weight: float32 [1024, 1024], P('fsdp')
- grad_output_bias: float32 [1024], P('fsdp')
- grad_first_gain: float32 [1024], P('fsdp')
- grad_first_shift: float32 [1024], P('fsdp')
- grad_expand_weight: float32 [1024, 4096], P('fsdp')
- grad_expand_bias: float32 [4096], P('fsdp')
- grad_reduce_weight: float32 [4096, 1024], P('fsdp')
- grad_reduce_bias: float32 [1024], P('fsdp')
- grad_second_gain: float32 [1024], P('fsdp')
- grad_second_shift: float32 [1024], P('fsdp')
Inputs may be any that keep to these rules, and one draw needn't show every extreme that they name: `segments`: A token's segment number is the position, within its sequence, of the last token of its document; it never falls along a sequence. Of the 2 sequences at each index of fsdp, one (which one varies) starts with a document of one token at position 0, followed by a document that ends within the last half of 256 positions, with at most one short document after it; in the others every document but the last holds 200 to 2000 tokens.
All inputs are finite; a program needn't handle non-finite values.
Results may differ from a plain program's by a relative error of at most 0.024.
Values may be sent and summed in bfloat16 or wider, within the bound.
No kernel may reach another device: no remote copies, remote signals or barrier semaphores. Data moves between devices by JAX's collectives and lax.ppermute only.
A program may use at most 192 MiB of HBM per device.

v0:
```python
import jax
import jax.numpy as jnp
from jax import lax
from jax.sharding import PartitionSpec as P

HEADS = 16
HEAD = 64


EPS = 1e-05
NEG = -1e30
SQRT_HALF = 0.7071067811865476
DENSITY = 0.3989422804014327


def from_behind(value, axis, steps):
    count = lax.axis_size(axis)
    pairs = [(source, (source + steps) % count) for source in range(count)]
    return lax.ppermute(value, axis, pairs)


def matmul(left, right):
    return jnp.dot(left, right, preferred_element_type=jnp.float32)


def dot_rows(left, right):
    return lax.dot_general(
        left, right, (((0,), (0,)), ((), ())), preferred_element_type=jnp.float32
    )


def dot_back(left, right):
    return lax.dot_general(
        left, right, (((1,), (1,)), ((), ())), preferred_element_type=jnp.float32
    )


def split_heads(values):
    return values.reshape(values.shape[0], values.shape[1], HEADS, HEAD)


def merge_heads(values):
    return values.reshape(values.shape[0], values.shape[1], HEADS * HEAD)


def normalize(values, gain, shift):
    mean = jnp.mean(values, axis=-1, keepdims=True)
    centred = values - mean
    inverse = lax.rsqrt(jnp.mean(centred * centred, axis=-1, keepdims=True) + EPS)
    normed = centred * inverse
    return (normed * gain + shift, normed, inverse)


def normalize_back(grad, normed, inverse, gain):
    scaled = grad * gain
    inner = (
        scaled
        - jnp.mean(scaled, axis=-1, keepdims=True)
        - normed * jnp.mean(scaled * normed, axis=-1, keepdims=True)
    )
    return (inner * inverse, jnp.sum(grad * normed, axis=0), jnp.sum(grad, axis=0))


def attend(state, query, keys, values, seg_query, seg_keys):
    top, denom, accum = state
    scores = jnp.einsum("bqhd,bkhd->bhqk", query, keys, preferred_element_type=jnp.float32)
    mask = (seg_query[:, :, None] == seg_keys[:, None, :])[:, None]
    masked = jnp.where(mask, scores, NEG)
    new_top = jnp.maximum(top, jnp.max(masked, axis=-1))
    weights = jnp.where(mask, jnp.exp(masked - new_top[..., None]), 0.0)
    factor = jnp.exp(top - new_top)
    denom = denom * factor + jnp.sum(weights, axis=-1)
    update = jnp.einsum(
        "bhqk,bkhd->bqhd", weights.astype(jnp.bfloat16), values, preferred_element_type=jnp.float32
    )
    accum = accum * jnp.swapaxes(factor, 1, 2)[..., None] + update
    return (new_top, denom, accum)


def attend_back(query, grad_out, log_total, delta, keys, values, seg_query, seg_keys):
    scores = jnp.einsum("bqhd,bkhd->bhqk", query, keys, preferred_element_type=jnp.float32)
    mask = (seg_query[:, :, None] == seg_keys[:, None, :])[:, None]
    probs = jnp.exp(jnp.where(mask, scores - log_total[..., None], NEG))
    grad_values = jnp.einsum(
        "bhqk,bqhd->bkhd", probs.astype(jnp.bfloat16), grad_out, preferred_element_type=jnp.float32
    )
    grad_probs = jnp.einsum("bqhd,bkhd->bhqk", grad_out, values, preferred_element_type=jnp.float32)
    grad_scores = (probs * (grad_probs - delta[..., None])).astype(jnp.bfloat16)
    grad_query = jnp.einsum(
        "bhqk,bkhd->bqhd", grad_scores, keys, preferred_element_type=jnp.float32
    )
    grad_keys = jnp.einsum(
        "bhqk,bqhd->bkhd", grad_scores, query, preferred_element_type=jnp.float32
    )
    return (grad_query, grad_keys, grad_values)


def block_segments(seg_all, offset, rows):
    count = lax.axis_size("ctx")
    source = (lax.axis_index("ctx") - offset) % count
    return lax.dynamic_slice_in_dim(seg_all, source * rows, rows, 1)


def context_stepwise(query, stacked, seg_query, seg_all, state):
    count = lax.axis_size("ctx")
    rows = stacked.shape[2]

    def apply(held, offset, current):
        seg_keys = block_segments(seg_all, offset, rows)
        return attend(
            current, query, split_heads(held[0]), split_heads(held[1]), seg_query, seg_keys
        )

    def turn(offset, carry):
        current, held = carry
        current = apply(held, offset, current)
        held = from_behind(held, "ctx", 1)
        return (current, held)

    state, held = lax.fori_loop(0, count - 1, turn, (state, stacked))
    return apply(held, count - 1, state)


def pass_grads(grads):
    return from_behind(grads.astype(jnp.bfloat16), "ctx", 1).astype(grads.dtype)


def context_back(query, grad_out, log_total, delta, stacked, seg_query, seg_all):
    count = lax.axis_size("ctx")
    rows = stacked.shape[2]

    def apply(held, offset):
        seg_keys = block_segments(seg_all, offset, rows)
        return attend_back(
            query,
            grad_out,
            log_total,
            delta,
            split_heads(held[0]),
            split_heads(held[1]),
            seg_query,
            seg_keys,
        )

    def turn(offset, carry):
        grad_query, held, grads = carry
        part_query, part_keys, part_values = apply(held, offset)
        grads = pass_grads(grads + jnp.stack([merge_heads(part_keys), merge_heads(part_values)]))
        held = from_behind(held, "ctx", 1)
        return (grad_query + part_query, held, grads)

    start_query = jnp.zeros(query.shape, jnp.float32)
    start_grads = jnp.zeros(stacked.shape, jnp.float32)
    grad_query, held, grads = lax.fori_loop(0, count - 1, turn, (start_query, stacked, start_grads))
    part_query, part_keys, part_values = apply(held, count - 1)
    grads = pass_grads(grads + jnp.stack([merge_heads(part_keys), merge_heads(part_values)]))
    return (grad_query + part_query, grads)


def gather_attention(query_weight, key_weight, value_weight, output_weight):
    return (
        lax.all_gather(query_weight.astype(jnp.bfloat16), "fsdp", axis=0, tiled=True),
        lax.all_gather(key_weight.astype(jnp.bfloat16), "fsdp", axis=0, tiled=True),
        lax.all_gather(value_weight.astype(jnp.bfloat16), "fsdp", axis=0, tiled=True),
        lax.all_gather(output_weight.astype(jnp.bfloat16), "fsdp", axis=0, tiled=True),
    )


def gather_feedforward(expand_weight, reduce_weight):
    return (
        lax.all_gather(expand_weight.astype(jnp.bfloat16), "fsdp", axis=0, tiled=True),
        lax.all_gather(reduce_weight.astype(jnp.bfloat16), "fsdp", axis=0, tiled=True),
    )


def attention_later(query_weight, key_weight, value_weight, output_weight):
    return (
        lax.all_gather(query_weight.astype(jnp.bfloat16), "fsdp", axis=0, tiled=True),
        lax.all_gather(key_weight.astype(jnp.bfloat16), "fsdp", axis=0, tiled=True),
        lax.all_gather(value_weight.astype(jnp.bfloat16), "fsdp", axis=0, tiled=True),
        lax.all_gather(output_weight.astype(jnp.bfloat16), "fsdp", axis=0, tiled=True),
    )


def feedforward_later(expand_weight, reduce_weight):
    return (
        lax.all_gather(expand_weight.astype(jnp.bfloat16), "fsdp", axis=0, tiled=True),
        lax.all_gather(reduce_weight.astype(jnp.bfloat16), "fsdp", axis=0, tiled=True),
    )


def body(
    tokens,
    segments,
    query_weight,
    query_bias,
    key_weight,
    value_weight,
    value_bias,
    output_weight,
    output_bias,
    first_gain,
    first_shift,
    expand_weight,
    expand_bias,
    reduce_weight,
    reduce_bias,
    second_gain,
    second_shift,
    cotangent,
):
    batch, rows, width = tokens.shape
    total_rows = batch * rows
    scale = HEAD ** (-0.5)
    full_query, full_key, full_value, full_output = gather_attention(
        query_weight, key_weight, value_weight, output_weight
    )
    full_expand, full_reduce = gather_feedforward(expand_weight, reduce_weight)
    (
        bias_query,
        bias_value,
        bias_output,
        gain_first,
        shift_first,
        bias_expand,
        bias_reduce,
        gain_second,
        shift_second,
    ) = (
        lax.all_gather(query_bias, "fsdp", axis=0, tiled=True),
        lax.all_gather(value_bias, "fsdp", axis=0, tiled=True),
        lax.all_gather(output_bias, "fsdp", axis=0, tiled=True),
        lax.all_gather(first_gain, "fsdp", axis=0, tiled=True),
        lax.all_gather(first_shift, "fsdp", axis=0, tiled=True),
        lax.all_gather(expand_bias, "fsdp", axis=0, tiled=True),
        lax.all_gather(reduce_bias, "fsdp", axis=0, tiled=True),
        lax.all_gather(second_gain, "fsdp", axis=0, tiled=True),
        lax.all_gather(second_shift, "fsdp", axis=0, tiled=True),
    )
    seg_all = lax.all_gather(segments, "ctx", axis=1, tiled=True)
    flat_in = tokens.reshape(total_rows, width)
    low_in = flat_in.astype(jnp.bfloat16)
    query = ((matmul(low_in, full_query) + bias_query) * scale).astype(jnp.bfloat16)
    keys = matmul(low_in, full_key).astype(jnp.bfloat16)
    values = (matmul(low_in, full_value) + bias_value).astype(jnp.bfloat16)
    query_heads = split_heads(query.reshape(batch, rows, width))
    stacked = jnp.stack([keys.reshape(batch, rows, width), values.reshape(batch, rows, width)])
    start_state = (
        jnp.full((batch, HEADS, rows), NEG, jnp.float32),
        jnp.zeros((batch, HEADS, rows), jnp.float32),
        jnp.zeros((batch, rows, HEADS, HEAD), jnp.float32),
    )
    top, denom, accum = context_stepwise(query_heads, stacked, segments, seg_all, start_state)
    context = accum / jnp.swapaxes(denom, 1, 2)[..., None]
    log_total = top + jnp.log(denom)
    context_low = context.reshape(total_rows, width).astype(jnp.bfloat16)
    branch = matmul(context_low, full_output) + bias_output
    hidden, normed_first, inverse_first = normalize(flat_in + branch, gain_first, shift_first)
    hidden_low = hidden.astype(jnp.bfloat16)
    expand = matmul(hidden_low, full_expand) + bias_expand
    normal_cdf = 0.5 * (1.0 + lax.erf(expand * SQRT_HALF))
    active_low = (expand * normal_cdf).astype(jnp.bfloat16)
    reduced = matmul(active_low, full_reduce) + bias_reduce
    result, normed_second, inverse_second = normalize(hidden + reduced, gain_second, shift_second)
    full_query, full_key, full_value, full_output = attention_later(
        query_weight, key_weight, value_weight, output_weight
    )
    full_expand, full_reduce = feedforward_later(expand_weight, reduce_weight)
    grad_out = cotangent.reshape(total_rows, width)
    grad_sum_second, grad_gain_second, grad_shift_second = normalize_back(
        grad_out, normed_second, inverse_second, gain_second
    )
    grad_reduced = grad_sum_second.astype(jnp.bfloat16)
    grad_bias_reduce = jnp.sum(grad_reduced.astype(jnp.float32), axis=0)
    grad_active = dot_back(grad_reduced, full_reduce)
    slope = normal_cdf + expand * DENSITY * jnp.exp(-0.5 * expand * expand)
    grad_expand = (grad_active * slope).astype(jnp.bfloat16)
    grad_bias_expand = jnp.sum(grad_expand.astype(jnp.float32), axis=0)
    grad_hidden = grad_sum_second + dot_back(grad_expand, full_expand)
    grad_pre, grad_gain_first, grad_shift_first = normalize_back(
        grad_hidden, normed_first, inverse_first, gain_first
    )
    grad_branch = grad_pre.astype(jnp.bfloat16)
    grad_bias_output = jnp.sum(grad_branch.astype(jnp.float32), axis=0)
    grad_context = dot_back(grad_branch, full_output).astype(jnp.bfloat16)
    grad_context_heads = split_heads(grad_context.reshape(batch, rows, width))
    delta = jnp.einsum("bqhd,bqhd->bhq", grad_context_heads.astype(jnp.float32), context)
    grad_query_heads, grads_home = context_back(
        query_heads, grad_context_heads, log_total, delta, stacked, segments, seg_all
    )
    grad_query_low = grad_query_heads.reshape(total_rows, width).astype(jnp.bfloat16) * scale
    grad_keys_low = grads_home[0].reshape(total_rows, width).astype(jnp.bfloat16)
    grad_values_low = grads_home[1].reshape(total_rows, width).astype(jnp.bfloat16)
    grad_bias_query = jnp.sum(grad_query_low.astype(jnp.float32), axis=0)
    grad_bias_value = jnp.sum(grad_values_low.astype(jnp.float32), axis=0)
    grad_in = (
        grad_pre
        + dot_back(grad_query_low, full_query)
        + dot_back(grad_keys_low, full_key)
        + dot_back(grad_values_low, full_value)
    )
    projected = jnp.concatenate([grad_query_low, grad_keys_low, grad_values_low], axis=1)
    row_grads = lax.psum_scatter(
        jnp.concatenate(
            [
                dot_rows(low_in, projected),
                dot_rows(context_low, grad_branch),
                dot_rows(hidden_low, grad_expand),
            ],
            axis=1,
        ).astype(jnp.bfloat16),
        "fsdp",
        scatter_dimension=0,
        tiled=True,
    )
    hidden_grads = lax.psum_scatter(
        dot_rows(active_low, grad_reduced).astype(jnp.bfloat16),
        "fsdp",
        scatter_dimension=0,
        tiled=True,
    )
    small = (
        lax.psum_scatter(
            grad_bias_query.astype(jnp.bfloat16), "fsdp", scatter_dimension=0, tiled=True
        ).astype(jnp.float32),
        lax.psum_scatter(
            grad_bias_value.astype(jnp.bfloat16), "fsdp", scatter_dimension=0, tiled=True
        ).astype(jnp.float32),
        lax.psum_scatter(
            grad_bias_output.astype(jnp.bfloat16), "fsdp", scatter_dimension=0, tiled=True
        ).astype(jnp.float32),
        lax.psum_scatter(
            grad_gain_first.astype(jnp.bfloat16), "fsdp", scatter_dimension=0, tiled=True
        ).astype(jnp.float32),
        lax.psum_scatter(
            grad_shift_first.astype(jnp.bfloat16), "fsdp", scatter_dimension=0, tiled=True
        ).astype(jnp.float32),
        lax.psum_scatter(
            grad_bias_expand.astype(jnp.bfloat16), "fsdp", scatter_dimension=0, tiled=True
        ).astype(jnp.float32),
        lax.psum_scatter(
            grad_bias_reduce.astype(jnp.bfloat16), "fsdp", scatter_dimension=0, tiled=True
        ).astype(jnp.float32),
        lax.psum_scatter(
            grad_gain_second.astype(jnp.bfloat16), "fsdp", scatter_dimension=0, tiled=True
        ).astype(jnp.float32),
        lax.psum_scatter(
            grad_shift_second.astype(jnp.bfloat16), "fsdp", scatter_dimension=0, tiled=True
        ).astype(jnp.float32),
    )
    summed = (
        lax.psum(row_grads, "ctx").astype(jnp.float32),
        lax.psum(hidden_grads, "ctx").astype(jnp.float32),
        lax.psum(small[0].astype(jnp.bfloat16), "ctx").astype(jnp.float32),
        lax.psum(small[1].astype(jnp.bfloat16), "ctx").astype(jnp.float32),
        lax.psum(small[2].astype(jnp.bfloat16), "ctx").astype(jnp.float32),
        lax.psum(small[3].astype(jnp.bfloat16), "ctx").astype(jnp.float32),
        lax.psum(small[4].astype(jnp.bfloat16), "ctx").astype(jnp.float32),
        lax.psum(small[5].astype(jnp.bfloat16), "ctx").astype(jnp.float32),
        lax.psum(small[6].astype(jnp.bfloat16), "ctx").astype(jnp.float32),
        lax.psum(small[7].astype(jnp.bfloat16), "ctx").astype(jnp.float32),
        lax.psum(small[8].astype(jnp.bfloat16), "ctx").astype(jnp.float32),
    )
    row_total = summed[0]
    return (
        result.reshape(batch, rows, width),
        grad_in.reshape(batch, rows, width),
        row_total[:, :width],
        summed[2],
        row_total[:, width : 2 * width],
        row_total[:, 2 * width : 3 * width],
        summed[3],
        row_total[:, 3 * width : 4 * width],
        summed[4],
        summed[5],
        summed[6],
        row_total[:, 4 * width :],
        summed[7],
        summed[1],
        summed[8],
        summed[9],
        summed[10],
    )


def solution(mesh):
    in_specs = (
        P("fsdp", "ctx", None),
        P("fsdp", "ctx"),
        P("fsdp", None),
        P("fsdp"),
        P("fsdp", None),
        P("fsdp", None),
        P("fsdp"),
        P("fsdp", None),
        P("fsdp"),
        P("fsdp"),
        P("fsdp"),
        P("fsdp", None),
        P("fsdp"),
        P("fsdp", None),
        P("fsdp"),
        P("fsdp"),
        P("fsdp"),
        P("fsdp", "ctx", None),
    )
    out_specs = (
        P("fsdp", "ctx", None),
        P("fsdp", "ctx", None),
        P("fsdp", None),
        P("fsdp"),
        P("fsdp", None),
        P("fsdp", None),
        P("fsdp"),
        P("fsdp", None),
        P("fsdp"),
        P("fsdp"),
        P("fsdp"),
        P("fsdp", None),
        P("fsdp"),
        P("fsdp", None),
        P("fsdp"),
        P("fsdp"),
        P("fsdp"),
    )
    return jax.shard_map(body, mesh=mesh, in_specs=in_specs, out_specs=out_specs, check_vma=False)
```

profile of v0, /device:TPU:0, one launch (start us, length us, event | category | flops | bytes accessed | tf_op | source)
XLA Modules:
  0.0 1533.3 jit_solution(3876228814544696402)
XLA Ops:
  20.9 11.5 all_gather.57
  35.0 11.3 all-gather
  46.4 7.6 all-gather.1
  54.0 10.5 all-gather.2
  64.5 7.6 all-gather.3
  72.2 10.3 all-gather.4
  82.4 13.9 all_gather.65
  96.3 7.8 all-gather.5
  104.1 9.7 all-gather.6
  113.8 7.8 all-gather.7
  136.3 16.9 %all-gather.19.cloned.1.call-done = bf16[1024,1024]{1,0:T(8,128)(2,1)} async-done(((bf16[256,1024]{1,0:T(8,128)(2,1)}), bf16[1024,1024]{1,0:T(8,128)(2,1)}) %all-gather.19.cloned.1.call-update) | async-done | bytes 2097168 | tf_op jit(solution)/shard_map/all_gather | solution.py:162
  159.1 196.7 %while.42 = (s32[]{:T(128)}, f32[2,16,256]{2,1,0:T(8,128)S(1)}, f32[2,16,256]{2,1,0:T(8,128)S(1)}, f32[2,256,16,64]{1,3,2,0:T(8,128)}, bf16[2,2,256,1024]{2,3,1,...) while((s32[]{:T(128)}, f32[2,16,256]{2,1,0:T(8,128)S(1)}, ...), condition=%wide.region_3.4_spmd.clone, body=%wide.region_0.3_spmd.clone.sunk | while | flops 559595520 | bytes 50471340 | solution.py:120
  163.1 5.9 select_reduce_fusion.3
  174.8 7.0 bitcast_add_fusion.7
  191.1 5.9 select_reduce_fusion.3
  202.9 7.7 bitcast_add_fusion.7
  219.2 5.9 select_reduce_fusion.3
  231.0 7.7 bitcast_add_fusion.7
  247.3 5.8 select_reduce_fusion.3
  259.0 7.7 bitcast_add_fusion.7
  275.3 5.9 select_reduce_fusion.3
  287.1 7.7 bitcast_add_fusion.7
  303.4 5.9 select_reduce_fusion.3
  315.1 7.6 bitcast_add_fusion.7
  331.5 5.9 select_reduce_fusion.3
  343.2 7.6 bitcast_add_fusion.7
  371.2 10.5 multiply_convert_fusion.2
  381.7 117.9 %all-gather.25.cloned.1.call-done = bf16[4096,1024]{1,0:T(8,128)(2,1)} async-done(((bf16[1024,1024]{1,0:T(8,128)(2,1)}), bf16[4096,1024]{1,0:T(8,128)(2,1)}) %all-gather.25.cloned.1.call-update) | async-done | bytes 8388624 | tf_op jit(solution)/shard_map/all_gather | solution.py:172
  499.6 8.9 fusion.77
  514.1 13.6 fusion.79
  527.7 7.8 multiply_reduce_fusion.1
  542.7 9.1 convolution_convert_fusion
  554.6 480.9 %while.43 = (s32[]{:T(128)}, f32[2,256,16,64]{1,3,2,0:T(8,128)}, bf16[2,2,256,1024]{2,3,1,0:T(8,128)(2,1)}, f32[2,2,256,1024]{2,3,1,0:T(8,128)}, s32[2,256]{1,0:...) while((s32[]{:T(128)}, f32[2,256,16,64]{1,3,2,0:T(8,128)}, ...), condition=%wide.region_15.16_spmd.clone, body=%wide.region_14.15_spmd.clone.sunk | while | flops 1365377024 | bytes 133669400 | solution.py:154
  580.9 20.2 %collective-permute-done.2 = bf16[2,2,256,1024]{2,3,1,0:T(8,128)(2,1)} collective-permute-done((bf16[2,2,256,1024]{2,3,1,0:T(8,128)(2,1)}, bf16[2,2,256,1024]{2,3,1,0:T(8,128)(2,1)}, u32[]{:S(2)}, u32[]{:S(2)}) %collective-permute-start.2) | collective-permute-done | bytes 2097184 | tf_op jit(solution)/shard_map/while/body/eval_jaxpr/ppermute | solution.py:19
  605.1 18.5 %collective-permute-done.1 = bf16[2,2,256,1024]{2,3,1,0:T(8,128)(2,1)} collective-permute-done((bf16[2,2,256,1024]{2,3,1,0:T(8,128)(2,1)}, bf16[2,2,256,1024]{2,3,1,0:T(8,128)(2,1)}, u32[]{:S(2)}, u32[]{:S(2)}) %collective-permute-start.1) | collective-permute-done | bytes 2097184 | tf_op jit(solution)/shard_map/while/body/eval_jaxpr/ppermute | solution.py:19
  643.6 5.6 bitcast_add_fusion.8
  649.2 20.7 %collective-permute-done.2 = bf16[2,2,256,1024]{2,3,1,0:T(8,128)(2,1)} collective-permute-done((bf16[2,2,256,1024]{2,3,1,0:T(8,128)(2,1)}, bf16[2,2,256,1024]{2,3,1,0:T(8,128)(2,1)}, u32[]{:S(2)}, u32[]{:S(2)}) %collective-permute-start.2) | collective-permute-done | bytes 2097184 | tf_op jit(solution)/shard_map/while/body/eval_jaxpr/ppermute | solution.py:19
  674.0 18.5 %collective-permute-done.1 = bf16[2,2,256,1024]{2,3,1,0:T(8,128)(2,1)} collective-permute-done((bf16[2,2,256,1024]{2,3,1,0:T(8,128)(2,1)}, bf16[2,2,256,1024]{2,3,1,0:T(8,128)(2,1)}, u32[]{:S(2)}, u32[]{:S(2)}) %collective-permute-start.1) | collective-permute-done | bytes 2097184 | tf_op jit(solution)/shard_map/while/body/eval_jaxpr/ppermute | solution.py:19
  711.9 5.6 bitcast_add_fusion.8
  717.4 21.1 %collective-permute-done.2 = bf16[2,2,256,1024]{2,3,1,0:T(8,128)(2,1)} collective-permute-done((bf16[2,2,256,1024]{2,3,1,0:T(8,128)(2,1)}, bf16[2,2,256,1024]{2,3,1,0:T(8,128)(2,1)}, u32[]{:S(2)}, u32[]{:S(2)}) %collective-permute-start.2) | collective-permute-done | bytes 2097184 | tf_op jit(solution)/shard_map/while/body/eval_jaxpr/ppermute | solution.py:19
  742.5 18.5 %collective-permute-done.1 = bf16[2,2,256,1024]{2,3,1,0:T(8,128)(2,1)} collective-permute-done((bf16[2,2,256,1024]{2,3,1,0:T(8,128)(2,1)}, bf16[2,2,256,1024]{2,3,1,0:T(8,128)(2,1)}, u32[]{:S(2)}, u32[]{:S(2)}) %collective-permute-start.1) | collective-permute-done | bytes 2097184 | tf_op jit(solution)/shard_map/while/body/eval_jaxpr/ppermute | solution.py:19
  780.5 5.6 bitcast_add_fusion.8
  786.0 21.1 %collective-permute-done.2 = bf16[2,2,256,1024]{2,3,1,0:T(8,128)(2,1)} collective-permute-done((bf16[2,2,256,1024]{2,3,1,0:T(8,128)(2,1)}, bf16[2,2,256,1024]{2,3,1,0:T(8,128)(2,1)}, u32[]{:S(2)}, u32[]{:S(2)}) %collective-permute-start.2) | collective-permute-done | bytes 2097184 | tf_op jit(solution)/shard_map/while/body/eval_jaxpr/ppermute | solution.py:19
  811.1 18.5 %collective-permute-done.1 = bf16[2,2,256,1024]{2,3,1,0:T(8,128)(2,1)} collective-permute-done((bf16[2,2,256,1024]{2,3,1,0:T(8,128)(2,1)}, bf16[2,2,256,1024]{2,3,1,0:T(8,128)(2,1)}, u32[]{:S(2)}, u32[]{:S(2)}) %collective-permute-start.1) | collective-permute-done | bytes 2097184 | tf_op jit(solution)/shard_map/while/body/eval_jaxpr/ppermute | solution.py:19
  849.1 5.6 bitcast_add_fusion.8
  854.6 21.1 %collective-permute-done.2 = bf16[2,2,256,1024]{2,3,1,0:T(8,128)(2,1)} collective-permute-done((bf16[2,2,256,1024]{2,3,1,0:T(8,128)(2,1)}, bf16[2,2,256,1024]{2,3,1,0:T(8,128)(2,1)}, u32[]{:S(2)}, u32[]{:S(2)}) %collective-permute-start.2) | collective-permute-done | bytes 2097184 | tf_op jit(solution)/shard_map/while/body/eval_jaxpr/ppermute | solution.py:19
  879.7 18.5 %collective-permute-done.1 = bf16[2,2,256,1024]{2,3,1,0:T(8,128)(2,1)} collective-permute-done((bf16[2,2,256,1024]{2,3,1,0:T(8,128)(2,1)}, bf16[2,2,256,1024]{2,3,1,0:T(8,128)(2,1)}, u32[]{:S(2)}, u32[]{:S(2)}) %collective-permute-start.1) | collective-permute-done | bytes 2097184 | tf_op jit(solution)/shard_map/while/body/eval_jaxpr/ppermute | solution.py:19
  917.7 5.6 bitcast_add_fusion.8
  923.3 21.1 %collective-permute-done.2 = bf16[2,2,256,1024]{2,3,1,0:T(8,128)(2,1)} collective-permute-done((bf16[2,2,256,1024]{2,3,1,0:T(8,128)(2,1)}, bf16[2,2,256,1024]{2,3,1,0:T(8,128)(2,1)}, u32[]{:S(2)}, u32[]{:S(2)}) %collective-permute-start.2) | collective-permute-done | bytes 2097184 | tf_op jit(solution)/shard_map/while/body/eval_jaxpr/ppermute | solution.py:19
  948.3 18.5 %collective-permute-done.1 = bf16[2,2,256,1024]{2,3,1,0:T(8,128)(2,1)} collective-permute-done((bf16[2,2,256,1024]{2,3,1,0:T(8,128)(2,1)}, bf16[2,2,256,1024]{2,3,1,0:T(8,128)(2,1)}, u32[]{:S(2)}, u32[]{:S(2)}) %collective-permute-start.1) | collective-permute-done | bytes 2097184 | tf_op jit(solution)/shard_map/while/body/eval_jaxpr/ppermute | solution.py:19
  986.3 5.6 bitcast_add_fusion.8
  991.9 21.1 %collective-permute-done.2 = bf16[2,2,256,1024]{2,3,1,0:T(8,128)(2,1)} collective-permute-done((bf16[2,2,256,1024]{2,3,1,0:T(8,128)(2,1)}, bf16[2,2,256,1024]{2,3,1,0:T(8,128)(2,1)}, u32[]{:S(2)}, u32[]{:S(2)}) %collective-permute-start.2) | collective-permute-done | bytes 2097184 | tf_op jit(solution)/shard_map/while/body/eval_jaxpr/ppermute | solution.py:19
  1016.9 18.5 %collective-permute-done.1 = bf16[2,2,256,1024]{2,3,1,0:T(8,128)(2,1)} collective-permute-done((bf16[2,2,256,1024]{2,3,1,0:T(8,128)(2,1)}, bf16[2,2,256,1024]{2,3,1,0:T(8,128)(2,1)}, u32[]{:S(2)}, u32[]{:S(2)}) %collective-permute-start.1) | collective-permute-done | bytes 2097184 | tf_op jit(solution)/shard_map/while/body/eval_jaxpr/ppermute | solution.py:19
  1047.3 6.4 fusion.32
  1056.6 5.7 copy.105
  1076.3 10.8 convolution_convert_fusion.1
  1087.1 7.0 collective-permute-done.3
  1100.5 8.3 convert_bitcast_fusion
  1108.8 8.7 copy.108
  1117.5 12.8 pad_maximum_fusion
  1130.4 277.9 %reduce-scatter.3.cloned.1.call-done = bf16[256,8192]{1,0:T(8,128)(2,1)} async-done(((bf16[1024,8192]{1,0:T(8,128)(2,1)}), bf16[256,8192]{1,0:T(8,128)(2,1)}) %reduce-scatter.3.cloned.1.call-update) | async-done | bytes 4194320 | tf_op jit(solution)/shard_map/reduce_scatter | solution.py:303
  1415.3 18.5 %all-reduce.11 = (bf16[1024]{0:T(1024)(128)(2,1)S(1)}, bf16[1024]{0:T(1024)(128)(2,1)S(1)}, bf16[1024]{0:T(1024)(128)(2,1)S(1)}, bf16[1024]{0:T(1024)(128)(2,1)S...) all-reduce(bf16[1024]{0:T(1024)(128)(2,1)S(1)} %reduce_sum.205, ...), channel_id=3, replica_groups=mesh['ctx'=8,'fsdp'=4] {'fsdp'}, use_global_device_ids=true, to_apply=%region_19.20.clone | all-reduce | flops 12288 | bytes 49152
  1434.4 13.3 all-reduce.9
  1459.0 58.6 %all-reduce.14.cloned.1.call-done = (bf16[256,8192]{1,0:T(8,128)(2,1)}, bf16[1024,1024]{1,0:T(8,128)(2,1)}) async-done(((bf16[256,8192]{1,0:T(8,128)(2,1)}, bf16[1024,1024]{1,0:T(8,128)(2,1)}), (bf16[256,8192]{1,0:T(8,128)(2,1)}, bf16[1024,1024]{1,0:T(8,128)(2,1)})) %all-reduce.14.cloned.1.call-update) | async-done | bytes 6291472 | tf_op jit(solution)/shard_map/psum | solution.py:352
  (453 shorter events, 401.9 us)
Async XLA Ops:
  7.2 115.9 %all-gather.17.cloned.1.call-start = ((), (), s32[]{:S(2)}) async-start(), calls=%async_computation.3 | async-start | bytes 2621440 | tf_op jit(solution)/shard_map/all_gather | solution.py:164
  9.5 117.0 %all-gather.15.cloned.1.call-start = ((), (), s32[]{:S(2)}) async-start(), calls=%async_computation.2 | async-start | bytes 2621440 | tf_op jit(solution)/shard_map/all_gather | solution.py:163
  10.5 142.7 %all-gather.19.cloned.1.call-start = ((), (), s32[]{:S(2)}) async-start(), calls=%async_computation.4 | async-start | bytes 2621440 | tf_op jit(solution)/shard_map/all_gather | solution.py:162
  11.4 355.1 %all-gather.21.cloned.1.call-start = ((), (), s32[]{:S(2)}) async-start(), calls=%async_computation.5 | async-start | bytes 2621440 | tf_op jit(solution)/shard_map/all_gather | solution.py:165
  12.4 358.5 %all-gather.23.cloned.1.call-start = ((), (), s32[]{:S(2)}) async-start(), calls=%async_computation.6 | async-start | bytes 10485760 | tf_op jit(solution)/shard_map/all_gather | solution.py:171
  16.3 483.3 %all-gather.25.cloned.1.call-start = ((), (), s32[]{:S(2)}) async-start(), calls=%async_computation.7 | async-start | bytes 10485760 | tf_op jit(solution)/shard_map/all_gather | solution.py:172
  20.2 14.8 copy-start.53
  20.2 26.2 %copy-start.54 = (f32[256]{0:T(256)S(1)}, f32[256]{0:T(256)}, u32[]{:S(2)}) copy-start(f32[256]{0:T(256)} %param.25) | copy-start | bytes 3076
  20.2 33.8 %copy-start.55 = (f32[256]{0:T(256)S(1)}, f32[256]{0:T(256)}, u32[]{:S(2)}) copy-start(f32[256]{0:T(256)} %param.30) | copy-start | bytes 3076
  20.2 44.3 %copy-start.56 = (f32[256]{0:T(256)S(1)}, f32[256]{0:T(256)}, u32[]{:S(2)}) copy-start(f32[256]{0:T(256)} %param.31) | copy-start | bytes 3076
  20.2 51.9 %copy-start.57 = (f32[256]{0:T(256)S(1)}, f32[256]{0:T(256)}, u32[]{:S(2)}) copy-start(f32[256]{0:T(256)} %param.32) | copy-start | bytes 3076
  20.3 62.2 %copy-start.46 = (f32[1024]{0:T(1024)S(1)}, f32[1024]{0:T(1024)}, u32[]{:S(2)}) copy-start(f32[1024]{0:T(1024)} %param.34) | copy-start | bytes 12292
  20.3 76.0 %copy-start.58 = (f32[256]{0:T(256)S(1)}, f32[256]{0:T(256)}, u32[]{:S(2)}) copy-start(f32[256]{0:T(256)} %param.36) | copy-start | bytes 3076
  20.3 83.8 %copy-start.59 = (f32[256]{0:T(256)S(1)}, f32[256]{0:T(256)}, u32[]{:S(2)}) copy-start(f32[256]{0:T(256)} %param.37) | copy-start | bytes 3076
  20.3 93.5 %copy-start.60 = (f32[256]{0:T(256)S(1)}, f32[256]{0:T(256)}, u32[]{:S(2)}) copy-start(f32[256]{0:T(256)} %param.38) | copy-start | bytes 3076
  20.3 101.3 %copy-start.5 = (f32[2,256,1024]{2,1,0:T(8,128)S(1)}, f32[2,256,1024]{2,1,0:T(8,128)}, u32[]{:S(2)}) copy-start(f32[2,256,1024]{2,1,0:T(8,128)} %param.39) | copy-start | bytes 6291460
  20.3 1110.1 %reduce-scatter.5.cloned.1.call-start = ((), (), s32[]{:S(2)}) async-start(), calls=%async_computation.9 | async-start | bytes 10485760 | tf_op jit(solution)/shard_map/reduce_scatter | solution.py:316
  33.2 327.9 %copy-start.18 = (pred[2,256,256]{1,2,0:T(8,128)(4,1)}, pred[2,256,256]{1,2,0:T(8,128)(4,1)S(1)}, u32[]{:S(2)}) copy-start(pred[2,256,256]{1,2,0:T(8,128)(4,1)S(1)} %broadcast_compare_fusion.2) | copy-start | bytes 393220
  35.0 118.2 %copy-start.25 = (bf16[512,1024]{1,0:T(8,128)(2,1)}, bf16[512,1024]{1,0:T(8,128)(2,1)S(1)}, u32[]{:S(2)}) copy-start(bf16[512,1024]{1,0:T(8,128)(2,1)S(1)} %bitcast_convert_fusion) | copy-start | bytes 3145732
  72.1 463.3 %copy-start.35 = (f32[4,1,256]{2,1,0:T(1,128)}, f32[4,1,256]{2,1,0:T(1,128)S(1)}, u32[]{:S(2)}) copy-start(f32[4,1,256]{2,1,0:T(1,128)S(1)} %all-gather.3) | copy-start | bytes 12292
  160.8 26.5 %collective-permute-start = (bf16[2,2,256,1024]{2,3,1,0:T(8,128)(2,1)S(1)}, bf16[2,2,256,1024]{2,3,1,0:T(8,128)(2,1)}, u32[]{:S(2)}, u32[]{:S(2)}) collective-permute-start(bf16[2,2,256,1024]{2,3,1,0:T(8,128)(2,1)S(1)} %copy.142), channel_id=1, source_target_pairs={{0,4},{4,8},{8,12},{12,16},{16,20},{20,24},{24,28},{28,0},{1,5},{5... | collective-permute-start | bytes 6291464 | tf_op jit(solution)/shard_map/while/body/eval_jaxpr/ppermute | solution.py:19
  169.6 5.2 copy-start.31
  188.9 26.5 %collective-permute-start = (bf16[2,2,256,1024]{2,3,1,0:T(8,128)(2,1)S(1)}, bf16[2,2,256,1024]{2,3,1,0:T(8,128)(2,1)}, u32[]{:S(2)}, u32[]{:S(2)}) collective-permute-start(bf16[2,2,256,1024]{2,3,1,0:T(8,128)(2,1)S(1)} %copy.142), channel_id=1, source_target_pairs={{0,4},{4,8},{8,12},{12,16},{16,20},{20,24},{24,28},{28,0},{1,5},{5... | collective-permute-start | bytes 6291464 | tf_op jit(solution)/shard_map/while/body/eval_jaxpr/ppermute | solution.py:19
  197.6 5.2 copy-start.31
  216.9 26.5 %collective-permute-start = (bf16[2,2,256,1024]{2,3,1,0:T(8,128)(2,1)S(1)}, bf16[2,2,256,1024]{2,3,1,0:T(8,128)(2,1)}, u32[]{:S(2)}, u32[]{:S(2)}) collective-permute-start(bf16[2,2,256,1024]{2,3,1,0:T(8,128)(2,1)S(1)} %copy.142), channel_id=1, source_target_pairs={{0,4},{4,8},{8,12},{12,16},{16,20},{20,24},{24,28},{28,0},{1,5},{5... | collective-permute-start | bytes 6291464 | tf_op jit(solution)/shard_map/while/body/eval_jaxpr/ppermute | solution.py:19
  225.7 5.3 copy-start.31
  245.0 26.5 %collective-permute-start = (bf16[2,2,256,1024]{2,3,1,0:T(8,128)(2,1)S(1)}, bf16[2,2,256,1024]{2,3,1,0:T(8,128)(2,1)}, u32[]{:S(2)}, u32[]{:S(2)}) collective-permute-start(bf16[2,2,256,1024]{2,3,1,0:T(8,128)(2,1)S(1)} %copy.142), channel_id=1, source_target_pairs={{0,4},{4,8},{8,12},{12,16},{16,20},{20,24},{24,28},{28,0},{1,5},{5... | collective-permute-start | bytes 6291464 | tf_op jit(solution)/shard_map/while/body/eval_jaxpr/ppermute | solution.py:19
  253.8 5.3 copy-start.31
  273.1 26.5 %collective-permute-start = (bf16[2,2,256,1024]{2,3,1,0:T(8,128)(2,1)S(1)}, bf16[2,2,256,1024]{2,3,1,0:T(8,128)(2,1)}, u32[]{:S(2)}, u32[]{:S(2)}) collective-permute-start(bf16[2,2,256,1024]{2,3,1,0:T(8,128)(2,1)S(1)} %copy.142), channel_id=1, source_target_pairs={{0,4},{4,8},{8,12},{12,16},{16,20},{20,24},{24,28},{28,0},{1,5},{5... | collective-permute-start | bytes 6291464 | tf_op jit(solution)/shard_map/while/body/eval_jaxpr/ppermute | solution.py:19
  281.8 5.3 copy-start.31
  301.1 26.5 %collective-permute-start = (bf16[2,2,256,1024]{2,3,1,0:T(8,128)(2,1)S(1)}, bf16[2,2,256,1024]{2,3,1,0:T(8,128)(2,1)}, u32[]{:S(2)}, u32[]{:S(2)}) collective-permute-start(bf16[2,2,256,1024]{2,3,1,0:T(8,128)(2,1)S(1)} %copy.142), channel_id=1, source_target_pairs={{0,4},{4,8},{8,12},{12,16},{16,20},{20,24},{24,28},{28,0},{1,5},{5... | collective-permute-start | bytes 6291464 | tf_op jit(solution)/shard_map/while/body/eval_jaxpr/ppermute | solution.py:19
  309.9 5.2 copy-start.31
  329.2 26.5 %collective-permute-start = (bf16[2,2,256,1024]{2,3,1,0:T(8,128)(2,1)S(1)}, bf16[2,2,256,1024]{2,3,1,0:T(8,128)(2,1)}, u32[]{:S(2)}, u32[]{:S(2)}) collective-permute-start(bf16[2,2,256,1024]{2,3,1,0:T(8,128)(2,1)S(1)} %copy.142), channel_id=1, source_target_pairs={{0,4},{4,8},{8,12},{12,16},{16,20},{20,24},{24,28},{28,0},{1,5},{5... | collective-permute-start | bytes 6291464 | tf_op jit(solution)/shard_map/while/body/eval_jaxpr/ppermute | solution.py:19
  338.0 5.2 copy-start.31
  370.5 165.0 %copy-start.13 = (f32[512,1024]{1,0:T(8,128)}, f32[512,1024]{1,0:T(8,128)S(1)}, u32[]{:S(2)}) copy-start(f32[512,1024]{1,0:T(8,128)S(1)} %get-tuple-element.682) | copy-start | bytes 6291460
  370.5 165.0 %copy-start.33 = (f32[512]{0:T(512)}, f32[512]{0:T(512)S(1)}, u32[]{:S(2)}) copy-start(f32[512]{0:T(512)S(1)} %broadcast_multiply_fusion.4) | copy-start | bytes 6148
  370.9 164.6 %copy-start.40 = (f32[512]{0:T(512)}, f32[512]{0:T(512)S(1)}, u32[]{:S(2)}) copy-start(f32[512]{0:T(512)S(1)} %add_rsqrt_fusion.1) | copy-start | bytes 6148
  371.2 128.4 %copy-start.49 = (f32[4,1,256]{2,1,0:T(1,128)S(1)}, f32[4,1,256]{2,1,0:T(1,128)}, u32[]{:S(2)}) copy-start(f32[4,1,256]{2,1,0:T(1,128)} %all-gather.5) | copy-start | bytes 12292
  512.9 14.8 slice-start
  514.1 13.6 copy-start.21
  514.1 13.6 slice-start.1
  551.9 856.4 %reduce-scatter.3.cloned.1.call-start = ((), (), s32[]{:S(2)}) async-start(), calls=%async_computation.8 | async-start | bytes 20971520 | tf_op jit(solution)/shard_map/reduce_scatter | solution.py:303
  574.4 26.7 %collective-permute-start.2 = (bf16[2,2,256,1024]{2,3,1,0:T(8,128)(2,1)}, bf16[2,2,256,1024]{2,3,1,0:T(8,128)(2,1)}, u32[]{:S(2)}, u32[]{:S(2)}) collective-permute-start(bf16[2,2,256,1024]{2,3,1,0:T(8,128)(2,1)} %fusion.178), channel_id=1, source_target_pairs={{0,4},{4,8},{8,12},{12,16},{16,20},{20,24},{24,28},{28,0},{1,5},{5... | collective-permute-start | bytes 6291464 | tf_op jit(solution)/shard_map/while/body/eval_jaxpr/ppermute | solution.py:19
  574.4 49.1 %collective-permute-start.1 = (bf16[2,2,256,1024]{2,3,1,0:T(8,128)(2,1)}, bf16[2,2,256,1024]{2,3,1,0:T(8,128)(2,1)}, u32[]{:S(2)}, u32[]{:S(2)}) collective-permute-start(bf16[2,2,256,1024]{2,3,1,0:T(8,128)(2,1)} %copy.154), channel_id=1, source_target_pairs={{0,4},{4,8},{8,12},{12,16},{16,20},{20,24},{24,28},{28,0},{1,5},{5... | collective-permute-start | bytes 6291464 | tf_op jit(solution)/shard_map/while/body/eval_jaxpr/ppermute | solution.py:19
  643.3 26.7 %collective-permute-start.2 = (bf16[2,2,256,1024]{2,3,1,0:T(8,128)(2,1)}, bf16[2,2,256,1024]{2,3,1,0:T(8,128)(2,1)}, u32[]{:S(2)}, u32[]{:S(2)}) collective-permute-start(bf16[2,2,256,1024]{2,3,1,0:T(8,128)(2,1)} %fusion.178), channel_id=1, source_target_pairs={{0,4},{4,8},{8,12},{12,16},{16,20},{20,24},{24,28},{28,0},{1,5},{5... | collective-permute-start | bytes 6291464 | tf_op jit(solution)/shard_map/while/body/eval_jaxpr/ppermute | solution.py:19
  643.3 49.1 %collective-permute-start.1 = (bf16[2,2,256,1024]{2,3,1,0:T(8,128)(2,1)}, bf16[2,2,256,1024]{2,3,1,0:T(8,128)(2,1)}, u32[]{:S(2)}, u32[]{:S(2)}) collective-permute-start(bf16[2,2,256,1024]{2,3,1,0:T(8,128)(2,1)} %copy.154), channel_id=1, source_target_pairs={{0,4},{4,8},{8,12},{12,16},{16,20},{20,24},{24,28},{28,0},{1,5},{5... | collective-permute-start | bytes 6291464 | tf_op jit(solution)/shard_map/while/body/eval_jaxpr/ppermute | solution.py:19
  711.9 26.7 %collective-permute-start.2 = (bf16[2,2,256,1024]{2,3,1,0:T(8,128)(2,1)}, bf16[2,2,256,1024]{2,3,1,0:T(8,128)(2,1)}, u32[]{:S(2)}, u32[]{:S(2)}) collective-permute-start(bf16[2,2,256,1024]{2,3,1,0:T(8,128)(2,1)} %fusion.178), channel_id=1, source_target_pairs={{0,4},{4,8},{8,12},{12,16},{16,20},{20,24},{24,28},{28,0},{1,5},{5... | collective-permute-start | bytes 6291464 | tf_op jit(solution)/shard_map/while/body/eval_jaxpr/ppermute | solution.py:19
  711.9 49.1 %collective-permute-start.1 = (bf16[2,2,256,1024]{2,3,1,0:T(8,128)(2,1)}, bf16[2,2,256,1024]{2,3,1,0:T(8,128)(2,1)}, u32[]{:S(2)}, u32[]{:S(2)}) collective-permute-start(bf16[2,2,256,1024]{2,3,1,0:T(8,128)(2,1)} %copy.154), channel_id=1, source_target_pairs={{0,4},{4,8},{8,12},{12,16},{16,20},{20,24},{24,28},{28,0},{1,5},{5... | collective-permute-start | bytes 6291464 | tf_op jit(solution)/shard_map/while/body/eval_jaxpr/ppermute | solution.py:19
  780.5 26.7 %collective-permute-start.2 = (bf16[2,2,256,1024]{2,3,1,0:T(8,128)(2,1)}, bf16[2,2,256,1024]{2,3,1,0:T(8,128)(2,1)}, u32[]{:S(2)}, u32[]{:S(2)}) collective-permute-start(bf16[2,2,256,1024]{2,3,1,0:T(8,128)(2,1)} %fusion.178), channel_id=1, source_target_pairs={{0,4},{4,8},{8,12},{12,16},{16,20},{20,24},{24,28},{28,0},{1,5},{5... | collective-permute-start | bytes 6291464 | tf_op jit(solution)/shard_map/while/body/eval_jaxpr/ppermute | solution.py:19
  780.5 49.1 %collective-permute-start.1 = (bf16[2,2,256,1024]{2,3,1,0:T(8,128)(2,1)}, bf16[2,2,256,1024]{2,3,1,0:T(8,128)(2,1)}, u32[]{:S(2)}, u32[]{:S(2)}) collective-permute-start(bf16[2,2,256,1024]{2,3,1,0:T(8,128)(2,1)} %copy.154), channel_id=1, source_target_pairs={{0,4},{4,8},{8,12},{12,16},{16,20},{20,24},{24,28},{28,0},{1,5},{5... | collective-permute-start | bytes 6291464 | tf_op jit(solution)/shard_map/while/body/eval_jaxpr/ppermute | solution.py:19
  849.1 26.7 %collective-permute-start.2 = (bf16[2,2,256,1024]{2,3,1,0:T(8,128)(2,1)}, bf16[2,2,256,1024]{2,3,1,0:T(8,128)(2,1)}, u32[]{:S(2)}, u32[]{:S(2)}) collective-permute-start(bf16[2,2,256,1024]{2,3,1,0:T(8,128)(2,1)} %fusion.178), channel_id=1, source_target_pairs={{0,4},{4,8},{8,12},{12,16},{16,20},{20,24},{24,28},{28,0},{1,5},{5... | collective-permute-start | bytes 6291464 | tf_op jit(solution)/shard_map/while/body/eval_jaxpr/ppermute | solution.py:19
  849.1 49.1 %collective-permute-start.1 = (bf16[2,2,256,1024]{2,3,1,0:T(8,128)(2,1)}, bf16[2,2,256,1024]{2,3,1,0:T(8,128)(2,1)}, u32[]{:S(2)}, u32[]{:S(2)}) collective-permute-start(bf16[2,2,256,1024]{2,3,1,0:T(8,128)(2,1)} %copy.154), channel_id=1, source_target_pairs={{0,4},{4,8},{8,12},{12,16},{16,20},{20,24},{24,28},{28,0},{1,5},{5... | collective-permute-start | bytes 6291464 | tf_op jit(solution)/shard_map/while/body/eval_jaxpr/ppermute | solution.py:19
  917.7 26.7 %collective-permute-start.2 = (bf16[2,2,256,1024]{2,3,1,0:T(8,128)(2,1)}, bf16[2,2,256,1024]{2,3,1,0:T(8,128)(2,1)}, u32[]{:S(2)}, u32[]{:S(2)}) collective-permute-start(bf16[2,2,256,1024]{2,3,1,0:T(8,128)(2,1)} %fusion.178), channel_id=1, source_target_pairs={{0,4},{4,8},{8,12},{12,16},{16,20},{20,24},{24,28},{28,0},{1,5},{5... | collective-permute-start | bytes 6291464 | tf_op jit(solution)/shard_map/while/body/eval_jaxpr/ppermute | solution.py:19
  917.7 49.1 %collective-permute-start.1 = (bf16[2,2,256,1024]{2,3,1,0:T(8,128)(2,1)}, bf16[2,2,256,1024]{2,3,1,0:T(8,128)(2,1)}, u32[]{:S(2)}, u32[]{:S(2)}) collective-permute-start(bf16[2,2,256,1024]{2,3,1,0:T(8,128)(2,1)} %copy.154), channel_id=1, source_target_pairs={{0,4},{4,8},{8,12},{12,16},{16,20},{20,24},{24,28},{28,0},{1,5},{5... | collective-permute-start | bytes 6291464 | tf_op jit(solution)/shard_map/while/body/eval_jaxpr/ppermute | solution.py:19
  986.3 26.7 %collective-permute-start.2 = (bf16[2,2,256,1024]{2,3,1,0:T(8,128)(2,1)}, bf16[2,2,256,1024]{2,3,1,0:T(8,128)(2,1)}, u32[]{:S(2)}, u32[]{:S(2)}) collective-permute-start(bf16[2,2,256,1024]{2,3,1,0:T(8,128)(2,1)} %fusion.178), channel_id=1, source_target_pairs={{0,4},{4,8},{8,12},{12,16},{16,20},{20,24},{24,28},{28,0},{1,5},{5... | collective-permute-start | bytes 6291464 | tf_op jit(solution)/shard_map/while/body/eval_jaxpr/ppermute | solution.py:19
  986.3 49.1 %collective-permute-start.1 = (bf16[2,2,256,1024]{2,3,1,0:T(8,128)(2,1)}, bf16[2,2,256,1024]{2,3,1,0:T(8,128)(2,1)}, u32[]{:S(2)}, u32[]{:S(2)}) collective-permute-start(bf16[2,2,256,1024]{2,3,1,0:T(8,128)(2,1)} %copy.154), channel_id=1, source_target_pairs={{0,4},{4,8},{8,12},{12,16},{16,20},{20,24},{24,28},{28,0},{1,5},{5... | collective-permute-start | bytes 6291464 | tf_op jit(solution)/shard_map/while/body/eval_jaxpr/ppermute | solution.py:19
  1056.6 5.7 copy-start.12
  1062.3 5.1 copy-start.3
  1062.4 5.1 copy-start.11
  1067.4 26.7 %collective-permute-start.3 = (bf16[2,2,256,1024]{3,2,1,0:T(8,128)(2,1)}, bf16[2,2,256,1024]{3,2,1,0:T(8,128)(2,1)}, u32[]{:S(2)}, u32[]{:S(2)}) collective-permute-start(bf16[2,2,256,1024]{3,2,1,0:T(8,128)(2,1)} %fusion.34), channel_id=1, source_target_pairs={{0,4},{4,8},{8,12},{12,16},{16,20},{20,24},{24,28},{28,0},{1,5},{5... | collective-permute-start | bytes 6291464 | tf_op jit(solution)/shard_map/ppermute | solution.py:19
  1130.3 387.3 %all-reduce.14.cloned.1.call-start = ((), (), s32[]{:S(2)}) async-start(), calls=%async_computation.10 | async-start | bytes 12582912 | tf_op jit(solution)/shard_map/psum | solution.py:352
  1410.9 4.4 copy-start.44
  1410.9 4.4 copy-start.45
  1411.0 41.8 %copy-start.17 = (bf16[1,2,256,1024]{3,2,1,0:T(8,128)(2,1)S(1)}, bf16[1,2,256,1024]{3,2,1,0:T(8,128)(2,1)}, u32[]{:S(2)}) copy-start(bf16[1,2,256,1024]{3,2,1,0:T(8,128)(2,1)} %get-tuple-element.670) | copy-start | bytes 3145732
  (57 other events, 149.4 us)
Sparse Core Ops, SparseCore 0:
  10.2 48.7 all-gather.16
  61.1 44.9 all-gather.14
  108.3 44.9 all-gather.18
  155.2 44.6 all-gather.20
  201.9 148.3 all-gather.22
  351.7 147.8 all-gather.24
  552.0 142.6 reduce-scatter.4
  1130.4 277.7 reduce-scatter.2
  1412.0 105.5 all-reduce.13
where the time goes:
time: 1540 us; the launch traced here: 1530 us
  waiting for transfers between devices  789 us (51%)
  matrix products  303 us (20%)
  local copies, waits for them, and re-layouts  149 us (10%)
  other arithmetic  143 us (9%)
  blocking collectives  130 us (8%)
  between operations  16.3 us (1%)
    ppermute x22, waiting for transfers between devices, from_behind(): return lax.ppermute(value, axis, pairs)  317 us
    reduce_scatter x1, waiting for transfers between devices, body(): lax.psum_scatter(jnp.concatenate([dot_rows(low_in, projected), dot_rows(c...  278 us
    all_gather x1, waiting for transfers between devices, gather_feedforward(): lax.all_gather(reduce_weight.astype(jnp.bfloat16), 'fsdp', axis=0, tiled=...  118 us
    psum x1, waiting for transfers between devices, body(): lax.psum(row_grads, 'ctx').astype(jnp.float32)  58.6 us
    dot_general x8, matrix products, attend(): jnp.einsum('bhqk,bkhd->bqhd', weights.astype(jnp.bfloat16), values, prefe...  56.1 us
    while x77, local copies, waits for them, and re-layouts  52.7 us
    convert_element_type x15, other arithmetic, pass_grads(): return from_behind(grads.astype(jnp.bfloat16), 'ctx', 1).astype(grads.dtype)  47.3 us
    dot_general x8, matrix products, attend(): jnp.einsum('bqhd,bkhd->bhqk', query, keys, preferred_element_type=jnp.flo...  42.3 us
  transfers between devices with their start and end apart: 31, of which 26 were waited for; matrix products, arithmetic and copies ran while one was open for 33% of the time, Pallas kernels for 0%

commit v1 on v0

v1 whole, which is shorter than its diff:
```python
import functools

import jax
import jax.numpy as jnp
from jax import lax
from jax.experimental import pallas as pl
from jax.experimental.pallas import tpu as pltpu
from jax.sharding import PartitionSpec as P

HEAD = 64
LANES = 128
EPS = 1e-05
BIG = 1e30
LOG2E = 1.4426950408889634
SQRT_HALF = 0.7071067811865476
DENSITY = 0.3989422804014327
BF = jnp.bfloat16
F32 = jnp.float32


def dot_nn(left, right):
    return jnp.dot(left, right, preferred_element_type=F32)


def dot_tn(left, right):
    return lax.dot_general(left, right, (((0,), (0,)), ((), ())), preferred_element_type=F32)


def dot_nt(left, right):
    return lax.dot_general(left, right, (((1,), (1,)), ((), ())), preferred_element_type=F32)


def exchange(value, axis, k):
    count = lax.axis_size(axis)
    return lax.ppermute(value, axis, [(i, i ^ k) for i in range(count)])


def peer(value, k):
    return exchange(value, "ctx", k)


def after(value, *needed):
    return lax.optimization_barrier((value, needed))[0]


def plane_list(count):
    return list(range(0, count, 2)) + list(range(1, count, 2))


def plane_order():
    return plane_list(lax.axis_size("ctx"))


def gather_even(value, low_first):
    count = lax.axis_size("ctx")
    got = {0: value}
    for k in range(2, count, 2):
        bits = [1 << b for b in range(1, count.bit_length()) if k >> b & 1]
        step = bits[-1] if low_first else bits[0]
        got[k] = peer(got[k ^ step], step)
    return [got[k] for k in range(0, count, 2)]


def by_owner(parts, axis, order=None, mesh_axis="ctx"):
    order = order or plane_order()
    stacked = jnp.stack([parts[order.index(k)] for k in range(len(order))])
    me = lax.axis_index(mesh_axis)
    return jnp.concatenate(
        [lax.dynamic_index_in_dim(stacked, me ^ g, 0, keepdims=False) for g in range(len(order))], axis=axis
    )


def rows_to_heads(value, width):
    count = lax.axis_size("ctx")
    me = lax.axis_index("ctx")
    mine, other = [], []
    for k in range(0, count, 2):
        to = me ^ k
        first = lax.dynamic_slice_in_dim(value, to * width, width, 1)
        second = lax.dynamic_slice_in_dim(value, (to ^ 1) * width, width, 1)
        got = jnp.concatenate([first, second], axis=1)
        if k:
            got = peer(got, k)
        mine.append(got[:, :width])
        other.append(got[:, width:])
    return jnp.concatenate(mine + [peer(jnp.concatenate(other, axis=0), 1)], axis=0)


def heads_to_rows(value):
    count = lax.axis_size("ctx")
    rows, width = value.shape[0] // count, value.shape[1]
    half = value.shape[0] // 2
    both = jnp.concatenate([value[:half], peer(value[half:], 1)], axis=1)
    even, odd = [], []
    for i, k in enumerate(range(0, count, 2)):
        got = both[i * rows : (i + 1) * rows]
        if k:
            got = peer(got, k)
        even.append(got[:, :width])
        odd.append(got[:, width:])
    return even + odd


def reduce_even(blocks, low_first):
    count = lax.axis_size("ctx")
    bits = [1 << b for b in range(1, count.bit_length() - 1)]
    if not low_first:
        bits = bits[::-1]
    held = dict(zip(range(0, count, 2), blocks))
    for bit in bits:
        sent = [k for k in held if k & bit]
        got = peer(jnp.stack([held[k] for k in sent]), bit)
        got = {k ^ bit: got[i] for i, k in enumerate(sent)}
        held = {k: (held[k].astype(F32) + got[k].astype(F32)).astype(BF) for k in held if not k & bit}
    return held[0]


def gather_shards(value):
    depth = lax.axis_size("fsdp")
    parts = [value[None]] + [exchange(value, "fsdp", j)[None] for j in range(1, depth)]
    return by_owner(parts, 0, list(range(depth)), "fsdp")


def reduce_shards(value):
    depth = lax.axis_size("fsdp")
    me = lax.axis_index("fsdp")
    total = lax.dynamic_index_in_dim(value, me, 0, keepdims=False).astype(F32)
    for j in range(1, depth):
        sent = lax.dynamic_index_in_dim(value, me ^ j, 0, keepdims=False)
        total = total + exchange(sent, "fsdp", j).astype(F32)
    return total


def in_terms(vector, count):
    terms = []
    for _ in range(count):
        terms.append(vector.astype(BF))
        vector = vector - terms[-1].astype(F32)
    return terms


def whole(shape):
    return pl.BlockSpec(shape, lambda *i: (0,) * len(shape))


def params(limit=48):
    return pltpu.CompilerParams(vmem_limit_bytes=limit << 20)


def cost(flops, size):
    return pl.CostEstimate(flops=flops, bytes_accessed=size, transcendentals=0)


def mask_columns(seg, bits):
    lane = jnp.arange(LANES) % HEAD
    bit = (seg[:, None] >> jnp.minimum(lane // 2, 30)) & 1
    flip = bit ^ (lane & 1)
    used = lane < 2 * bits
    for_query = jnp.where(used & (flip == 1), -BIG, 0.0).astype(BF)
    for_key = jnp.where(used, 1 - flip, ((lane >= 60) & (lane < 63)).astype(jnp.int32)).astype(BF)
    return for_query, for_key


def lane_index():
    return lax.broadcasted_iota(jnp.int32, (1, LANES), 1)


def merge(main, extra, h):
    lane = lane_index()
    return jnp.where((lane < HEAD) if h == 0 else (lane >= HEAD), main, extra)


def with_terms(extra, number):
    lane = lane_index() % HEAD
    first = number.astype(BF).astype(F32)
    rest = number - first
    second = rest.astype(BF).astype(F32)
    third = rest - second
    terms = jnp.where(lane == 60, first, jnp.where(lane == 61, second, third)).astype(BF)
    return jnp.where((lane >= 60) & (lane < 63), terms, extra)


def forward_kernel(q, k, v, mask_q, mask_k, out, lse, key_side, value_side, *, heads):
    lane = lane_index()

    @pl.when(pl.program_id(0) == 0)
    def _():
        for h in range(heads):
            key_side[h] = merge(k[...], mask_k[...], h)
            value_side[h] = merge(v[...], jnp.ones((1, LANES), BF), h)

    whole, whole_lse = None, None
    for h in range(heads):
        scores = dot_nt(merge(q[...], mask_q[...], h), key_side[h])
        top = jnp.max(scores, axis=1, keepdims=True)
        weights = jnp.exp2(scores - top).astype(BF)
        both = dot_nn(weights, value_side[h])
        total = pltpu.roll(both, HEAD, 1)
        context, log_total = both / total, top + jnp.log2(total)
        if whole is None:
            whole, whole_lse = context, log_total
        else:
            whole = jnp.where(lane < HEAD, whole, context)
            whole_lse = jnp.where(lane < HEAD, whole_lse, log_total)
    out[...] = whole.astype(BF)
    lse[...] = whole_lse


def attend(qkv, mask_q, mask_k, heads, block):
    count = qkv.shape[0]
    part = lambda j: pl.BlockSpec((block, LANES), lambda i: (i, j))
    full = lambda j: pl.BlockSpec((count, LANES), lambda i: (0, j))
    products = 2 * 2 * count * count * LANES * heads
    return pl.pallas_call(
        functools.partial(forward_kernel, heads=heads),
        grid=(count // block,),
        in_specs=[part(0), full(1), full(2), part(0), full(0)],
        out_specs=[part(0), part(0)],
        out_shape=[jax.ShapeDtypeStruct((count, LANES), BF), jax.ShapeDtypeStruct((count, LANES), F32)],
        scratch_shapes=[pltpu.VMEM((heads, count, LANES), BF), pltpu.VMEM((heads, count, LANES), BF)],
        compiler_params=pltpu.CompilerParams(vmem_limit_bytes=48 << 20),
        cost_estimate=pl.CostEstimate(
            flops=products * 2, bytes_accessed=12 * count * LANES, transcendentals=count * count * heads
        ),
        name="attend",
    )(qkv, qkv, qkv, mask_q, mask_k)


def backward_kernel(*refs, heads, steps, block, pieces):
    q, k, v, mask_q, mask_k, out, lse = refs[:7]
    parts = refs[7 : 7 + pieces]
    grads, key_side, value_side, dk_t, dv_t, dc_all = refs[7 + pieces :]
    lane = lane_index()
    step = pl.program_id(0)

    @pl.when(step == 0)
    def _():
        ones = ((lane % HEAD >= 60) & (lane % HEAD < 63)).astype(F32).astype(BF)
        for h in range(heads):
            key_side[h] = merge(k[...], mask_k[...], h)
            value_side[h] = merge(v[...], ones, h)
        dk_t[...] = jnp.zeros_like(dk_t)
        dv_t[...] = jnp.zeros_like(dv_t)
        if pieces == 1:
            dc_all[...] = parts[0][...]
        else:
            for i in range(pieces):
                dc_all[i * block : (i + 1) * block, :] = parts[i][:, :LANES]
                dc_all[(pieces + i) * block : (pieces + i + 1) * block, :] = parts[i][:, LANES:]

    dc = dc_all.at[pl.ds(pl.multiple_of(step * block, block), block), :]
    product = dc[...].astype(F32) * out[...].astype(F32)
    low = jnp.sum(jnp.where(lane < HEAD, product, 0.0), axis=1, keepdims=True)
    high = jnp.sum(jnp.where(lane < HEAD, 0.0, product), axis=1, keepdims=True)
    query_extra = with_terms(mask_q[...], -pltpu.roll(lse[...], HEAD, 1))
    grad_extra = with_terms(jnp.zeros((1, LANES), BF), jnp.where(lane < HEAD, -high, -low))
    q_t, dc_t = q[...].T, dc[...].T
    dq = None
    for h in range(heads):
        probs = jnp.exp2(dot_nt(merge(q[...], query_extra, h), key_side[h]))
        centred = dot_nt(merge(dc[...], grad_extra, h), value_side[h])
        ds = (probs * centred).astype(BF)
        part = dot_nn(ds, key_side[h])
        dq = part if dq is None else jnp.where(lane < HEAD, dq, part)
        own = slice(HEAD * h, HEAD * h + HEAD)
        dk_t[own, :] += dot_nn(q_t[own, :], ds)
        dv_t[own, :] += dot_nn(dc_t[own, :], probs.astype(BF))
    grads[pl.ds(pl.multiple_of(step * block, block), block), :LANES] = (
        dq.astype(BF).astype(F32) * HEAD**-0.5
    ).astype(BF)

    @pl.when(step == steps - 1)
    def _():
        grads[:, LANES : 2 * LANES] = (dk_t[...] * (1.0 / LOG2E)).T.astype(BF)
        grads[:, 2 * LANES :] = dv_t[...].T.astype(BF)


def attend_back(qkv, mask_q, mask_k, dc, out, lse, heads, block):
    dc = dc if isinstance(dc, list) else [dc]
    count = qkv.shape[0]
    part = lambda j: pl.BlockSpec((block, LANES), lambda i: (i, j))
    full = lambda j: pl.BlockSpec((count, LANES), lambda i: (0, j))
    products = 5 * 2 * count * count * LANES * heads
    return pl.pallas_call(
        functools.partial(backward_kernel, heads=heads, steps=count // block, block=block, pieces=len(dc)),
        grid=(count // block,),
        in_specs=[part(0), full(1), full(2), part(0), full(0), part(0), part(0)] + [whole(v.shape) for v in dc],
        out_specs=pl.BlockSpec((count, 3 * LANES), lambda i: (0, 0)),
        out_shape=jax.ShapeDtypeStruct((count, 3 * LANES), BF),
        scratch_shapes=[
            pltpu.VMEM((heads, count, LANES), BF),
            pltpu.VMEM((heads, count, LANES), BF),
            pltpu.VMEM((LANES, count), F32),
            pltpu.VMEM((LANES, count), F32),
            pltpu.VMEM((count, LANES), BF),
        ],
        compiler_params=pltpu.CompilerParams(vmem_limit_bytes=56 << 20),
        cost_estimate=pl.CostEstimate(
            flops=products, bytes_accessed=16 * count * LANES, transcendentals=count * count * heads
        ),
        name="attend_back",
    )(qkv, qkv, qkv, mask_q, mask_k, out, lse, *dc)


def project_kernel(*refs, blocks):
    weight, bias, factor, out = refs[blocks:]
    row = 0
    for ref in refs[:blocks]:
        got = (dot_nn(ref[...], weight[...]) + bias[...]) * factor[...]
        out[row : row + ref.shape[0], :] = got.astype(BF)
        row += ref.shape[0]


def project(blocks, weight, bias, factor):
    width, line = weight.shape
    args = (*blocks, weight, bias[None], factor[None])
    shape = (sum(v.shape[0] for v in blocks), line)
    return pl.pallas_call(
        functools.partial(project_kernel, blocks=len(blocks)),
        in_specs=[whole(v.shape) for v in args],
        out_specs=whole(shape),
        out_shape=jax.ShapeDtypeStruct(shape, BF),
        grid=(1,),
        compiler_params=params(),
        cost_estimate=cost(2 * shape[0] * width * line, 2 * shape[0] * (width + line)),
        name="project",
    )(*args)


def flatten_blocks(blocks):
    flat, parts = [], []
    for n, block in enumerate(blocks):
        first = 0
        for part in block:
            flat.append(part)
            parts.append((n, first))
            first += part.shape[0]
    return flat, tuple(parts)


def assemble_kernel(me, *refs, parts, thin, folds):
    out = refs[-1]
    shard = len({n for n, _ in parts}) * thin
    block = refs[0].shape[2]
    order = plane_list(len({n for n, _ in parts}))
    for ref, (n, first) in zip(refs, parts):
        for z in range(ref.shape[0]):
            row = pl.multiple_of((first + z) * shard + (me[0] ^ order[n]) * thin, thin)
            for f in range(folds):
                out[pl.ds(row, thin), f * block : (f + 1) * block] = ref[z, f * thin : (f + 1) * thin, :]


def assemble_output(blocks, shard, thin, me):
    flat, parts = flatten_blocks(blocks)
    _, tall, block = flat[0].shape
    strip = tall - shard
    folds = strip // thin
    width = folds * block
    specs = [pl.BlockSpec((v.shape[0], strip, block), lambda i: (0, shard // strip, 0)) for v in flat]
    return pl.pallas_call(
        functools.partial(assemble_kernel, parts=parts, thin=thin, folds=folds),
        grid=(1,),
        in_specs=[pl.BlockSpec(memory_space=pltpu.SMEM)] + specs,
        out_specs=whole((width, width)),
        out_shape=jax.ShapeDtypeStruct((width, width), BF),
        compiler_params=params(),
        cost_estimate=cost(0, 4 * width * width),
        name="assemble_output",
    )(me, *flat)


def branch_kernel(me, *refs, pieces, aliased):
    weight, tokens, bias, gain, shift = refs[pieces : pieces + 5]
    context, hidden, low, normed, inverse = refs[pieces + 5 + aliased :]
    second = (me[0] & 1) == 1
    pair = refs[0].shape[1]
    for i in range(pieces):
        at = pl.multiple_of(((me[0] ^ (2 * i)) // 2) * pair, pair)
        got = refs[i][...]
        swapped = jnp.concatenate([got[:, pair // 2 :], got[:, : pair // 2]], axis=1)
        context[:, pl.ds(at, pair)] = jnp.where(second, swapped, got)
    total = tokens[...] + dot_nn(context[...], weight[...]) + bias[...]
    mean = jnp.mean(total, axis=1, keepdims=True)
    centred = total - mean
    scale = lax.rsqrt(jnp.mean(centred * centred, axis=1, keepdims=True) + EPS)
    unit = centred * scale
    out = unit * gain[...] + shift[...]
    hidden[...] = out
    low[...] = out.astype(BF)
    normed[...] = unit
    inverse[...] = jnp.broadcast_to(scale, inverse.shape)


def branch(s, me, pieces, weight, tokens, bias, gain, shift, earlier):
    batch, rows, width = tokens.shape
    at = pl.BlockSpec((None, rows, width), lambda i: (s, 0, 0))
    thin = pl.BlockSpec((None, rows, LANES), lambda i: (s, 0, 0))
    vec = whole((1, width))
    earlier = earlier or ()
    first = 1 + len(pieces) + 5
    full = lambda t: jax.ShapeDtypeStruct((batch, rows, width), t)
    return pl.pallas_call(
        functools.partial(branch_kernel, pieces=len(pieces), aliased=len(earlier)),
        grid=(1,),
        in_specs=[pl.BlockSpec(memory_space=pltpu.SMEM)]
        + [whole(v.shape) for v in pieces]
        + [whole(weight.shape), at, vec, vec, vec]
        + [pl.BlockSpec(memory_space=pl.ANY)] * len(earlier),
        out_specs=[at, at, at, at, thin],
        out_shape=[full(BF), full(F32), full(BF), full(F32), jax.ShapeDtypeStruct((batch, rows, LANES), F32)],
        input_output_aliases={first + i: i for i in range(len(earlier))},
        compiler_params=params(),
        cost_estimate=cost(2 * rows * width * width, 2 * width * width + 18 * rows * width),
        name="branch",
    )(me, *pieces, weight, tokens, bias[None], gain[None], shift[None], *earlier)


def fetch_blocks(refs, parts, slots, sems, step, middle, shard):
    def copies(i):
        made = []
        for j, (ref, (n, first)) in enumerate(zip(refs, parts)):
            if n % middle == i:
                target = slots.at[i % 2, n // middle, pl.ds(first, ref.shape[0])]
                made.append(pltpu.make_async_copy(ref.at[:, :shard, :], target, sems.at[j]))
        return made

    for i in range(middle):

        @pl.when(step == i)
        def _():
            if i == 0:
                for copy in copies(0):
                    copy.start()
            if i + 1 < middle:
                for copy in copies(i + 1):
                    copy.start()
            for copy in copies(i):
                copy.wait()


def expand_kernel(*refs, middle, depth, parts):
    low, bias_even, bias_odd = refs[:3]
    blocks = refs[3 : 3 + len(parts)]
    outs = refs[3 + len(parts) : 7 + len(parts)]
    slots, sems = refs[7 + len(parts) :]
    step = pl.program_id(0)
    shard = slots.shape[3]
    fetch_blocks(blocks, parts, slots, sems, step, middle, shard)
    slot = step % 2
    rows = low.shape[0] // 2
    for parity, bias in enumerate((bias_even, bias_odd)):
        for part in range(2):
            at = slice(part * rows, part * rows + rows)
            total = bias[...]
            for z in range(depth):
                total = total + dot_nn(low[at, z * shard : (z + 1) * shard], slots[slot, parity, z])
            cdf = 0.5 * (1.0 + lax.erf(total * SQRT_HALF))
            outs[parity][at, :] = (total * cdf).astype(BF)
            outs[2 + parity][at, :] = (cdf + total * DENSITY * jnp.exp(-0.5 * total * total)).astype(BF)


def expand_forward(low, bias_halves, blocks, shard):
    rows, width = low.shape
    middle = len(blocks) // 2
    depth = width // shard
    block = blocks[0][0].shape[2]
    flat, parts = flatten_blocks(blocks)
    bias = pl.BlockSpec((None, 1, block), lambda i: (i, 0, 0))
    out = pl.BlockSpec((rows, block), lambda i: (0, i))
    return pl.pallas_call(
        functools.partial(expand_kernel, middle=middle, depth=depth, parts=parts),
        grid=(middle,),
        in_specs=[whole(low.shape), bias, bias] + [pl.BlockSpec(memory_space=pl.ANY)] * len(flat),
        out_specs=[out] * 4,
        out_shape=[jax.ShapeDtypeStruct((rows, middle * block), BF)] * 4,
        scratch_shapes=[pltpu.VMEM((2, 2, depth, shard, block), BF), pltpu.SemaphoreType.DMA((len(flat),))],
        compiler_params=params(),
        cost_estimate=cost(4 * rows * width * middle * block, 4 * width * middle * block + 8 * rows * middle * block),
        name="expand",
    )(low, *bias_halves, *flat)


def norm_back(grad, normed, inverse, gain):
    scaled = grad * gain
    first = jnp.mean(scaled, axis=1, keepdims=True)
    second = jnp.mean(scaled * normed, axis=1, keepdims=True)
    return inverse * (scaled - first - normed * second)


def reduce_kernel(
    act_even, act_odd, w_even, w_odd, hidden, grad_out, bias, gain, shift, result, du, low, sums, total, *, steps
):
    step = pl.program_id(0)
    block = act_even.shape[1]
    width = total.shape[1]
    part = dot_nn(act_even[...], w_even[...].reshape(block, width))
    part = part + dot_nn(act_odd[...], w_odd[...].reshape(block, width))

    @pl.when(step == 0)
    def _():
        total[...] = part + bias[...]
        sums[...] = jnp.zeros_like(sums)

    @pl.when(step > 0)
    def _():
        total[...] += part

    @pl.when(step == steps - 1)
    def _():
        rows = 64

        @pl.loop(0, total.shape[0] // rows)
        def _(i):
            at = pl.ds(pl.multiple_of(i * rows, rows), rows)
            value = total[at, :] + hidden[at, :]
            mean = jnp.mean(value, axis=1, keepdims=True)
            centred = value - mean
            inverse = lax.rsqrt(jnp.mean(centred * centred, axis=1, keepdims=True) + EPS)
            normed = centred * inverse
            result[at, :] = normed * gain[...] + shift[...]
            grad = grad_out[at, :]
            back = norm_back(grad, normed, inverse, gain[...])
            du[at, :] = back
            rounded = back.astype(BF)
            low[at, :] = rounded
            sums[0:1, :] += jnp.sum(grad * normed, axis=0, keepdims=True)
            sums[1:2, :] += jnp.sum(grad, axis=0, keepdims=True)
            sums[2:3, :] += jnp.sum(rounded.astype(F32), axis=0, keepdims=True)


def reduce_forward(acts, weights, hidden, grad_out, bias, gain, shift):
    rows, width = hidden.shape
    depth, middle, piece, _ = weights[0].shape
    block = depth * piece
    act = pl.BlockSpec((rows, block), lambda i: (0, i))
    weight = pl.BlockSpec((depth, None, piece, width), lambda i: (0, i, 0, 0))
    full, vec = whole((rows, width)), whole((1, width))
    return pl.pallas_call(
        functools.partial(reduce_kernel, steps=middle),
        grid=(middle,),
        in_specs=[act, act, weight, weight, full, full, vec, vec, vec],
        out_specs=[full, full, full, whole((8, width))],
        out_shape=[
            jax.ShapeDtypeStruct((rows, width), F32),
            jax.ShapeDtypeStruct((rows, width), F32),
            jax.ShapeDtypeStruct((rows, width), BF),
            jax.ShapeDtypeStruct((8, width), F32),
        ],
        scratch_shapes=[pltpu.VMEM((rows, width), F32)],
        compiler_params=params(),
        cost_estimate=cost(4 * rows * width * middle * block, 4 * width * middle * block + 16 * rows * width),
        name="reduce",
    )(*acts, *weights, hidden, grad_out, bias[None], gain[None], shift[None])


def feed_back_kernel(*refs, middle, depth, steps, parts):
    low, w_even, w_odd, slope_even, slope_odd, du_second, normed, inverse, gain = refs[:9]
    refs = refs[9:]
    blocks = refs[: len(parts)]
    de_even, de_odd, bias_even, bias_odd, du, da, sums = refs[len(parts) : 7 + len(parts)]
    slots, sems, total = refs[7 + len(parts) :]
    step = pl.program_id(0)
    shard, block = slots.shape[3], slots.shape[4]
    width = total.shape[1]
    fetch_blocks(blocks, parts, slots, sems, step, middle, shard)
    slot = step % 2

    @pl.when(step == 0)
    def _():
        total[...] = du_second[...]
        sums[...] = jnp.zeros_like(sums)

    for parity, (weight, slope, de, bias) in enumerate(
        ((w_even, slope_even, de_even, bias_even), (w_odd, slope_odd, de_odd, bias_odd))
    ):
        grad = dot_nt(low[...], weight[...].reshape(block, width)) * slope[...].astype(F32)
        rounded = grad.astype(BF)
        de[...] = rounded
        bias[...] = jnp.sum(rounded.astype(F32), axis=0, keepdims=True)
        for z in range(depth):
            total[:, z * shard : (z + 1) * shard] += dot_nt(rounded, slots[slot, parity, z])

    @pl.when(step == steps - 1)
    def _():
        rows = 64

        @pl.loop(0, total.shape[0] // rows)
        def _(i):
            at = pl.ds(pl.multiple_of(i * rows, rows), rows)
            grad, unit = total[at, :], normed[at, :]
            back = norm_back(grad, unit, inverse[at, 0:1], gain[...])
            du[at, :] = back
            rounded = back.astype(BF)
            da[at, :] = rounded
            sums[0:1, :] += jnp.sum(grad * unit, axis=0, keepdims=True)
            sums[1:2, :] += jnp.sum(grad, axis=0, keepdims=True)
            sums[2:3, :] += jnp.sum(rounded.astype(F32), axis=0, keepdims=True)


def feed_back(low, weights, slopes, du_second, normed, inverse, gain, blocks, shard):
    rows, width = low.shape
    depth, middle, piece, _ = weights[0].shape
    block = depth * piece
    flat, parts = flatten_blocks(blocks)
    act = pl.BlockSpec((rows, block), lambda i: (0, i))
    bias = pl.BlockSpec((None, 1, block), lambda i: (i, 0, 0))
    weight = pl.BlockSpec((depth, None, piece, width), lambda i: (0, i, 0, 0))
    full, vec = whole((rows, width)), whole((1, width))
    return pl.pallas_call(
        functools.partial(feed_back_kernel, middle=middle, depth=depth, steps=middle, parts=parts),
        grid=(middle,),
        in_specs=[full, weight, weight, act, act, full, full, whole((rows, LANES)), vec]
        + [pl.BlockSpec(memory_space=pl.ANY)] * len(flat),
        out_specs=[act, act, bias, bias, full, full, whole((8, width))],
        out_shape=[
            jax.ShapeDtypeStruct((rows, middle * block), BF),
            jax.ShapeDtypeStruct((rows, middle * block), BF),
            jax.ShapeDtypeStruct((middle, 1, block), F32),
            jax.ShapeDtypeStruct((middle, 1, block), F32),
            jax.ShapeDtypeStruct((rows, width), F32),
            jax.ShapeDtypeStruct((rows, width), BF),
            jax.ShapeDtypeStruct((8, width), F32),
        ],
        scratch_shapes=[
            pltpu.VMEM((2, 2, depth, shard, block), BF),
            pltpu.SemaphoreType.DMA((len(flat),)),
            pltpu.VMEM((rows, width), F32),
        ],
        compiler_params=params(56),
        cost_estimate=cost(8 * rows * width * middle * block, 8 * width * middle * block + 16 * rows * width),
        name="feed_back",
    )(low, *weights, *slopes, du_second, normed, inverse, gain[None], *flat)


def context_back_kernel(me, da, weight, mine, other, whole_grad, *, middle):
    whole_grad[...] = dot_nt(da[...], weight[...]).astype(BF)
    rows = da.shape[0]
    width = mine.shape[1]
    second = (me[0] & 1) == 1
    for i in range(middle):
        at = pl.multiple_of(((me[0] ^ (2 * i)) // 2) * 2 * width, 2 * width)
        pair = whole_grad[:, pl.ds(at, 2 * width)]
        low, high = pair[:, :width], pair[:, width:]
        mine[i * rows : (i + 1) * rows, :] = jnp.where(second, high, low)
        other[i * rows : (i + 1) * rows, :] = jnp.where(second, low, high)


def context_back(s, me, da, weight, own_width, middle):
    _, rows, width = da.shape
    shape = (middle * rows, own_width)
    return pl.pallas_call(
        functools.partial(context_back_kernel, middle=middle),
        grid=(1,),
        in_specs=[
            pl.BlockSpec(memory_space=pltpu.SMEM),
            pl.BlockSpec((None, rows, width), lambda i: (s, 0, 0)),
            whole(weight.shape),
        ],
        out_specs=[whole(shape)] * 2,
        out_shape=[jax.ShapeDtypeStruct(shape, BF)] * 2,
        scratch_shapes=[pltpu.VMEM((rows, width), BF)],
        compiler_params=params(),
        cost_estimate=cost(2 * rows * width * width, 2 * width * width + 4 * rows * width),
        name="context_back",
    )(me, da, weight)


def gradient_kernel(act, other_act, grad, other_grad, out):
    depth, piece, width = out.shape
    total = dot_tn(act[...], grad[...]) + dot_tn(other_act[...], other_grad[...])
    out[...] = total.astype(BF).reshape(depth, piece, width)


def reduce_gradient(act, other_act, grad, other_grad, depth, piece):
    rows, width = grad.shape
    block = depth * piece
    middle = act.shape[1] // block
    column = pl.BlockSpec((rows, block), lambda i: (0, i))
    full = whole((rows, width))
    return pl.pallas_call(
        gradient_kernel,
        grid=(middle,),
        in_specs=[column, column, full, full],
        out_specs=pl.BlockSpec((depth, None, piece, width), lambda i: (0, i, 0, 0)),
        out_shape=jax.ShapeDtypeStruct((depth, middle, piece, width), BF),
        compiler_params=params(),
        cost_estimate=cost(4 * rows * width * middle * block, 2 * width * middle * block + 4 * rows * middle * block),
        name="reduce_gradient",
    )(act, other_act, grad, other_grad)


def expand_gradient_kernel(
    me, low, other_low, context, other_context, de, other_de, da, other_da, kept_a, sent_a, kept_b, sent_b, *, middle
):
    block = de.shape[1] // middle
    rows = kept_a.shape[1]
    own = kept_a.shape[2] - block
    first, second = low[...].T, other_low[...].T
    third, fourth = context[...].T, other_context[...].T
    for i in range(middle):
        at = slice(i * block, (i + 1) * block)
        wide = (dot_nn(first, de[:, at]) + dot_nn(second, other_de[:, at])).astype(BF)
        where = pl.ds(pl.multiple_of((me[0] ^ (2 * i)) * own, own), own)
        thin = (dot_nn(third, da[:, where]) + dot_nn(fourth, other_da[:, where])).astype(BF)
        for target, n, part in (
            (sent_a if i >= 2 else kept_a, i % 2, slice(0, rows)),
            (sent_b if i % 2 else kept_b, i // 2, slice(rows, 2 * rows)),
        ):
            target[n, :, :block] = wide[part]
            target[n, :, block:] = thin[part]


def expand_gradient(me, low, other_low, context, other_context, de, other_de, da, other_da, own):
    rows, width = low.shape
    middle = 4
    block = de.shape[1] // middle
    args = (low, other_low, context, other_context, de, other_de, da, other_da)
    shape = (2, width // 2, block + own)
    return pl.pallas_call(
        functools.partial(expand_gradient_kernel, middle=middle),
        grid=(1,),
        in_specs=[pl.BlockSpec(memory_space=pltpu.SMEM)] + [whole(v.shape) for v in args],
        out_specs=[whole(shape)] * 4,
        out_shape=[jax.ShapeDtypeStruct(shape, BF)] * 4,
        compiler_params=params(56),
        cost_estimate=cost(4 * rows * width * middle * (block + own), 4 * width * middle * block),
        name="expand_gradient",
    )(me, *args)


def unpack_expand_kernel(me, *refs, depth):
    wide, thin = refs[-2:]
    count = len(refs) - 2
    block = wide.shape[1] // count
    piece, own = block // depth, thin.shape[1] // count
    for n, k in enumerate(plane_list(count)):
        g = me[0] ^ k
        for z in range(depth):
            at = pl.multiple_of(z * count * piece + g * piece, piece)
            wide[:, pl.ds(at, piece)] = refs[n][:, z * piece : (z + 1) * piece].astype(F32)
        thin[:, pl.ds(pl.multiple_of(g * own, own), own)] = refs[n][:, block:].astype(F32)


def unpack_expand(me, blocks, depth, hidden, width):
    shard = blocks[0].shape[0]
    shapes = [(shard, hidden), (shard, width)]
    return pl.pallas_call(
        functools.partial(unpack_expand_kernel, depth=depth),
        grid=(1,),
        in_specs=[pl.BlockSpec(memory_space=pltpu.SMEM)] + [whole(v.shape) for v in blocks],
        out_specs=[whole(v) for v in shapes],
        out_shape=[jax.ShapeDtypeStruct(v, F32) for v in shapes],
        compiler_params=params(),
        cost_estimate=cost(0, 6 * shard * (hidden + width)),
        name="unpack_expand",
    )(me, *blocks)


def unpack_heads_kernel(me, *refs):
    outs, bias = refs[-4:-1], refs[-1]
    count = len(refs) - 4
    shard, width = outs[0].shape
    own = width // count
    bias[...] = jnp.zeros_like(bias)
    for n, k in enumerate(plane_list(count)):
        where = pl.ds(pl.multiple_of((me[0] ^ k) * own, own), own)
        tail = refs[n][shard : shard + 16, :].astype(F32)
        for t in range(3):
            at = slice(t * own, (t + 1) * own)
            outs[t][:, where] = refs[n][:shard, at].astype(F32)
            bias[t : t + 1, where] = tail[0:1, at] + tail[1:2, at]


def unpack_heads(me, blocks, shard, width):
    shapes = [(shard, width)] * 3 + [(8, width)]
    return pl.pallas_call(
        unpack_heads_kernel,
        grid=(1,),
        in_specs=[pl.BlockSpec(memory_space=pltpu.SMEM)] + [whole(v.shape) for v in blocks],
        out_specs=[whole(v) for v in shapes],
        out_shape=[jax.ShapeDtypeStruct(v, F32) for v in shapes],
        compiler_params=params(),
        cost_estimate=cost(0, 18 * shard * width),
        name="unpack_heads",
    )(me, *blocks)


def heads_gradient_kernel(*refs, blocks, last):
    if last:
        grads, before = refs[blocks : blocks + 2]
        out, sums, total = refs[blocks + 2 :]
        total[...] = before[...]
    else:
        grads = refs[blocks]
        total, sums = refs[blocks + 1 :]
        total[...] = jnp.zeros_like(total)
    row = 0
    for ref in refs[:blocks]:
        total[...] += dot_tn(grads[row : row + ref.shape[0], :], ref[...])
        row += ref.shape[0]
    sums[...] = jnp.broadcast_to(jnp.sum(grads[...].astype(F32), axis=0, keepdims=True), sums.shape)
    if last:
        out[...] = total[...].T.astype(BF)


def heads_gradient(blocks, grads, before=None):
    line = grads.shape[1]
    width = blocks[0].shape[1]
    last = before is not None
    args = (*blocks, grads) + ((before,) if last else ())
    shapes = [jax.ShapeDtypeStruct((width, line), BF) if last else jax.ShapeDtypeStruct((line, width), F32)]
    shapes.append(jax.ShapeDtypeStruct((8, line), F32))
    return pl.pallas_call(
        functools.partial(heads_gradient_kernel, blocks=len(blocks), last=last),
        grid=(1,),
        in_specs=[whole(v.shape) for v in args],
        out_specs=[whole(v.shape) for v in shapes],
        out_shape=shapes,
        scratch_shapes=[pltpu.VMEM((line, width), F32)] if last else [],
        compiler_params=params(),
        cost_estimate=cost(2 * grads.shape[0] * width * line, 2 * grads.shape[0] * width + 6 * width * line),
        name="heads_gradient",
    )(*args)


def normalize(values, gain, shift):
    mean = jnp.mean(values, axis=-1, keepdims=True)
    centred = values - mean
    inverse = lax.rsqrt(jnp.mean(centred * centred, axis=-1, keepdims=True) + EPS)
    normed = centred * inverse
    return normed * gain + shift, normed, inverse


def normalize_back(grad, normed, inverse, gain):
    scaled = grad * gain
    inner = (
        scaled
        - jnp.mean(scaled, axis=-1, keepdims=True)
        - normed * jnp.mean(scaled * normed, axis=-1, keepdims=True)
    )
    return inner * inverse, jnp.sum(grad * normed, axis=0), jnp.sum(grad, axis=0)


def column_sums(values):
    return jnp.sum(values.astype(F32), axis=0)


def plain_body(
    tokens,
    segments,
    query_weight,
    query_bias,
    key_weight,
    value_weight,
    value_bias,
    output_weight,
    output_bias,
    first_gain,
    first_shift,
    expand_weight,
    expand_bias,
    reduce_weight,
    reduce_bias,
    second_gain,
    second_shift,
    cotangent,
):
    batch, rows, width = tokens.shape
    count, depth = lax.axis_size("ctx"), lax.axis_size("fsdp")
    me, my_shard = lax.axis_index("ctx"), lax.axis_index("fsdp")
    shard = query_weight.shape[0]
    hidden = expand_weight.shape[1]
    own_width = width // count
    heads = own_width // HEAD
    piece = hidden // depth // count
    block = depth * piece
    half = hidden // 2
    order = plane_order()
    evens = order[: count // 2]
    scale = HEAD**-0.5
    bits = (count * rows - 1).bit_length()

    columns = lambda w: lax.dynamic_slice_in_dim(w, me * own_width, own_width, 1).astype(BF)
    names = (query_bias, value_bias, output_bias, first_gain, first_shift, reduce_bias, second_gain, second_shift)
    packed = jnp.concatenate(names + (expand_bias,))
    terms = jnp.concatenate(in_terms(packed, 3))
    line = 3 * own_width
    lines = -(-terms.shape[0] // (16 * line)) * 16
    terms = jnp.pad(terms, (0, lines * line - terms.shape[0])).reshape(lines, line)
    own_heads = jnp.concatenate([columns(query_weight), columns(key_weight), columns(value_weight)], axis=1)
    own_heads = gather_shards(jnp.concatenate([own_heads, terms], axis=0))
    packed = own_heads[:, shard:].reshape(depth, lines * line)[:, : 3 * packed.shape[0]]
    packed = jnp.sum(packed.reshape(depth, 3, -1).astype(F32), axis=1)
    own_heads = own_heads[:, :shard].reshape(width, line)
    (bias_query, bias_value, bias_output, gain_first, shift_first, bias_reduce, gain_second, shift_second) = (
        packed[:, i * shard : (i + 1) * shard].reshape(width) for i in range(len(names))
    )
    wide_bias = packed[:, len(names) * shard :].reshape(depth, count, piece)
    bias_halves = [
        jnp.stack([lax.dynamic_index_in_dim(wide_bias, me ^ k, 1, keepdims=False) for k in ks], axis=1).reshape(half)
        for ks in (evens, order[count // 2 :])
    ]
    own_part = lambda v: lax.dynamic_slice_in_dim(v, me * own_width, own_width, 0)
    head_bias = jnp.concatenate([own_part(bias_query), jnp.zeros((own_width,), F32), own_part(bias_value)])
    head_scale = jnp.concatenate([jnp.full((own_width,), scale * LOG2E, F32), jnp.ones((2 * own_width,), F32)])

    thin = shard // count
    folds = width // block
    strip = lax.dynamic_slice_in_dim(output_weight, me * thin, thin, 0).astype(BF)
    strip = jnp.concatenate([strip[:, i * block : (i + 1) * block] for i in range(folds)], axis=0)
    block_expand = lax.dynamic_slice_in_dim(expand_weight.reshape(shard, depth, count * piece), me * piece, piece, 2)
    block_expand = jnp.concatenate([block_expand.reshape(shard, block).astype(BF), strip], axis=0)
    block_expand = lax.all_gather(block_expand, "fsdp", axis=0)
    block_reduce = lax.dynamic_slice_in_dim(reduce_weight, me * piece, piece, 0).astype(BF)
    block_reduce = lax.all_gather(block_reduce, "fsdp", axis=0)

    groups = jnp.stack([w.reshape(shard, count, own_width) for w in (query_weight, key_weight, value_weight)], axis=2)
    half_heads = jnp.concatenate(
        [lax.dynamic_index_in_dim(groups, me ^ k, 1, keepdims=False).reshape(shard, line).astype(BF) for k in evens],
        axis=1,
    )
    half_heads = lax.all_gather(half_heads, "fsdp", axis=0, tiled=True)
    other_heads = peer(half_heads, 1)

    seg = segments
    for b in range(count.bit_length() - 1):
        seg = jnp.concatenate([seg, peer(seg, 1 << b)], axis=1)
    seg = seg.reshape(batch, count, rows)
    seg = jnp.concatenate([seg[:, k] for k in order], axis=1)

    lanes = lambda v: v if own_width == LANES else jnp.pad(v, ((0, 0), (0, LANES - own_width)))
    kept, context_parts = [], []
    for s in range(batch):
        even = jnp.concatenate(gather_even(tokens[s].astype(BF), s % 2 == 0), axis=0)
        odd = peer(even, 1)
        qkv = jnp.concatenate([dot_nn(even, own_heads), dot_nn(odd, own_heads)], axis=0)
        qkv = ((qkv + head_bias) * head_scale).astype(BF)
        if own_width != LANES:
            qkv = jnp.concatenate([lanes(qkv[:, i * own_width : (i + 1) * own_width]) for i in range(3)], axis=1)
        mask_q, mask_k = mask_columns(seg[s], bits)
        out, lse = attend(qkv, mask_q, mask_k, heads, rows)
        kept.append((even, odd, qkv, mask_q, mask_k, out, lse))
        context_parts.append(by_owner(heads_to_rows(out[:, :own_width]), 1))

    got_expand = gather_even(block_expand, True)
    got_expand += [peer(v, 1) for v in got_expand]
    got_reduce = gather_even(block_reduce, False)
    got_reduce += [peer(v, 1) for v in got_reduce]
    full_output = by_owner(
        [
            jnp.concatenate([v[:, shard + i * thin : shard + (i + 1) * thin] for i in range(folds)], axis=2)
            for v in got_expand
        ],
        1,
    ).reshape(width, width)
    middle = count // 2
    expand_halves = [
        jnp.concatenate([v[:, :shard].reshape(width, depth, piece) for v in vs], axis=2).reshape(width, half)
        for vs in (got_expand[:middle], got_expand[middle:])
    ]
    reduce_halves = [
        jnp.concatenate(vs, axis=1).reshape(half, width) for vs in (got_reduce[:middle], got_reduce[middle:])
    ]

    firsts = []
    for s in range(batch):
        branch = dot_nn(context_parts[s], full_output) + bias_output
        firsts.append(normalize(tokens[s] + branch, gain_first, shift_first))
    hidden_in, normed_first, inverse_first = (jnp.concatenate(v, axis=0) for v in zip(*firsts))
    context_low = jnp.concatenate(context_parts, axis=0)
    hidden_low = hidden_in.astype(BF)
    halves = []
    reduced = bias_reduce
    for weight, back, bias in zip(expand_halves, reduce_halves, bias_halves):
        expand = dot_nn(hidden_low, weight) + bias
        cdf = 0.5 * (1.0 + lax.erf(expand * SQRT_HALF))
        active = (expand * cdf).astype(BF)
        slope = cdf + expand * DENSITY * jnp.exp(-0.5 * expand * expand)
        reduced = reduced + dot_nn(active, back)
        halves.append((weight, back, active, slope.astype(BF)))
    result, normed_second, inverse_second = normalize(hidden_in + reduced, gain_second, shift_second)

    grad_out = cotangent.reshape(batch * rows, width)
    grad_sum_second, grad_gain_second, grad_shift_second = normalize_back(
        grad_out, normed_second, inverse_second, gain_second
    )
    grad_reduced = grad_sum_second.astype(BF)
    grad_bias_reduce = column_sums(grad_reduced)

    def chip_sum(make):
        got = peer(make(1).astype(BF), 1)
        return (make(0) + got.astype(F32)).astype(BF)

    sum_reduce = chip_sum(lambda i: dot_tn(halves[i][2], grad_reduced))
    sum_reduce = lax.psum_scatter(sum_reduce, "fsdp", scatter_dimension=0, tiled=True)
    sum_reduce = reduce_even(jnp.split(sum_reduce, middle, axis=0), False)

    grad_hidden = grad_sum_second
    grad_expands = []
    for weight, back, active, slope in halves:
        grad_expand = (dot_nt(grad_reduced, back) * slope.astype(F32)).astype(BF)
        grad_hidden = grad_hidden + dot_nt(grad_expand, weight)
        grad_expands.append(grad_expand)
    grad_bias_expand = [column_sums(g).reshape(depth, middle, piece) for g in grad_expands]
    grad_pre, grad_gain_first, grad_shift_first = normalize_back(
        grad_hidden, normed_first, inverse_first, gain_first
    )
    grad_branch = grad_pre.astype(BF)
    grad_bias_output = column_sums(grad_branch)
    grad_context = dot_nt(grad_branch, full_output).astype(BF)

    sum_expand = chip_sum(lambda i: dot_tn(hidden_low, grad_expands[i])).reshape(width, depth, middle, piece)
    sum_expand = reduce_even([sum_expand[:, :, i].reshape(width, block) for i in range(middle)], True)
    branch_blocks = jnp.concatenate(
        [lax.dynamic_slice_in_dim(grad_branch, (me ^ k) * own_width, own_width, 1) for k in order], axis=1
    )
    sum_output = chip_sum(
        lambda i: dot_tn(context_low, branch_blocks[:, i * width // 2 : (i + 1) * width // 2])
    )
    sum_output = reduce_even(jnp.split(sum_output, middle, axis=1), False)
    sum_expand = jnp.concatenate([sum_expand, sum_output], axis=1)
    sum_expand = lax.psum_scatter(sum_expand, "fsdp", scatter_dimension=0, tiled=True)

    grads = []
    for s in range(batch):
        even, odd, qkv, mask_q, mask_k, out, lse = kept[s]
        dc = lanes(rows_to_heads(grad_context[s * rows : (s + 1) * rows], own_width))
        got = attend_back(qkv, mask_q, mask_k, dc, out, lse, heads, rows)
        if own_width != LANES:
            got = jnp.concatenate([got[:, i * LANES : i * LANES + own_width] for i in range(3)], axis=1)
        grads.append(got)
    middle_row = count * rows // 2
    grad_heads = sum(
        dot_tn(kept[s][0], grads[s][:middle_row]) + dot_tn(kept[s][1], grads[s][middle_row:]) for s in range(batch)
    ).astype(BF)
    grad_head_bias = jnp.pad(
        jnp.stack(in_terms(sum(column_sums(g) for g in grads), 2)), ((0, 14), (0, 0))
    )
    home_heads = jnp.concatenate(
        [grad_heads.reshape(depth, shard, line), jnp.broadcast_to(grad_head_bias, (depth, 16, line))], axis=1
    )
    home_heads = reduce_shards(home_heads)
    home_heads = jnp.concatenate(
        [home_heads[:shard].astype(BF)]
        + [v[None] for v in in_terms(home_heads[shard] + home_heads[shard + 1], 2)]
        + [jnp.zeros((14, line), BF)],
        axis=0,
    )
    back_rows = [heads_to_rows(g) for g in grads]
    back_even = jnp.concatenate([jnp.concatenate(r[:middle], axis=1) for r in back_rows], axis=0)
    back_odd = jnp.concatenate([jnp.concatenate(r[middle:], axis=1) for r in back_rows], axis=0)
    grad_in = grad_pre + dot_nt(back_even, half_heads) + dot_nt(back_odd, other_heads)

    def spread(value, low_first):
        got = gather_even(value, low_first)
        odd = peer(jnp.stack(got), 1)
        return by_owner([v[None] for v in got] + [odd[i : i + 1] for i in range(middle)], 0)

    wide = lax.all_gather(sum_expand, "ctx", axis=0)
    grad_expand_weight = jnp.transpose(wide[:, :, :block].reshape(count, shard, depth, piece), (1, 2, 0, 3))
    grad_expand_weight = grad_expand_weight.reshape(shard, hidden).astype(F32)
    grad_output_weight = jnp.transpose(wide[:, :, block:], (1, 0, 2)).reshape(shard, width).astype(F32)
    grad_reduce_weight = lax.all_gather(sum_reduce, "ctx", axis=0, tiled=True).astype(F32)
    wide_heads = spread(home_heads, True)
    wide_shards = jnp.transpose(wide_heads[:, :shard].reshape(count, shard, 3, own_width), (2, 1, 0, 3))
    grad_query_weight, grad_key_weight, grad_value_weight = (
        wide_shards[i].reshape(shard, width).astype(F32) for i in range(3)
    )
    wide_biases = jnp.sum(wide_heads[:, shard : shard + 2].astype(F32), axis=1).reshape(count, 3, own_width)
    own_shard = lambda v: lax.dynamic_slice_in_dim(v.reshape(width), my_shard * shard, shard, 0)

    vectors = (
        grad_bias_output,
        grad_gain_first,
        grad_shift_first,
        grad_bias_reduce,
        grad_gain_second,
        grad_shift_second,
    )
    wide_bias = by_owner([g[:, i] for g in grad_bias_expand for i in range(middle)], 1)
    small = jnp.concatenate([v.reshape(depth, shard) for v in vectors] + [wide_bias], axis=1)
    for b in range(count.bit_length() - 1):
        small = small + peer(small, 1 << b)
    small = reduce_shards(small)
    vec = [small[i * shard : (i + 1) * shard] for i in range(len(vectors))]
    vec_expand = small[len(vectors) * shard :]
    return (
        result.reshape(batch, rows, width),
        grad_in.reshape(batch, rows, width),
        grad_query_weight,
        own_shard(wide_biases[:, 0]),
        grad_key_weight,
        grad_value_weight,
        own_shard(wide_biases[:, 2]),
        grad_output_weight,
        vec[0],
        vec[1],
        vec[2],
        grad_expand_weight,
        vec_expand,
        grad_reduce_weight,
        vec[3],
        vec[4],
        vec[5],
    )


def even_pieces(own, other):
    rows = own.shape[0]
    both = jnp.concatenate([own, other], axis=1)
    middle = lax.axis_size("ctx") // 2
    rows = rows // middle
    pieces = [both[i * rows : (i + 1) * rows] for i in range(middle)]
    return [pieces[0]] + [peer(pieces[i], 2 * i) for i in range(1, middle)]


def body(
    tokens,
    segments,
    query_weight,
    query_bias,
    key_weight,
    value_weight,
    value_bias,
    output_weight,
    output_bias,
    first_gain,
    first_shift,
    expand_weight,
    expand_bias,
    reduce_weight,
    reduce_bias,
    second_gain,
    second_shift,
    cotangent,
):
    batch, rows, width = tokens.shape
    count, depth = lax.axis_size("ctx"), lax.axis_size("fsdp")
    me, my_shard = lax.axis_index("ctx"), lax.axis_index("fsdp")
    me_array = me.astype(jnp.int32).reshape(1)
    shard = query_weight.shape[0]
    hidden = expand_weight.shape[1]
    own_width = width // count
    heads = own_width // HEAD
    piece = hidden // depth // count
    block = depth * piece
    middle = count // 2
    order = plane_order()
    evens, odds = order[:middle], order[middle:]
    scale = HEAD**-0.5
    bits = (count * rows - 1).bit_length()
    all_rows = batch * rows

    columns = lambda w: lax.dynamic_slice_in_dim(w, me * own_width, own_width, 1).astype(BF)
    names = (query_bias, value_bias, output_bias, first_gain, first_shift, reduce_bias, second_gain, second_shift)
    packed = jnp.concatenate(names + (expand_bias,))
    size = packed.shape[0]
    terms = jnp.concatenate(in_terms(packed, 3))
    line = 3 * own_width
    lines = -(-terms.shape[0] // (16 * line)) * 16
    terms = jnp.pad(terms, (0, lines * line - terms.shape[0])).reshape(lines, line)
    own_heads = jnp.concatenate([columns(query_weight), columns(key_weight), columns(value_weight)], axis=1)
    own_heads = gather_shards(jnp.concatenate([own_heads, terms], axis=0))
    packed = own_heads[:, shard:].reshape(depth, lines * line)[:, : 3 * size]
    packed = jnp.sum(packed.reshape(depth, 3, -1).astype(F32), axis=1)
    own_heads = own_heads[:, :shard].reshape(width, line)
    (bias_query, bias_value, bias_output, gain_first, shift_first, bias_reduce, gain_second, shift_second) = (
        packed[:, i * shard : (i + 1) * shard].reshape(width) for i in range(len(names))
    )
    wide_bias = packed[:, len(names) * shard :].reshape(depth, count, piece)
    bias_halves = [
        jnp.stack([lax.dynamic_index_in_dim(wide_bias, me ^ k, 1, keepdims=False).reshape(1, block) for k in ks])
        for ks in (evens, odds)
    ]
    own_part = lambda v: lax.dynamic_slice_in_dim(v, me * own_width, own_width, 0)
    head_bias = jnp.concatenate([own_part(bias_query), jnp.zeros((own_width,), F32), own_part(bias_value)])
    head_scale = jnp.concatenate([jnp.full((own_width,), scale * LOG2E, F32), jnp.ones((2 * own_width,), F32)])

    thin = shard // count
    folds = width // block
    strip = lax.dynamic_slice_in_dim(output_weight, me * thin, thin, 0).astype(BF)
    strip = jnp.concatenate([strip[:, i * block : (i + 1) * block] for i in range(folds)], axis=0)
    block_expand = [
        lax.dynamic_slice_in_dim(expand_weight, (z * count + me) * piece, piece, 1).astype(BF) for z in range(depth)
    ]
    block_expand = jnp.concatenate([jnp.concatenate(block_expand, axis=1), strip], axis=0)
    block_expand = lax.all_gather(block_expand, "fsdp", axis=0)

    reduce_blocks = [lax.dynamic_slice_in_dim(reduce_weight, (me ^ k) * piece, piece, 0).astype(BF) for k in evens]
    reduce_own = lax.all_gather(jnp.stack(reduce_blocks), "fsdp", axis=0)

    def plane(value):
        first, second = peer(value, 2), peer(value, 4)
        part = value.shape[0] // 2
        return first, second, (peer(first[:part], 4), peer(second[part:], 2))

    def chip(blocks):
        return blocks + [jax.tree.map(lambda v: peer(v, 1), b) for b in blocks]

    low_in = [tokens[s].astype(BF) for s in range(batch)]
    first = plane(low_in[0])
    seg = after(segments, first[0])
    for b in range(count.bit_length() - 1):
        seg = jnp.concatenate([seg, peer(seg, 1 << b)], axis=1)
    seg = seg.reshape(batch, count, rows)
    seg = jnp.concatenate([seg[:, k] for k in order], axis=1)
    masks = [mask_columns(seg[s], bits) for s in range(batch)]
    second = plane(after(low_in[1], first[0], first[1]))
    kept = []
    for s, got in enumerate((first, second)):
        blocks = chip([(low_in[s],), (got[0],), (got[1],), got[2]])
        blocks = [v for b in blocks for v in b]
        qkv = project(blocks, own_heads, head_bias, head_scale)
        if s == 0:
            qkv = after(qkv, second[0], second[1])
        out, lse = attend(qkv, *masks[s], heads, rows)
        kept.append((blocks, qkv, *masks[s], out, lse))
    sent = [kept[s][4] for s in range(batch)]

    expand_plane = plane(after(block_expand, sent[0]))
    got_expand = chip([(block_expand,), (expand_plane[0],), (expand_plane[1],), expand_plane[2]])
    full_output = assemble_output(got_expand, shard, thin, me_array)

    earlier = None
    for s in range(batch):
        half = sent[s].shape[0] // 2
        pieces = even_pieces(sent[s][:half], peer(sent[s][half:], 1))
        earlier = branch(s, me_array, pieces, full_output, tokens, bias_output, gain_first, shift_first, earlier)
    context_low, hidden_in, hidden_low, normed_first, inverse_first = (
        v.reshape(all_rows, v.shape[2]) for v in earlier
    )

    act_even, act_odd, slope_even, slope_odd = expand_forward(hidden_low, bias_halves, got_expand, shard)
    reduce_own = after(reduce_own, hidden_low)
    reduce_halves = [reduce_own, peer(reduce_own, 1)]
    result, du_second, dr, sums_second = reduce_forward(
        (act_even, act_odd),
        reduce_halves,
        hidden_in,
        cotangent.reshape(all_rows, width),
        bias_reduce,
        gain_second,
        shift_second,
    )

    de_even, de_odd, sums_even, sums_odd, grad_pre, da, sums_first = feed_back(
        dr, reduce_halves, (slope_even, slope_odd), du_second, normed_first, inverse_first, gain_first, got_expand, shard
    )
    da_parts = da.reshape(batch, rows, width)
    own_grads, other_grads = zip(
        *(context_back(s, me_array, da_parts, full_output, own_width, middle) for s in range(batch))
    )
    dc = [even_pieces(own_grads[0], peer(other_grads[0], 1))]

    other_low, other_context = peer(hidden_low, 1), peer(context_low, 1)
    other_de, other_da = peer(de_odd, 1), peer(da, 1)
    kept_a, sent_a, kept_b, sent_b = expand_gradient(
        me_array, hidden_low, other_low, context_low, other_context, de_even, other_de, da, other_da, own_width
    )
    got_a, got_b = peer(sent_a, 4), peer(sent_b, 2)

    other_act, other_dr = peer(act_odd, 1), peer(dr, 1)
    sum_reduce = reduce_gradient(act_even, other_act, dr, other_dr, depth, piece)

    dc[0][0] = after(dc[0][0], kept_a, sum_reduce)
    dc.append(even_pieces(own_grads[1], peer(other_grads[1], 1)))
    sum_reduce = lax.psum_scatter(sum_reduce, "fsdp", scatter_dimension=0, tiled=False)

    add = lambda a, b: (a.astype(F32) + b.astype(F32)).astype(BF)
    half = count * rows // 2
    before, head_sums = None, 0.0
    grad_in, grads = [], []
    for s in range(batch):
        blocks, qkv, mask_q, mask_k, out, lse = kept[s]
        grads.append(attend_back(qkv, mask_q, mask_k, dc[s], out, lse, heads, rows))
        if s == 0:
            got_a, got_b = after((got_a, got_b), grads[0])
            next_a, next_b = add(kept_a, got_a), add(kept_b, got_b)
            got_a, got_b = peer(next_a[1], 2), peer(next_b[1], 4)
        before, sums = heads_gradient(blocks, grads[s], before)
        head_sums = head_sums + sums[0]
        away = peer(dot_nt(grads[s][half:], own_heads).astype(BF), 1)
        home = (dot_nt(grads[s][:half], own_heads) + away.astype(F32)).astype(BF)
        if s == 0:
            dc[1][0] = after(dc[1][0], home)
        got = [home[:rows]] + [peer(home[i * rows : (i + 1) * rows], 2 * i) for i in range(1, middle)]
        grad_in.append((s, got))
    got_a, got_b = after((got_a, got_b), grads[1])
    sum_expand = jnp.concatenate([add(next_a[0], got_a), add(next_b[0], got_b)], axis=0)
    sum_expand = lax.psum_scatter(sum_expand, "fsdp", scatter_dimension=0, tiled=True)
    sum_reduce = reduce_even([after(sum_reduce, grads[1])[i] for i in range(middle)], False)
    grad_in = [
        grad_pre[s * rows : (s + 1) * rows] + sum(v.astype(F32) for v in got) for s, got in grad_in
    ]
    grad_heads = before
    grad_head_bias = jnp.pad(jnp.stack(in_terms(head_sums, 2)), ((0, 14), (0, 0)))
    home_heads = jnp.concatenate(
        [grad_heads.reshape(depth, shard, line), jnp.broadcast_to(grad_head_bias, (depth, 16, line))], axis=1
    )
    home_heads = reduce_shards(home_heads)
    home_heads = jnp.concatenate(
        [home_heads[:shard].astype(BF)]
        + [v[None] for v in in_terms(home_heads[shard] + home_heads[shard + 1], 2)]
        + [jnp.zeros((14, line), BF)],
        axis=0,
    )

    def spread(value):
        got = plane(value)
        got = (value, got[0], got[1], jnp.concatenate(got[2], axis=0))
        return [*got] + [peer(v, 1) for v in got]

    grad_query_weight, grad_key_weight, grad_value_weight, wide_biases = unpack_heads(
        me_array, spread(home_heads), shard, width
    )
    grad_expand_weight, grad_output_weight = unpack_expand(me_array, spread(sum_expand), depth, hidden, width)
    grad_reduce_weight = lax.all_gather(sum_reduce, "ctx", axis=0, tiled=True).astype(F32)
    own_shard = lambda v: lax.dynamic_slice_in_dim(v, my_shard * shard, shard, 0)

    vectors = (sums_first[2], sums_first[0], sums_first[1], sums_second[2], sums_second[0], sums_second[1])
    wide_bias = by_owner(
        [sums[i, 0].reshape(depth, 1, piece) for sums in (sums_even, sums_odd) for i in range(middle)], 1
    ).reshape(depth, hidden // depth)
    small = jnp.concatenate([v.reshape(depth, shard) for v in vectors] + [wide_bias], axis=1)
    for b in range(count.bit_length() - 1):
        small = small + peer(small, 1 << b)
    small = reduce_shards(small)
    vec = [small[i * shard : (i + 1) * shard] for i in range(len(vectors))]
    vec_expand = small[len(vectors) * shard :]
    return (
        result.reshape(batch, rows, width),
        jnp.stack(grad_in),
        grad_query_weight,
        own_shard(wide_biases[0]),
        grad_key_weight,
        grad_value_weight,
        own_shard(wide_biases[2]),
        grad_output_weight,
        vec[0],
        vec[1],
        vec[2],
        grad_expand_weight,
        vec_expand,
        grad_reduce_weight,
        vec[3],
        vec[4],
        vec[5],
    )


def solution(mesh):
    seq = P("fsdp", "ctx", None)
    mat = P("fsdp", None)
    vec = P("fsdp")
    in_specs = (
        seq,
        P("fsdp", "ctx"),
        mat,
        vec,
        mat,
        mat,
        vec,
        mat,
        vec,
        vec,
        vec,
        mat,
        vec,
        mat,
        vec,
        vec,
        vec,
        seq,
    )
    out_specs = (seq, seq, mat, vec, mat, mat, vec, mat, vec, vec, vec, mat, vec, mat, vec, vec, vec)
    count, depth = mesh.shape["ctx"], mesh.shape["fsdp"]

    def layer(*args):
        width, hidden = args[0].shape[2], args[11].shape[1]
        piece, own_width = hidden // depth // count, width // count
        tiled = count == 8 and args[0].shape[0] == 2 and piece % LANES == 0 and own_width == LANES
        tiled = tiled and width // depth // count % 16 == 0
        return (body if tiled else plain_body)(*args)

    return jax.shard_map(layer, mesh=mesh, in_specs=in_specs, out_specs=out_specs, check_vma=False)
```

time: 1540 us -> 511 us (0.33)
  waiting for transfers between devices: 789 us -> 155 us
  matrix products: 303 us -> 10.9 us
  Pallas kernels: 0 us -> 180 us
  blocking collectives: 130 us -> 0 us
  other arithmetic: 143 us -> 23.6 us
  local copies, waits for them, and re-layouts: 149 us -> 48 us
  starting transfers between devices: 2.22 us -> 72.8 us
    dot_general x72 -> x4, matrix products: 303 us -> 10.9 us  [dot_nt(): lax.dot_general(left, right, (((1,), (1,)), ((), ())), preferred_element_...]
    reduce_scatter x2, waiting for transfers between devices: 278 us -> 0.02 us  [the longest x1 0.02 us: body(): lax.psum_scatter(sum_reduce, 'fsdp', scatter_dimension=0, tiled=False)]
    pallas_call x0 -> x20, Pallas kernels: none -> 180 us  [the longest x2 49.6 us: attend_back(): pl.pallas_call(functools.partial(backward_kernel, heads=heads, steps=coun...]
    ppermute x22 -> x95, waiting for transfers between devices: 317 us -> 155 us  [exchange(): return lax.ppermute(value, axis, [(i, i ^ k) for i in range(count)])]
    all_gather x6 -> x3, waiting for transfers between devices: 135 us -> 0.01 us  [the longest x1 0.01 us: body(): block_expand = lax.all_gather(block_expand, 'fsdp', axis=0)]
    all_gather x10 -> x0, blocking collectives: 98.1 us -> none  [the longest x1 13.9 us: body(): lax.all_gather(expand_bias, 'fsdp', axis=0, tiled=True)]
    ppermute x22 -> x95, starting transfers between devices: 1.85 us -> 72.4 us  [exchange(): return lax.ppermute(value, axis, [(i, i ^ k) for i in range(count)])]
    psum x1 -> x0, waiting for transfers between devices: 58.6 us -> none  [body(): lax.psum(row_grads, 'ctx').astype(jnp.float32)]
  transfers between devices with their start and end apart: 31 -> 100, of which waited for: 26 -> 26; matrix products, arithmetic and copies ran while one was open for 33% -> 9% of each run, Pallas kernels for 0% -> 36%
where the time goes in v1:
time: 511 us; the launch traced here: 506 us
  Pallas kernels  180 us (35%)
  waiting for transfers between devices  155 us (30%)
  starting transfers between devices  72.8 us (14%)
  local copies, waits for them, and re-layouts  48 us (9%)
  other arithmetic  23.6 us (5%)
  between operations  15.8 us (3%)
  matrix products  10.9 us (2%)
    ppermute x95, waiting for transfers between devices, exchange(): return lax.ppermute(value, axis, [(i, i ^ k) for i in range(count)])  155 us
    ppermute x95, starting transfers between devices, exchange(): return lax.ppermute(value, axis, [(i, i ^ k) for i in range(count)])  72.4 us
    pallas_call x2, Pallas kernels, attend_back(): pl.pallas_call(functools.partial(backward_kernel, heads=heads, steps=coun...  49.6 us
    unnamed x255, local copies, waits for them, and re-layouts  33.2 us
    pallas_call x2, Pallas kernels, attend(): pl.pallas_call(functools.partial(forward_kernel, heads=heads), grid=(coun...  29.3 us
    pallas_call x1, Pallas kernels, feed_back(): pl.pallas_call(functools.partial(feed_back_kernel, middle=middle, depth=d...  21 us
    pallas_call x1, Pallas kernels, reduce_forward(): pl.pallas_call(functools.partial(reduce_kernel, steps=middle), grid=(midd...  13.9 us
    pallas_call x1, Pallas kernels, expand_gradient(): pl.pallas_call(functools.partial(expand_gradient_kernel, middle=middle),...  12.7 us
  transfers between devices with their start and end apart: 100, of which 26 were waited for; matrix products, arithmetic and copies ran while one was open for 9% of the time, Pallas kernels for 36%

profile of v1, /device:TPU:0, one launch (start us, length us, event | category | flops | bytes accessed | tf_op | source)
XLA Modules:
  0.0 506.5 jit_solution(6061263290855676518)
XLA Ops:
  7.3 1.8 convert.13
  9.3 3.0 collective-permute-start
  18.7 3.6 collective-permute-start.13
  23.1 1.7 fusion.12
  26.1 7.0 %collective-permute-done.13 = bf16[288,384]{1,0:T(8,128)(2,1)S(1)} collective-permute-done((bf16[288,384]{1,0:T(8,128)(2,1)}, bf16[288,384]{1,0:T(8,128)(2,1)S(1)}, u32[]{:S(2)}, u32[]{:S(2)}) %collective-permute-start.13) | collective-permute-done | bytes 221216 | tf_op jit(solution)/shard_map/ppermute | solution.py:35
  33.0 27.8 %collective-permute-done.12 = bf16[288,384]{1,0:T(8,128)(2,1)S(1)} collective-permute-done((bf16[288,384]{1,0:T(8,128)(2,1)}, bf16[288,384]{1,0:T(8,128)(2,1)S(1)}, u32[]{:S(2)}, u32[]{:S(2)}) %collective-permute-start.12) | collective-permute-done | bytes 221216 | tf_op jit(solution)/shard_map/ppermute | solution.py:35
  62.8 1.6 collective-permute-start.21
  67.0 5.0 collective-permute-done.15
  72.5 5.4 %collective-permute-done.16 = s32[2,1024]{1,0:T(2,128)S(1)} collective-permute-done((s32[2,1024]{1,0:T(2,128)S(1)}, s32[2,1024]{1,0:T(2,128)S(1)}, u32[]{:S(2)}, u32[]{:S(2)}) %collective-permute-start.16) | collective-permute-done | bytes 8224 | tf_op jit(solution)/shard_map/ppermute | solution.py:35
  79.9 2.3 select_convert_fusion
  82.2 4.7 collective-permute-done.22.refs_4_
  89.5 2.2 select_convert_fusion.1
  93.3 4.6 project.3.q.k.v.refs_0_.refs_1_.refs_2_
  100.5 14.6 %attend.3 = (bf16[2048,128]{1,0:T(8,128)(2,1)S(1)}, f32[2048,128]{1,0:T(8,128)S(1)}) custom-call(bf16[2048,384]{1,0:T(8,128)(2,1)S(1)} %copy-done.19, bf16[2048,384]{1,0:T(8,128)(2,1)S(1)} %copy-done.19, bf16[2048,384]{1,0:T(8,128)(2,1)S(1)} %copy-done.19, bf16[2048,128]{1,0:T(8,128)(2,1)S(1)} %get-tuple-element.237.mask_q.refs_3_, ...), custom_call_target="tpu_custom_call" | custom-call | flops 8589934592 | bytes 3145728 | tf_op jit(solution)/shard_map/attend/pallas_call | solution.py:214
  118.5 5.1 %project.2.q.k.v.refs_0_.refs_1_.refs_2_ = bf16[2048,384]{1,0:T(8,128)(2,1)} custom-call(bf16[256,1024]{1,0:T(8,128)(2,1)S(1)} %get-tuple-element.76.refs_0_, bf16[256,1024]{1,0:T(8,128)(2,1)S(1)} %collective-permute-done.2.refs_1_, bf16[256,1024]{1,0:T(8,128)(2,1)S(1)} %collective-permute-done.3.refs_2_, bf16[128,1024]{1,0:T(8,128)(2,1)} %collective-permute-done.4.refs_3_, ...), custom_call_target="tpu_custom_call" | custom-call | flops 1610612736 | bytes 5767168 | tf_op jit(solution)/shard_map/project/pallas_call | solution.py:318
  123.6 1.6 collective-permute-start.29
  126.6 14.8 %attend.2 = (bf16[2048,128]{1,0:T(8,128)(2,1)S(1)}, f32[2048,128]{1,0:T(8,128)S(1)}) custom-call(bf16[2048,384]{1,0:T(8,128)(2,1)S(1)} %copy-done.18, bf16[2048,384]{1,0:T(8,128)(2,1)S(1)} %copy-done.18, bf16[2048,384]{1,0:T(8,128)(2,1)S(1)} %copy-done.18, bf16[2048,128]{1,0:T(8,128)(2,1)S(1)} %copy-done.45, bf16[2048,128]{1,0:T(8,128)(2,1)S(1)} %copy-done.44), custom_call_target="tpu_custom_call" | custom-call | flops 8589934592 | bytes 3145728 | tf_op jit(solution)/shard_map/attend/pallas_call | solution.py:214
  143.2 6.6 %collective-permute-done.28.refs_1_.refs_4_.refs_10_ = bf16[4,320,512]{2,1,0:T(8,128)(2,1)S(1)} collective-permute-done((bf16[4,320,512]{2,1,0:T(8,128)(2,1)}, bf16[4,320,512]{2,1,0:T(8,128)(2,1)S(1)}, u32[]{:S(2)}, u32[]{:S(2)}) %collective-permute-start.28) | collective-permute-done | bytes 1310752 | tf_op jit(solution)/shard_map/ppermute | solution.py:35
  149.9 4.8 collective-permute-done.29.refs_2_.refs_5_.refs_11_
  154.6 1.6 collective-permute-start.30
  157.4 14.4 %collective-permute-done.30.refs_3_.refs_6_.refs_12_ = bf16[2,320,512]{2,1,0:T(8,128)(2,1)S(1)} collective-permute-done((bf16[2,320,512]{2,1,0:T(8,128)(2,1)S(1)}, bf16[2,320,512]{2,1,0:T(8,128)(2,1)S(1)}, u32[]{:S(2)}, u32[]{:S(2)}) %collective-permute-start.30) | collective-permute-done | bytes 655392 | tf_op jit(solution)/shard_map/ppermute | solution.py:35
  173.9 1.9 collective-permute-start.40
  177.5 1.9 collective-permute-start.20
  179.5 2.7 assemble_output.1.refs_4_.weight
  182.5 3.9 branch.2
  187.5 3.9 branch.3
  194.2 2.0 copy-done.21
  201.8 10.9 %expand.1 = (bf16[512,2048]{1,0:T(8,128)(2,1)}, bf16[512,2048]{1,0:T(8,128)(2,1)}, bf16[512,2048]{1,0:T(8,128)(2,1)}, bf16[512,2048]{1,0:T(8,128)(2,1)}) custom-call(bf16[512,1024]{1,0:T(8,128)(2,1)S(1)} %bitcast.234, f32[4,1,512]{2,1,0:T(1,128)S(1)} %pad_maximum_fusion.9.refs_1_, f32[4,1,512]{2,1,0:T(1,128)S(1)} %pad_maximum_fusion.10.refs_2_, ...), custom_call_target="tpu_custom_call" | custom-call | flops 4294967296 | bytes 16777216 | tf_op jit(solution)/shard_map/expand/pallas_call | solution.py:470
  212.9 1.6 copy-done.14
  214.5 13.9 %reduce.33 = (f32[512,1024]{1,0:T(8,128)}, f32[512,1024]{1,0:T(8,128)S(1)}, bf16[512,1024]{1,0:T(8,128)(2,1)S(1)}, f32[8,1024]{1,0:T(8,128)S(1)}) custom-call(bf16[512,2048]{1,0:T(8,128)(2,1)S(1)} %copy-done.14, bf16[512,2048]{1,0:T(8,128)(2,1)} %get-tuple-element.89.act_odd, bf16[4,4,128,1024]{3,2,1,0:T(8,128)(2,1)} %bitcast.248, ...), custom_call_target="tpu_custom_call" | custom-call | flops 4294967296 | bytes 16777216 | tf_op jit(solution)/shard_map/reduce/pallas_call | solution.py:538
  230.7 3.0 collective-permute-done.48.other_grad
  233.7 7.4 %reduce_gradient.1 = bf16[4,4,128,1024]{3,2,1,0:T(8,128)(2,1)} custom-call(bf16[512,2048]{1,0:T(8,128)(2,1)S(1)} %copy-done.14, bf16[512,2048]{1,0:T(8,128)(2,1)} %copy-done.92, bf16[512,1024]{1,0:T(8,128)(2,1)S(1)} %get-tuple-element.93.refs_0_.grad, bf16[512,1024]{1,0:T(8,128)(2,1)S(1)} %collective-permute-done.48.other_grad), custom_call_target="tpu_custom_call" | custom-call | flops 4294967296 | bytes 8388608 | tf_op jit(solution)/shard_map/reduce_gradient/pallas_call | solution.py:680
  242.1 21.0 %feed_back.1 = (bf16[512,2048]{1,0:T(8,128)(2,1)}, bf16[512,2048]{1,0:T(8,128)(2,1)}, f32[4,1,512]{2,1,0:T(1,128)}, f32[4,1,512]{2,1,0:T(1,128)}, f32[512,1024]{...) custom-call(bf16[512,1024]{1,0:T(8,128)(2,1)} %copy-done.63, bf16[4,4,128,1024]{3,2,1,0:T(8,128)(2,1)} %bitcast.249, ...), custom_call_target="tpu_custom_call" | custom-call | flops 8589934592 | bytes 25165824 | tf_op jit(solution)/shard_map/feed_back/pallas_call | solution.py:609
  270.1 2.2 collective-permute-start.51
  273.6 12.7 %expand_gradient.1 = (bf16[2,512,640]{2,1,0:T(8,128)(2,1)}, bf16[2,512,640]{2,1,0:T(8,128)(2,1)}, bf16[2,512,640]{2,1,0:T(8,128)(2,1)}, bf16[2,512,640]{2,1,0:T(8,128)(2,1)}) custom-call(s32[1]{0:T(128)} %bitcast.me, bf16[512,1024]{1,0:T(8,128)(2,1)} %bitcast.233, bf16[512,1024]{1,0:T(8,128)(2,1)} %collective-permute-done.43.other_low, ...), custom_call_target="tpu_custom_call" | custom-call | flops 5368709120 | bytes 8388608 | tf_op jit(solution)/shard_map/expand_gradient/pallas_call | solution.py:719
  288.5 24.9 %attend_back.2.refs_10_ = bf16[2048,384]{1,0:T(8,128)(2,1)} custom-call(bf16[2048,384]{1,0:T(8,128)(2,1)} %project.3.q.k.v.refs_0_.refs_1_.refs_2_, bf16[2048,384]{1,0:T(8,128)(2,1)} %project.3.q.k.v.refs_0_.refs_1_.refs_2_, bf16[2048,384]{1,0:T(8,128)(2,1)} %project.3.q.k.v.refs_0_.refs_1_.refs_2_, bf16[2048,128]{1,0:T(8,128)(2,1)} %copy-done.48, ...), custom_call_target="tpu_custom_call" | custom-call | flops 10737418240 | bytes 4194304 | tf_op jit(solution)/shard_map/attend_back/pallas_call | solution.py:284
  313.3 2.5 convolution_convert_fusion.1
  322.3 1.6 add_convert_fusion.3
  325.5 1.6 collective-permute-start.78
  327.1 2.6 add_convert_fusion.1
  331.1 24.7 %attend_back.3.refs_10_ = bf16[2048,384]{1,0:T(8,128)(2,1)} custom-call(bf16[2048,384]{1,0:T(8,128)(2,1)} %project.2.q.k.v.refs_0_.refs_1_.refs_2_, bf16[2048,384]{1,0:T(8,128)(2,1)} %project.2.q.k.v.refs_0_.refs_1_.refs_2_, bf16[2048,384]{1,0:T(8,128)(2,1)} %project.2.q.k.v.refs_0_.refs_1_.refs_2_, bf16[2048,128]{1,0:T(8,128)(2,1)} %get-tuple-element.238.mask_q.refs_3_, ...), custom_call_target="tpu_custom_call" | custom-call | flops 10737418240 | bytes 4194304 | tf_op jit(solution)/shard_map/attend_back/pallas_call | solution.py:284
  365.0 3.9 heads_gradient.2
  370.1 2.6 convolution_convert_fusion
  372.9 4.8 heads_gradient.3
  379.8 6.6 %collective-permute-done.94 = bf16[1,128,1024]{2,1,0:T(8,128)(2,1)S(1)} collective-permute-done((bf16[1,128,1024]{2,1,0:T(8,128)(2,1)S(1)}, bf16[1,128,1024]{2,1,0:T(8,128)(2,1)S(1)}, u32[]{:S(2)}, u32[]{:S(2)}) %collective-permute-start.94) | collective-permute-done | bytes 262176 | tf_op jit(solution)/shard_map/ppermute | solution.py:35
  389.1 3.1 collective-permute-done.88
  393.3 2.9 collective-permute-done.89
  397.2 2.7 collective-permute-start.91
  399.9 3.6 collective-permute-done.65
  408.7 6.1 %collective-permute-done.67.refs_1_ = bf16[272,384]{1,0:T(8,128)(2,1)S(1)} collective-permute-done((bf16[272,384]{1,0:T(8,128)(2,1)S(1)}, bf16[272,384]{1,0:T(8,128)(2,1)S(1)}, u32[]{:S(2)}, u32[]{:S(2)}) %collective-permute-start.67) | collective-permute-done | bytes 208928 | tf_op jit(solution)/shard_map/ppermute | solution.py:35
  414.8 1.6 collective-permute-start.69
  419.6 5.7 %collective-permute-done.70 = bf16[136,384]{1,0:T(8,128)(2,1)S(1)} collective-permute-done((bf16[136,384]{1,0:T(8,128)(2,1)S(1)}, bf16[136,384]{1,0:T(8,128)(2,1)S(1)}, u32[]{:S(2)}, u32[]{:S(2)}) %collective-permute-start.70) | collective-permute-done | bytes 104480 | tf_op jit(solution)/shard_map/ppermute | solution.py:35
  426.7 2.1 collective-permute-start.54
  430.0 2.0 unpack_heads.1
  433.0 3.1 add_convert_fusion
  436.1 22.3 %collective-permute-done.79.refs_1_ = bf16[256,640]{1,0:T(8,128)(2,1)S(1)} collective-permute-done((bf16[256,640]{1,0:T(8,128)(2,1)}, bf16[256,640]{1,0:T(8,128)(2,1)S(1)}, u32[]{:S(2)}, u32[]{:S(2)}) %collective-permute-start.79) | collective-permute-done | bytes 327712 | tf_op jit(solution)/shard_map/ppermute | solution.py:35
  458.5 2.3 collective-permute-start.81
  462.6 2.3 collective-permute-done.81
  464.9 2.1 collective-permute-start.62
  470.8 8.0 %collective-permute-done.63 = bf16[256,1024]{1,0:T(8,128)(2,1)S(1)} collective-permute-done((bf16[256,1024]{1,0:T(8,128)(2,1)S(1)}, bf16[256,1024]{1,0:T(8,128)(2,1)S(1)}, u32[]{:S(2)}, u32[]{:S(2)}) %collective-permute-start.63) | collective-permute-done | bytes 524320 | tf_op jit(solution)/shard_map/ppermute | solution.py:35
  478.8 9.5 %collective-permute-done.62 = bf16[256,1024]{1,0:T(8,128)(2,1)S(1)} collective-permute-done((bf16[256,1024]{1,0:T(8,128)(2,1)S(1)}, bf16[256,1024]{1,0:T(8,128)(2,1)S(1)}, u32[]{:S(2)}, u32[]{:S(2)}) %collective-permute-start.62) | collective-permute-done | bytes 524320 | tf_op jit(solution)/shard_map/ppermute | solution.py:35
  489.0 2.0 add_bitcast_fusion.1
  492.6 3.0 unpack_expand.1
  495.6 4.1 bitcast_convert_fusion
  (530 shorter events, 103.4 us)
Async XLA Ops:
  7.2 110.4 %all-gather.7.cloned.1.call-start = ((), (), s32[]{:S(2)}) async-start(), calls=%async_computation.4 | async-start | bytes 1638400 | tf_op jit(solution)/shard_map/all_gather | solution.py:1187
  9.3 52.4 %collective-permute-start = (bf16[256,1024]{1,0:T(8,128)(2,1)S(1)}, bf16[256,1024]{1,0:T(8,128)(2,1)S(1)}, u32[]{:S(2)}, u32[]{:S(2)}) collective-permute-start(bf16[256,1024]{1,0:T(8,128)(2,1)S(1)} %get-tuple-element.161.refs_0_), channel_id=1, source_target_pairs={{0,8},{4,12},{8,0},{12,4},{16,24},{20,28},{24,16},{28,20},{1,9},{5... | collective-permute-start | bytes 1572872 | tf_op jit(solution)/shard_map/ppermute | solution.py:35
  12.3 49.4 %collective-permute-start.1 = (bf16[256,1024]{1,0:T(8,128)(2,1)S(1)}, bf16[256,1024]{1,0:T(8,128)(2,1)}, u32[]{:S(2)}, u32[]{:S(2)}) collective-permute-start(bf16[256,1024]{1,0:T(8,128)(2,1)S(1)} %get-tuple-element.161.refs_0_), channel_id=1, source_target_pairs={{0,16},{4,20},{8,24},{12,28},{16,0},{20,4},{24,8},{28,12},{1,17},{... | collective-permute-start | bytes 1572872 | tf_op jit(solution)/shard_map/ppermute | solution.py:35
  15.8 178.4 %all-gather.9.cloned.1.call-start = ((), (), s32[]{:S(2)}) async-start(), calls=%async_computation.5 | async-start | bytes 5242880 | tf_op jit(solution)/shard_map/all_gather | solution.py:1190
  18.7 14.3 %collective-permute-start.13 = (bf16[288,384]{1,0:T(8,128)(2,1)}, bf16[288,384]{1,0:T(8,128)(2,1)S(1)}, u32[]{:S(2)}, u32[]{:S(2)}) collective-permute-start(bf16[288,384]{1,0:T(8,128)(2,1)} %get-tuple-element.193), channel_id=1, source_target_pairs={{0,3},{1,2},{2,1},{3,0},{4,7},{5,6},{6,5},{7,4},{8,11},{9,10},{10,... | collective-permute-start | bytes 663560 | tf_op jit(solution)/shard_map/ppermute | solution.py:35
  22.3 38.5 %collective-permute-start.12 = (bf16[288,384]{1,0:T(8,128)(2,1)}, bf16[288,384]{1,0:T(8,128)(2,1)S(1)}, u32[]{:S(2)}, u32[]{:S(2)}) collective-permute-start(bf16[288,384]{1,0:T(8,128)(2,1)} %get-tuple-element.193), channel_id=1, source_target_pairs={{0,2},{1,3},{2,0},{3,1},{4,6},{5,7},{6,4},{7,5},{8,10},{9,11},{10,... | collective-permute-start | bytes 663560 | tf_op jit(solution)/shard_map/ppermute | solution.py:35
  22.3 38.5 %collective-permute-start.11 = (bf16[288,384]{1,0:T(8,128)(2,1)}, bf16[288,384]{1,0:T(8,128)(2,1)S(1)}, u32[]{:S(2)}, u32[]{:S(2)}) collective-permute-start(bf16[288,384]{1,0:T(8,128)(2,1)} %get-tuple-element.193), channel_id=1, source_target_pairs={{0,1},{1,0},{2,3},{3,2},{4,5},{5,4},{6,7},{7,6},{8,9},{9,8},{10,11... | collective-permute-start | bytes 663560 | tf_op jit(solution)/shard_map/ppermute | solution.py:35
  26.0 332.0 %reduce-scatter.5.cloned.1.call-start = ((), (), s32[]{:S(2)}) async-start(), calls=%async_computation.3 | async-start | bytes 5242880 | tf_op jit(solution)/shard_map/reduce_scatter | solution.py:1267
  33.0 54.4 %collective-permute-start.23 = (bf16[256,1024]{1,0:T(8,128)(2,1)S(1)}, bf16[256,1024]{1,0:T(8,128)(2,1)S(1)}, u32[]{:S(2)}, u32[]{:S(2)}) collective-permute-start(bf16[256,1024]{1,0:T(8,128)(2,1)S(1)} %get-tuple-element.161.refs_0_), channel_id=1, source_target_pairs={{0,4},{4,0},{8,12},{12,8},{16,20},{20,16},{24,28},{28,24},{1,5},{5... | collective-permute-start | bytes 1572872 | tf_op jit(solution)/shard_map/ppermute | solution.py:35
  61.7 18.0 %collective-permute-start.2 = (bf16[256,1024]{1,0:T(8,128)(2,1)S(1)}, bf16[256,1024]{1,0:T(8,128)(2,1)S(1)}, u32[]{:S(2)}, u32[]{:S(2)}) collective-permute-start(bf16[256,1024]{1,0:T(8,128)(2,1)S(1)} %get-tuple-element.76.refs_0_), channel_id=1, source_target_pairs={{0,8},{4,12},{8,0},{12,4},{16,24},{20,28},{24,16},{28,20},{1,9},{5... | collective-permute-start | bytes 1572872 | tf_op jit(solution)/shard_map/ppermute | solution.py:35
  62.3 24.6 %collective-permute-start.3 = (bf16[256,1024]{1,0:T(8,128)(2,1)S(1)}, bf16[256,1024]{1,0:T(8,128)(2,1)S(1)}, u32[]{:S(2)}, u32[]{:S(2)}) collective-permute-start(bf16[256,1024]{1,0:T(8,128)(2,1)S(1)} %get-tuple-element.76.refs_0_), channel_id=1, source_target_pairs={{0,16},{4,20},{8,24},{12,28},{16,0},{20,4},{24,8},{28,12},{1,17},{... | collective-permute-start | bytes 1572872 | tf_op jit(solution)/shard_map/ppermute | solution.py:35
  62.8 15.2 %collective-permute-start.21 = (bf16[128,1024]{1,0:T(8,128)(2,1)S(1)}, bf16[128,1024]{1,0:T(8,128)(2,1)S(1)}, u32[]{:S(2)}, u32[]{:S(2)}) collective-permute-start(bf16[128,1024]{1,0:T(8,128)(2,1)S(1)} %slice.455), channel_id=1, source_target_pairs={{0,16},{4,20},{8,24},{12,28},{16,0},{20,4},{24,8},{28,12},{1,17},{... | collective-permute-start | bytes 786440 | tf_op jit(solution)/shard_map/ppermute | solution.py:35
  79.7 12.0 %collective-permute-start.25 = (bf16[256,1024]{1,0:T(8,128)(2,1)}, bf16[256,1024]{1,0:T(8,128)(2,1)S(1)}, u32[]{:S(2)}, u32[]{:S(2)}) collective-permute-start(bf16[256,1024]{1,0:T(8,128)(2,1)} %collective-permute-done.1.refs_2_), channel_id=1, source_target_pairs={{0,4},{4,0},{8,12},{12,8},{16,20},{20,16},{24,28},{28,24},{1,5},{5... | collective-permute-start | bytes 1572872 | tf_op jit(solution)/shard_map/ppermute | solution.py:35
  87.4 11.1 %collective-permute-start.4 = (bf16[128,1024]{1,0:T(8,128)(2,1)S(1)}, bf16[128,1024]{1,0:T(8,128)(2,1)}, u32[]{:S(2)}, u32[]{:S(2)}) collective-permute-start(bf16[128,1024]{1,0:T(8,128)(2,1)S(1)} %slice.432), channel_id=1, source_target_pairs={{0,16},{4,20},{8,24},{12,28},{16,0},{20,4},{24,8},{28,12},{1,17},{... | collective-permute-start | bytes 786440 | tf_op jit(solution)/shard_map/ppermute | solution.py:35
  88.0 10.8 %collective-permute-start.5 = (bf16[128,1024]{1,0:T(8,128)(2,1)S(1)}, bf16[128,1024]{1,0:T(8,128)(2,1)}, u32[]{:S(2)}, u32[]{:S(2)}) collective-permute-start(bf16[128,1024]{1,0:T(8,128)(2,1)S(1)} %slice.433), channel_id=1, source_target_pairs={{0,8},{4,12},{8,0},{12,4},{16,24},{20,28},{24,16},{28,20},{1,9},{5... | collective-permute-start | bytes 786440 | tf_op jit(solution)/shard_map/ppermute | solution.py:35
  91.7 25.9 %collective-permute-start.6 = (bf16[256,1024]{1,0:T(8,128)(2,1)S(1)}, bf16[256,1024]{1,0:T(8,128)(2,1)S(1)}, u32[]{:S(2)}, u32[]{:S(2)}) collective-permute-start(bf16[256,1024]{1,0:T(8,128)(2,1)S(1)} %get-tuple-element.76.refs_0_), channel_id=1, source_target_pairs={{0,4},{4,0},{8,12},{12,8},{16,20},{20,16},{24,28},{28,24},{1,5},{5... | collective-permute-start | bytes 1572872 | tf_op jit(solution)/shard_map/ppermute | solution.py:35
  97.9 20.1 %collective-permute-start.7 = (bf16[256,1024]{1,0:T(8,128)(2,1)S(1)}, bf16[256,1024]{1,0:T(8,128)(2,1)S(1)}, u32[]{:S(2)}, u32[]{:S(2)}) collective-permute-start(bf16[256,1024]{1,0:T(8,128)(2,1)S(1)} %collective-permute-done.2.refs_1_), channel_id=1, source_target_pairs={{0,4},{4,0},{8,12},{12,8},{16,20},{20,16},{24,28},{28,24},{1,5},{5... | collective-permute-start | bytes 1572872 | tf_op jit(solution)/shard_map/ppermute | solution.py:35
  98.2 20.3 %collective-permute-start.8 = (bf16[256,1024]{1,0:T(8,128)(2,1)S(1)}, bf16[256,1024]{1,0:T(8,128)(2,1)}, u32[]{:S(2)}, u32[]{:S(2)}) collective-permute-start(bf16[256,1024]{1,0:T(8,128)(2,1)S(1)} %collective-permute-done.3.refs_2_), channel_id=1, source_target_pairs={{0,4},{4,0},{8,12},{12,8},{16,20},{20,16},{24,28},{28,24},{1,5},{5... | collective-permute-start | bytes 1572872 | tf_op jit(solution)/shard_map/ppermute | solution.py:35
  98.5 20.0 %collective-permute-start.9 = (bf16[128,1024]{1,0:T(8,128)(2,1)}, bf16[128,1024]{1,0:T(8,128)(2,1)}, u32[]{:S(2)}, u32[]{:S(2)}) collective-permute-start(bf16[128,1024]{1,0:T(8,128)(2,1)} %collective-permute-done.4.refs_3_), channel_id=1, source_target_pairs={{0,4},{4,0},{8,12},{12,8},{16,20},{20,16},{24,28},{28,24},{1,5},{5... | collective-permute-start | bytes 786440 | tf_op jit(solution)/shard_map/ppermute | solution.py:35
  98.8 19.8 %collective-permute-start.10 = (bf16[128,1024]{1,0:T(8,128)(2,1)}, bf16[128,1024]{1,0:T(8,128)(2,1)}, u32[]{:S(2)}, u32[]{:S(2)}) collective-permute-start(bf16[128,1024]{1,0:T(8,128)(2,1)} %collective-permute-done.5.refs_4_), channel_id=1, source_target_pairs={{0,4},{4,0},{8,12},{12,8},{16,20},{20,16},{24,28},{28,24},{1,5},{5... | collective-permute-start | bytes 786440 | tf_op jit(solution)/shard_map/ppermute | solution.py:35
  117.7 23.9 %collective-permute-start.37 = (bf16[1024,128]{1,0:T(8,128)(2,1)}, bf16[1024,128]{1,0:T(8,128)(2,1)S(1)}, u32[]{:S(2)}, u32[]{:S(2)}) collective-permute-start(bf16[1024,128]{1,0:T(8,128)(2,1)} %get-tuple-element.182), channel_id=1, source_target_pairs={{0,4},{4,0},{8,12},{12,8},{16,20},{20,16},{24,28},{28,24},{1,5},{5... | collective-permute-start | bytes 786440 | tf_op jit(solution)/shard_map/ppermute | solution.py:35
  118.0 31.8 %collective-permute-start.28 = (bf16[4,320,512]{2,1,0:T(8,128)(2,1)}, bf16[4,320,512]{2,1,0:T(8,128)(2,1)S(1)}, u32[]{:S(2)}, u32[]{:S(2)}) collective-permute-start(bf16[4,320,512]{2,1,0:T(8,128)(2,1)} %bitcast.225), channel_id=1, source_target_pairs={{0,8},{4,12},{8,0},{12,4},{16,24},{20,28},{24,16},{28,20},{1,9},{5... | collective-permute-start | bytes 3932168 | tf_op jit(solution)/shard_map/ppermute | solution.py:35
  123.6 31.0 %collective-permute-start.29 = (bf16[4,320,512]{2,1,0:T(8,128)(2,1)S(1)}, bf16[4,320,512]{2,1,0:T(8,128)(2,1)S(1)}, u32[]{:S(2)}, u32[]{:S(2)}) collective-permute-start(bf16[4,320,512]{2,1,0:T(8,128)(2,1)S(1)} %bitcast.227), channel_id=1, source_target_pairs={{0,16},{4,20},{8,24},{12,28},{16,0},{20,4},{24,8},{28,12},{1,17},{... | collective-permute-start | bytes 3932168 | tf_op jit(solution)/shard_map/ppermute | solution.py:35
  141.5 14.8 %collective-permute-start.17 = (bf16[1024,128]{1,0:T(8,128)(2,1)S(1)}, bf16[1024,128]{1,0:T(8,128)(2,1)S(1)}, u32[]{:S(2)}, u32[]{:S(2)}) collective-permute-start(bf16[1024,128]{1,0:T(8,128)(2,1)S(1)} %get-tuple-element.188), channel_id=1, source_target_pairs={{0,4},{4,0},{8,12},{12,8},{16,20},{20,16},{24,28},{28,24},{1,5},{5... | collective-permute-start | bytes 786440 | tf_op jit(solution)/shard_map/ppermute | solution.py:35
  141.6 13.0 %collective-permute-start.38 = (bf16[256,256]{1,0:T(8,128)(2,1)S(1)}, bf16[256,256]{1,0:T(8,128)(2,1)S(1)}, u32[]{:S(2)}, u32[]{:S(2)}) collective-permute-start(bf16[256,256]{1,0:T(8,128)(2,1)S(1)} %get-tuple-element.180), channel_id=1, source_target_pairs={{0,8},{4,12},{8,0},{12,4},{16,24},{20,28},{24,16},{28,20},{1,9},{5... | collective-permute-start | bytes 393224 | tf_op jit(solution)/shard_map/ppermute | solution.py:35
  143.0 30.2 %collective-permute-start.32 = (bf16[4,320,512]{2,1,0:T(8,128)(2,1)S(1)}, bf16[4,320,512]{2,1,0:T(8,128)(2,1)S(1)}, u32[]{:S(2)}, u32[]{:S(2)}) collective-permute-start(bf16[4,320,512]{2,1,0:T(8,128)(2,1)S(1)} %bitcast.228), channel_id=1, source_target_pairs={{0,4},{4,0},{8,12},{12,8},{16,20},{20,16},{24,28},{28,24},{1,5},{5... | collective-permute-start | bytes 3932168 | tf_op jit(solution)/shard_map/ppermute | solution.py:35
  149.8 24.1 %collective-permute-start.33 = (bf16[4,320,512]{2,1,0:T(8,128)(2,1)S(1)}, bf16[4,320,512]{2,1,0:T(8,128)(2,1)S(1)}, u32[]{:S(2)}, u32[]{:S(2)}) collective-permute-start(bf16[4,320,512]{2,1,0:T(8,128)(2,1)S(1)} %collective-permute-done.28.refs_1_.refs_4_.refs_10_), channel_id=1, source_target_pairs={{0,4},{4,0},{8,12},{12,8},{16,20},{20,16},{24,28},{28,24},{1,5},{5... | collective-permute-start | bytes 3932168 | tf_op jit(solution)/shard_map/ppermute | solution.py:35
  154.6 21.2 %collective-permute-start.34 = (bf16[4,320,512]{2,1,0:T(8,128)(2,1)S(1)}, bf16[4,320,512]{2,1,0:T(8,128)(2,1)S(1)}, u32[]{:S(2)}, u32[]{:S(2)}) collective-permute-start(bf16[4,320,512]{2,1,0:T(8,128)(2,1)S(1)} %collective-permute-done.29.refs_2_.refs_5_.refs_11_), channel_id=1, source_target_pairs={{0,4},{4,0},{8,12},{12,8},{16,20},{20,16},{24,28},{28,24},{1,5},{5... | collective-permute-start | bytes 3932168 | tf_op jit(solution)/shard_map/ppermute | solution.py:35
  154.6 17.1 %collective-permute-start.30 = (bf16[2,320,512]{2,1,0:T(8,128)(2,1)S(1)}, bf16[2,320,512]{2,1,0:T(8,128)(2,1)S(1)}, u32[]{:S(2)}, u32[]{:S(2)}) collective-permute-start(bf16[2,320,512]{2,1,0:T(8,128)(2,1)S(1)} %slice.458), channel_id=1, source_target_pairs={{0,16},{4,20},{8,24},{12,28},{16,0},{20,4},{24,8},{28,12},{1,17},{... | collective-permute-start | bytes 1966088 | tf_op jit(solution)/shard_map/ppermute | solution.py:35
  156.3 16.9 %collective-permute-start.31 = (bf16[2,320,512]{2,1,0:T(8,128)(2,1)S(1)}, bf16[2,320,512]{2,1,0:T(8,128)(2,1)S(1)}, u32[]{:S(2)}, u32[]{:S(2)}) collective-permute-start(bf16[2,320,512]{2,1,0:T(8,128)(2,1)S(1)} %slice.459), channel_id=1, source_target_pairs={{0,8},{4,12},{8,0},{12,4},{16,24},{20,28},{24,16},{28,20},{1,9},{5... | collective-permute-start | bytes 1966088 | tf_op jit(solution)/shard_map/ppermute | solution.py:35
  176.9 10.6 %collective-permute-start.19 = (bf16[256,256]{1,0:T(8,128)(2,1)S(1)}, bf16[256,256]{1,0:T(8,128)(2,1)S(1)}, u32[]{:S(2)}, u32[]{:S(2)}) collective-permute-start(bf16[256,256]{1,0:T(8,128)(2,1)S(1)} %get-tuple-element.187), channel_id=1, source_target_pairs={{0,16},{4,20},{8,24},{12,28},{16,0},{20,4},{24,8},{28,12},{1,17},{... | collective-permute-start | bytes 393224 | tf_op jit(solution)/shard_map/ppermute | solution.py:35
  194.1 18.7 %collective-permute-start.41 = (bf16[4,4,128,1024]{3,2,1,0:T(8,128)(2,1)}, bf16[4,4,128,1024]{3,2,1,0:T(8,128)(2,1)}, u32[]{:S(2)}, u32[]{:S(2)}) collective-permute-start(bf16[4,4,128,1024]{3,2,1,0:T(8,128)(2,1)} %bitcast.247), channel_id=1, source_target_pairs={{0,4},{4,0},{8,12},{12,8},{16,20},{20,16},{24,28},{28,24},{1,5},{5... | collective-permute-start | bytes 12582920 | tf_op jit(solution)/shard_map/ppermute | solution.py:35
  212.7 18.0 %collective-permute-start.47 = (bf16[512,2048]{1,0:T(8,128)(2,1)}, bf16[512,2048]{1,0:T(8,128)(2,1)S(1)}, u32[]{:S(2)}, u32[]{:S(2)}) collective-permute-start(bf16[512,2048]{1,0:T(8,128)(2,1)} %get-tuple-element.89.act_odd), channel_id=1, source_target_pairs={{0,4},{4,0},{8,12},{12,8},{16,20},{20,16},{24,28},{28,24},{1,5},{5... | collective-permute-start | bytes 6291464 | tf_op jit(solution)/shard_map/ppermute | solution.py:35
  230.2 38.6 %collective-permute-start.43 = (bf16[512,1024]{1,0:T(8,128)(2,1)S(1)}, bf16[512,1024]{1,0:T(8,128)(2,1)}, u32[]{:S(2)}, u32[]{:S(2)}) collective-permute-start(bf16[512,1024]{1,0:T(8,128)(2,1)S(1)} %bitcast.235), channel_id=1, source_target_pairs={{0,4},{4,0},{8,12},{12,8},{16,20},{20,16},{24,28},{28,24},{1,5},{5... | collective-permute-start | bytes 3145736 | tf_op jit(solution)/shard_map/ppermute | solution.py:35
  230.2 39.6 %collective-permute-start.44 = (bf16[512,1024]{1,0:T(8,128)(2,1)S(1)}, bf16[512,1024]{1,0:T(8,128)(2,1)}, u32[]{:S(2)}, u32[]{:S(2)}) collective-permute-start(bf16[512,1024]{1,0:T(8,128)(2,1)S(1)} %bitcast.232), channel_id=1, source_target_pairs={{0,4},{4,0},{8,12},{12,8},{16,20},{20,16},{24,28},{28,24},{1,5},{5... | collective-permute-start | bytes 3145736 | tf_op jit(solution)/shard_map/ppermute | solution.py:35
  242.1 189.9 %reduce-scatter.3.cloned.1.call-start = ((), (), s32[]{:S(2)}) async-start(), calls=%async_computation.2 | async-start | bytes 1638400 | tf_op jit(solution)/shard_map/reduce_scatter | solution.py:1290
  267.7 49.3 %collective-permute-start.56 = (bf16[1024,128]{1,0:T(8,128)(2,1)S(1)}, bf16[1024,128]{1,0:T(8,128)(2,1)S(1)}, u32[]{:S(2)}, u32[]{:S(2)}) collective-permute-start(bf16[1024,128]{1,0:T(8,128)(2,1)S(1)} %get-tuple-element.111), channel_id=1, source_target_pairs={{0,4},{4,0},{8,12},{12,8},{16,20},{20,16},{24,28},{28,24},{1,5},{5... | collective-permute-start | bytes 786440 | tf_op jit(solution)/shard_map/ppermute | solution.py:35
  268.8 18.0 %collective-permute-start.49 = (bf16[256,256]{1,0:T(8,128)(2,1)S(1)}, bf16[256,256]{1,0:T(8,128)(2,1)S(1)}, u32[]{:S(2)}, u32[]{:S(2)}) collective-permute-start(bf16[256,256]{1,0:T(8,128)(2,1)S(1)} %get-tuple-element.176), channel_id=1, source_target_pairs={{0,8},{4,12},{8,0},{12,4},{16,24},{20,28},{24,16},{28,20},{1,9},{5... | collective-permute-start | bytes 393224 | tf_op jit(solution)/shard_map/ppermute | solution.py:35
  269.8 18.0 %collective-permute-start.50 = (bf16[256,256]{1,0:T(8,128)(2,1)S(1)}, bf16[256,256]{1,0:T(8,128)(2,1)S(1)}, u32[]{:S(2)}, u32[]{:S(2)}) collective-permute-start(bf16[256,256]{1,0:T(8,128)(2,1)S(1)} %get-tuple-element.175), channel_id=1, source_target_pairs={{0,16},{4,20},{8,24},{12,28},{16,0},{20,4},{24,8},{28,12},{1,17},{... | collective-permute-start | bytes 393224 | tf_op jit(solution)/shard_map/ppermute | solution.py:35
  270.1 17.7 %collective-permute-start.51 = (bf16[256,256]{1,0:T(8,128)(2,1)S(1)}, bf16[256,256]{1,0:T(8,128)(2,1)S(1)}, u32[]{:S(2)}, u32[]{:S(2)}) collective-permute-start(bf16[256,256]{1,0:T(8,128)(2,1)S(1)} %get-tuple-element.174), channel_id=1, source_target_pairs={{0,24},{4,28},{8,16},{12,20},{16,8},{20,12},{24,0},{28,4},{1,25},{... | collective-permute-start | bytes 393224 | tf_op jit(solution)/shard_map/ppermute | solution.py:35
  286.3 34.1 %collective-permute-start.75 = (bf16[2,512,640]{2,1,0:T(8,128)(2,1)}, bf16[2,512,640]{2,1,0:T(8,128)(2,1)S(1)}, u32[]{:S(2)}, u32[]{:S(2)}) collective-permute-start(bf16[2,512,640]{2,1,0:T(8,128)(2,1)} %get-tuple-element.121), channel_id=1, source_target_pairs={{0,16},{4,20},{8,24},{12,28},{16,0},{20,4},{24,8},{28,12},{1,17},{... | collective-permute-start | bytes 3932168 | tf_op jit(solution)/shard_map/ppermute | solution.py:35
  286.8 35.6 %collective-permute-start.76 = (bf16[2,512,640]{2,1,0:T(8,128)(2,1)}, bf16[2,512,640]{2,1,0:T(8,128)(2,1)S(1)}, u32[]{:S(2)}, u32[]{:S(2)}) collective-permute-start(bf16[2,512,640]{2,1,0:T(8,128)(2,1)} %get-tuple-element.122), channel_id=1, source_target_pairs={{0,8},{4,12},{8,0},{12,4},{16,24},{20,28},{24,16},{28,20},{1,9},{5... | collective-permute-start | bytes 3932168 | tf_op jit(solution)/shard_map/ppermute | solution.py:35
  317.8 12.0 %collective-permute-start.57 = (bf16[256,256]{1,0:T(8,128)(2,1)S(1)}, bf16[256,256]{1,0:T(8,128)(2,1)S(1)}, u32[]{:S(2)}, u32[]{:S(2)}) collective-permute-start(bf16[256,256]{1,0:T(8,128)(2,1)S(1)} %get-tuple-element.172), channel_id=1, source_target_pairs={{0,8},{4,12},{8,0},{12,4},{16,24},{20,28},{24,16},{28,20},{1,9},{5... | collective-permute-start | bytes 393224 | tf_op jit(solution)/shard_map/ppermute | solution.py:35
  318.8 10.9 %collective-permute-start.58 = (bf16[256,256]{1,0:T(8,128)(2,1)S(1)}, bf16[256,256]{1,0:T(8,128)(2,1)S(1)}, u32[]{:S(2)}, u32[]{:S(2)}) collective-permute-start(bf16[256,256]{1,0:T(8,128)(2,1)S(1)} %get-tuple-element.171), channel_id=1, source_target_pairs={{0,16},{4,20},{8,24},{12,28},{16,0},{20,4},{24,8},{28,12},{1,17},{... | collective-permute-start | bytes 393224 | tf_op jit(solution)/shard_map/ppermute | solution.py:35
  324.0 31.8 %collective-permute-start.77 = (bf16[512,640]{1,0:T(8,128)(2,1)S(1)}, bf16[512,640]{1,0:T(8,128)(2,1)S(1)}, u32[]{:S(2)}, u32[]{:S(2)}) collective-permute-start(bf16[512,640]{1,0:T(8,128)(2,1)S(1)} %slice_bitcast_fusion.2), channel_id=1, source_target_pairs={{0,8},{4,12},{8,0},{12,4},{16,24},{20,28},{24,16},{28,20},{1,9},{5... | collective-permute-start | bytes 1966088 | tf_op jit(solution)/shard_map/ppermute | solution.py:35
  325.5 30.3 %collective-permute-start.78 = (bf16[512,640]{1,0:T(8,128)(2,1)S(1)}, bf16[512,640]{1,0:T(8,128)(2,1)S(1)}, u32[]{:S(2)}, u32[]{:S(2)}) collective-permute-start(bf16[512,640]{1,0:T(8,128)(2,1)S(1)} %slice_bitcast_fusion.1), channel_id=1, source_target_pairs={{0,16},{4,20},{8,24},{12,28},{16,0},{20,4},{24,8},{28,12},{1,17},{... | collective-permute-start | bytes 1966088 | tf_op jit(solution)/shard_map/ppermute | solution.py:35
  357.4 138.2 %all-gather.11.cloned.1.call-start = ((), (), s32[]{:S(2)}) async-start(), calls=%async_computation.6 | async-start | bytes 2359296 | tf_op jit(solution)/shard_map/all_gather | solution.py:1317
  357.9 29.4 %collective-permute-start.87 = (f32[4,2560]{1,0:T(4,128)S(1)}, f32[4,2560]{1,0:T(4,128)}, u32[]{:S(2)}, u32[]{:S(2)}) collective-permute-start(f32[4,2560]{1,0:T(4,128)S(1)} %constant_dynamic-update-slice_fusion.37), channel_id=1, source_target_pairs={{0,4},{4,0},{8,12},{12,8},{16,20},{20,16},{24,28},{28,24},{1,5},{5... | collective-permute-start | bytes 122888 | tf_op jit(solution)/shard_map/ppermute | solution.py:35
  359.1 18.6 %collective-permute-start.93 = (bf16[2,128,1024]{2,1,0:T(8,128)(2,1)S(1)}, bf16[2,128,1024]{2,1,0:T(8,128)(2,1)S(1)}, u32[]{:S(2)}, u32[]{:S(2)}) collective-permute-start(bf16[2,128,1024]{2,1,0:T(8,128)(2,1)S(1)} %stack.58), channel_id=1, source_target_pairs={{0,16},{4,20},{8,24},{12,28},{16,0},{20,4},{24,8},{28,12},{1,17},{... | collective-permute-start | bytes 1572872 | tf_op jit(solution)/shard_map/ppermute | solution.py:35
  372.7 60.2 %collective-permute-start.60 = (bf16[1024,1024]{1,0:T(8,128)(2,1)}, bf16[1024,1024]{1,0:T(8,128)(2,1)}, u32[]{:S(2)}, u32[]{:S(2)}) collective-permute-start(bf16[1024,1024]{1,0:T(8,128)(2,1)} %convolution_convert_fusion), channel_id=1, source_target_pairs={{0,4},{4,0},{8,12},{12,8},{16,20},{20,16},{24,28},{28,24},{1,5},{5... | collective-permute-start | bytes 6291464 | tf_op jit(solution)/shard_map/ppermute | solution.py:35
  378.9 18.3 %collective-permute-start.66 = (bf16[272,384]{1,0:T(8,128)(2,1)S(1)}, bf16[272,384]{1,0:T(8,128)(2,1)S(1)}, u32[]{:S(2)}, u32[]{:S(2)}) collective-permute-start(bf16[272,384]{1,0:T(8,128)(2,1)S(1)} %get-tuple-element.169), channel_id=1, source_target_pairs={{0,3},{1,2},{2,1},{3,0},{4,7},{5,6},{6,5},{7,4},{8,11},{9,10},{10,... | collective-permute-start | bytes 626696 | tf_op jit(solution)/shard_map/ppermute | solution.py:35
  379.8 23.8 %collective-permute-start.65 = (bf16[272,384]{1,0:T(8,128)(2,1)S(1)}, bf16[272,384]{1,0:T(8,128)(2,1)}, u32[]{:S(2)}, u32[]{:S(2)}) collective-permute-start(bf16[272,384]{1,0:T(8,128)(2,1)S(1)} %get-tuple-element.168), channel_id=1, source_target_pairs={{0,2},{1,3},{2,0},{3,1},{4,6},{5,7},{6,4},{7,5},{8,10},{9,11},{10,... | collective-permute-start | bytes 626696 | tf_op jit(solution)/shard_map/ppermute | solution.py:35
  386.4 17.2 %collective-permute-start.64 = (bf16[272,384]{1,0:T(8,128)(2,1)S(1)}, bf16[272,384]{1,0:T(8,128)(2,1)}, u32[]{:S(2)}, u32[]{:S(2)}) collective-permute-start(bf16[272,384]{1,0:T(8,128)(2,1)S(1)} %get-tuple-element.167), channel_id=1, source_target_pairs={{0,1},{1,0},{2,3},{3,2},{4,5},{5,4},{6,7},{7,6},{8,9},{9,8},{10,11... | collective-permute-start | bytes 626696 | tf_op jit(solution)/shard_map/ppermute | solution.py:35
  426.5 35.5 %collective-permute-start.55 = (bf16[256,1024]{1,0:T(8,128)(2,1)}, bf16[256,1024]{1,0:T(8,128)(2,1)S(1)}, u32[]{:S(2)}, u32[]{:S(2)}) collective-permute-start(bf16[256,1024]{1,0:T(8,128)(2,1)} %get-tuple-element.156), channel_id=1, source_target_pairs={{0,24},{4,28},{8,16},{12,20},{16,8},{20,12},{24,0},{28,4},{1,25},{... | collective-permute-start | bytes 1572872 | tf_op jit(solution)/shard_map/ppermute | solution.py:35
  426.7 43.5 %collective-permute-start.54 = (bf16[256,1024]{1,0:T(8,128)(2,1)}, bf16[256,1024]{1,0:T(8,128)(2,1)S(1)}, u32[]{:S(2)}, u32[]{:S(2)}) collective-permute-start(bf16[256,1024]{1,0:T(8,128)(2,1)} %get-tuple-element.157), channel_id=1, source_target_pairs={{0,16},{4,20},{8,24},{12,28},{16,0},{20,4},{24,8},{28,12},{1,17},{... | collective-permute-start | bytes 1572872 | tf_op jit(solution)/shard_map/ppermute | solution.py:35
  428.8 41.4 %collective-permute-start.53 = (bf16[256,1024]{1,0:T(8,128)(2,1)S(1)}, bf16[256,1024]{1,0:T(8,128)(2,1)S(1)}, u32[]{:S(2)}, u32[]{:S(2)}) collective-permute-start(bf16[256,1024]{1,0:T(8,128)(2,1)S(1)} %get-tuple-element.155), channel_id=1, source_target_pairs={{0,8},{4,12},{8,0},{12,4},{16,24},{20,28},{24,16},{28,20},{1,9},{5... | collective-permute-start | bytes 1572872 | tf_op jit(solution)/shard_map/ppermute | solution.py:35
  432.0 26.5 %collective-permute-start.79 = (bf16[256,640]{1,0:T(8,128)(2,1)}, bf16[256,640]{1,0:T(8,128)(2,1)S(1)}, u32[]{:S(2)}, u32[]{:S(2)}) collective-permute-start(bf16[256,640]{1,0:T(8,128)(2,1)} %reduce-scatter.3.cloned.1.call-done.refs_0_), channel_id=1, source_target_pairs={{0,8},{4,12},{8,0},{12,4},{16,24},{20,28},{24,16},{28,20},{1,9},{5... | collective-permute-start | bytes 983048 | tf_op jit(solution)/shard_map/ppermute | solution.py:35
  432.9 27.9 %collective-permute-start.80 = (bf16[256,640]{1,0:T(8,128)(2,1)}, bf16[256,640]{1,0:T(8,128)(2,1)S(1)}, u32[]{:S(2)}, u32[]{:S(2)}) collective-permute-start(bf16[256,640]{1,0:T(8,128)(2,1)} %reduce-scatter.3.cloned.1.call-done.refs_0_), channel_id=1, source_target_pairs={{0,16},{4,20},{8,24},{12,28},{16,0},{20,4},{24,8},{28,12},{1,17},{... | collective-permute-start | bytes 983048 | tf_op jit(solution)/shard_map/ppermute | solution.py:35
  462.0 16.8 %collective-permute-start.63 = (bf16[256,1024]{1,0:T(8,128)(2,1)S(1)}, bf16[256,1024]{1,0:T(8,128)(2,1)S(1)}, u32[]{:S(2)}, u32[]{:S(2)}) collective-permute-start(bf16[256,1024]{1,0:T(8,128)(2,1)S(1)} %get-tuple-element.159), channel_id=1, source_target_pairs={{0,24},{4,28},{8,16},{12,20},{16,8},{20,12},{24,0},{28,4},{1,25},{... | collective-permute-start | bytes 1572872 | tf_op jit(solution)/shard_map/ppermute | solution.py:35
  464.9 23.3 %collective-permute-start.62 = (bf16[256,1024]{1,0:T(8,128)(2,1)S(1)}, bf16[256,1024]{1,0:T(8,128)(2,1)S(1)}, u32[]{:S(2)}, u32[]{:S(2)}) collective-permute-start(bf16[256,1024]{1,0:T(8,128)(2,1)S(1)} %get-tuple-element.160), channel_id=1, source_target_pairs={{0,16},{4,20},{8,24},{12,28},{16,0},{20,4},{24,8},{28,12},{1,17},{... | collective-permute-start | bytes 1572872 | tf_op jit(solution)/shard_map/ppermute | solution.py:35
  468.1 20.9 %collective-permute-start.61 = (bf16[256,1024]{1,0:T(8,128)(2,1)S(1)}, bf16[256,1024]{1,0:T(8,128)(2,1)S(1)}, u32[]{:S(2)}, u32[]{:S(2)}) collective-permute-start(bf16[256,1024]{1,0:T(8,128)(2,1)S(1)} %get-tuple-element.158), channel_id=1, source_target_pairs={{0,8},{4,12},{8,0},{12,4},{16,24},{20,28},{24,16},{28,20},{1,9},{5... | collective-permute-start | bytes 1572872 | tf_op jit(solution)/shard_map/ppermute | solution.py:35
  470.2 22.4 %collective-permute-start.83 = (bf16[256,640]{1,0:T(8,128)(2,1)S(1)}, bf16[256,640]{1,0:T(8,128)(2,1)S(1)}, u32[]{:S(2)}, u32[]{:S(2)}) collective-permute-start(bf16[256,640]{1,0:T(8,128)(2,1)S(1)} %copy-done.50), channel_id=1, source_target_pairs={{0,4},{4,0},{8,12},{12,8},{16,20},{20,16},{24,28},{28,24},{1,5},{5... | collective-permute-start | bytes 983048 | tf_op jit(solution)/shard_map/ppermute | solution.py:35
  470.3 22.3 %collective-permute-start.84 = (bf16[256,640]{1,0:T(8,128)(2,1)S(1)}, bf16[256,640]{1,0:T(8,128)(2,1)S(1)}, u32[]{:S(2)}, u32[]{:S(2)}) collective-permute-start(bf16[256,640]{1,0:T(8,128)(2,1)S(1)} %collective-permute-done.79.refs_1_), channel_id=1, source_target_pairs={{0,4},{4,0},{8,12},{12,8},{16,20},{20,16},{24,28},{28,24},{1,5},{5... | collective-permute-start | bytes 983048 | tf_op jit(solution)/shard_map/ppermute | solution.py:35
  478.8 13.8 %collective-permute-start.85 = (bf16[256,640]{1,0:T(8,128)(2,1)S(1)}, bf16[256,640]{1,0:T(8,128)(2,1)S(1)}, u32[]{:S(2)}, u32[]{:S(2)}) collective-permute-start(bf16[256,640]{1,0:T(8,128)(2,1)S(1)} %collective-permute-done.80.refs_2_), channel_id=1, source_target_pairs={{0,4},{4,0},{8,12},{12,8},{16,20},{20,16},{24,28},{28,24},{1,5},{5... | collective-permute-start | bytes 983048 | tf_op jit(solution)/shard_map/ppermute | solution.py:35
  (137 other events, 1061.8 us)
Sparse Core Ops, SparseCore 0:
  15.9 46.2 all-gather.6
  64.4 78.9 all-gather.8
  242.2 74.5 reduce-scatter.4
  357.5 29.9 reduce-scatter.2
  389.5 40.6 all-gather.10

commit v2 on v1

--- a/solution.py
+++ b/solution.py
@@ -9,6 +9,8 @@
 
 HEAD = 64
 LANES = 128
+VMEM_LIMIT = 62 << 20
+COST_SHARE = 64
 EPS = 1e-05
 BIG = 1e30
 LOG2E = 1.4426950408889634
@@ -41,6 +43,10 @@
 
 def after(value, *needed):
     return lax.optimization_barrier((value, needed))[0]
+
+
+def join(*values):
+    return lax.optimization_barrier(values)
 
 
 def plane_list(count):
@@ -131,6 +137,15 @@
     return total
 
 
+def gather_doubling(value):
+    got = value[None]
+    step = 1
+    while step < lax.axis_size("fsdp"):
+        got = jnp.concatenate([got, exchange(got, "fsdp", step)], axis=0)
+        step *= 2
+    return got
+
+
 def in_terms(vector, count):
     terms = []
     for _ in range(count):
@@ -143,12 +158,14 @@
     return pl.BlockSpec(shape, lambda *i: (0,) * len(shape))
 
 
-def params(limit=48):
-    return pltpu.CompilerParams(vmem_limit_bytes=limit << 20)
-
-
-def cost(flops, size):
-    return pl.CostEstimate(flops=flops, bytes_accessed=size, transcendentals=0)
+def params(limit=VMEM_LIMIT):
+    return pltpu.CompilerParams(vmem_limit_bytes=limit)
+
+
+def cost(flops, size, exps=0):
+    return pl.CostEstimate(
+        flops=flops // COST_SHARE, bytes_accessed=size // COST_SHARE, transcendentals=exps // COST_SHARE
+    )
 
 
 def mask_columns(seg, bits):
@@ -218,18 +235,25 @@
         out_specs=[part(0), part(0)],
         out_shape=[jax.ShapeDtypeStruct((count, LANES), BF), jax.ShapeDtypeStruct((count, LANES), F32)],
         scratch_shapes=[pltpu.VMEM((heads, count, LANES), BF), pltpu.VMEM((heads, count, LANES), BF)],
-        compiler_params=pltpu.CompilerParams(vmem_limit_bytes=48 << 20),
-        cost_estimate=pl.CostEstimate(
-            flops=products * 2, bytes_accessed=12 * count * LANES, transcendentals=count * count * heads
-        ),
+        compiler_params=params(48 << 20),
+        cost_estimate=cost(products * 2, 12 * count * LANES, count * count * heads),
         name="attend",
     )(qkv, qkv, qkv, mask_q, mask_k)
 
 
-def backward_kernel(*refs, heads, steps, block, pieces):
+def backward_kernel(*refs, heads, first, steps, total, block, pieces):
     q, k, v, mask_q, mask_k, out, lse = refs[:7]
     parts = refs[7 : 7 + pieces]
-    grads, key_side, value_side, dk_t, dv_t, dc_all = refs[7 + pieces :]
+    refs = refs[7 + pieces :]
+    if first:
+        grads_before, dk_before, dv_before = refs[:3]
+        refs = refs[3:]
+    grads = refs[0]
+    if steps < total:
+        dk_t, dv_t = refs[1:3]
+        key_side, value_side, dc_all = refs[3:]
+    else:
+        key_side, value_side, dc_all, dk_t, dv_t = refs[1:]
     lane = lane_index()
     step = pl.program_id(0)
 
@@ -239,8 +263,13 @@
         for h in range(heads):
             key_side[h] = merge(k[...], mask_k[...], h)
             value_side[h] = merge(v[...], ones, h)
-        dk_t[...] = jnp.zeros_like(dk_t)
-        dv_t[...] = jnp.zeros_like(dv_t)
+        if first:
+            dk_t[...] = dk_before[...]
+            dv_t[...] = dv_before[...]
+            grads[: first * block, :LANES] = grads_before[...]
+        else:
+            dk_t[...] = jnp.zeros_like(dk_t)
+            dv_t[...] = jnp.zeros_like(dv_t)
         if pieces == 1:
             dc_all[...] = parts[0][...]
         else:
@@ -248,7 +277,7 @@
                 dc_all[i * block : (i + 1) * block, :] = parts[i][:, :LANES]
                 dc_all[(pieces + i) * block : (pieces + i + 1) * block, :] = parts[i][:, LANES:]
 
-    dc = dc_all.at[pl.ds(pl.multiple_of(step * block, block), block), :]
+    dc = dc_all.at[pl.ds(pl.multiple_of((first + step) * block, block), block), :]
     product = dc[...].astype(F32) * out[...].astype(F32)
     low = jnp.sum(jnp.where(lane < HEAD, product, 0.0), axis=1, keepdims=True)
     high = jnp.sum(jnp.where(lane < HEAD, 0.0, product), axis=1, keepdims=True)
@@ -265,64 +294,84 @@
         own = slice(HEAD * h, HEAD * h + HEAD)
         dk_t[own, :] += dot_nn(q_t[own, :], ds)
         dv_t[own, :] += dot_nn(dc_t[own, :], probs.astype(BF))
-    grads[pl.ds(pl.multiple_of(step * block, block), block), :LANES] = (
-        dq.astype(BF).astype(F32) * HEAD**-0.5
-    ).astype(BF)
-
-    @pl.when(step == steps - 1)
-    def _():
-        grads[:, LANES : 2 * LANES] = (dk_t[...] * (1.0 / LOG2E)).T.astype(BF)
-        grads[:, 2 * LANES :] = dv_t[...].T.astype(BF)
-
-
-def attend_back(qkv, mask_q, mask_k, dc, out, lse, heads, block):
+    at = step * block if steps < total else (first + step) * block
+    grads[pl.ds(pl.multiple_of(at, block), block), :LANES] = (dq.astype(BF).astype(F32) * HEAD**-0.5).astype(BF)
+    if steps == total:
+
+        @pl.when(step == steps - first - 1)
+        def _():
+            grads[:, LANES : 2 * LANES] = (dk_t[...] * (1.0 / LOG2E)).T.astype(BF)
+            grads[:, 2 * LANES :] = dv_t[...].T.astype(BF)
+
+
+def attend_back(qkv, mask_q, mask_k, dc, out, lse, heads, block, part=None, before=None, place=0):
     dc = dc if isinstance(dc, list) else [dc]
     count = qkv.shape[0]
-    part = lambda j: pl.BlockSpec((block, LANES), lambda i: (i, j))
+    total = count // block
+    first = total // 2 if part == 1 else 0
+    steps = total // 2 if part == 0 else total
+    piece = lambda j: pl.BlockSpec((block, LANES), lambda i: (first + i, j))
     full = lambda j: pl.BlockSpec((count, LANES), lambda i: (0, j))
     products = 5 * 2 * count * count * LANES * heads
-    return pl.pallas_call(
-        functools.partial(backward_kernel, heads=heads, steps=count // block, block=block, pieces=len(dc)),
-        grid=(count // block,),
-        in_specs=[part(0), full(1), full(2), part(0), full(0), part(0), part(0)] + [whole(v.shape) for v in dc],
-        out_specs=pl.BlockSpec((count, 3 * LANES), lambda i: (0, 0)),
-        out_shape=jax.ShapeDtypeStruct((count, 3 * LANES), BF),
-        scratch_shapes=[
-            pltpu.VMEM((heads, count, LANES), BF),
-            pltpu.VMEM((heads, count, LANES), BF),
-            pltpu.VMEM((LANES, count), F32),
-            pltpu.VMEM((LANES, count), F32),
-            pltpu.VMEM((count, LANES), BF),
-        ],
-        compiler_params=pltpu.CompilerParams(vmem_limit_bytes=56 << 20),
-        cost_estimate=pl.CostEstimate(
-            flops=products, bytes_accessed=16 * count * LANES, transcendentals=count * count * heads
+    side = (LANES, count)
+    shapes = [jax.ShapeDtypeStruct((count, 3 * LANES), BF)]
+    scratch = [
+        pltpu.VMEM((heads, count, LANES), BF),
+        pltpu.VMEM((heads, count, LANES), BF),
+        pltpu.VMEM((count, LANES), BF),
+    ]
+    if part == 0:
+        shapes = [jax.ShapeDtypeStruct((count // 2, LANES), BF)] + [jax.ShapeDtypeStruct(side, F32)] * 2
+    else:
+        scratch += [pltpu.VMEM(side, F32)] * 2
+    before = before or []
+    got = pl.pallas_call(
+        functools.partial(
+            backward_kernel, heads=heads, first=first, steps=steps, total=total, block=block, pieces=len(dc)
         ),
+        grid=(steps - first,),
+        in_specs=[piece(0), full(1), full(2), piece(0), full(0), piece(0), piece(0)]
+        + [pl.BlockSpec((block if len(dc) > 1 else count, v.shape[1]), lambda i: (place, 0)) for v in dc]
+        + [whole(v.shape) for v in before],
+        out_specs=[whole(v.shape) for v in shapes],
+        out_shape=shapes,
+        scratch_shapes=scratch,
+        compiler_params=params(),
+        cost_estimate=cost(products, 16 * count * LANES, count * count * heads),
         name="attend_back",
-    )(qkv, qkv, qkv, mask_q, mask_k, out, lse, *dc)
-
-
-def project_kernel(*refs, blocks):
-    weight, bias, factor, out = refs[blocks:]
-    row = 0
-    for ref in refs[:blocks]:
-        got = (dot_nn(ref[...], weight[...]) + bias[...]) * factor[...]
-        out[row : row + ref.shape[0], :] = got.astype(BF)
-        row += ref.shape[0]
-
-
-def project(blocks, weight, bias, factor):
+    )(qkv, qkv, qkv, mask_q, mask_k, out, lse, *dc, *before)
+    return got if part == 0 else got[0]
+
+
+def project_kernel(*refs, blocks, rows, bits):
+    weight, bias, factor, out, mask_q, mask_k = refs[blocks:]
+    lane = lane_index() % HEAD
+    used = lane < 2 * bits
+    fixed = ((lane >= 60) & (lane < 63)).astype(F32).astype(BF)
+    for i, ref in enumerate(refs[:blocks]):
+        at = slice(i * rows, (i + 1) * rows)
+        got = (dot_nn(ref[:rows, :], weight[...]) + bias[...]) * factor[...]
+        out[at, :] = got.astype(BF)
+        parts = ref[rows : rows + 16, : 2 * rows].astype(F32)
+        number = (parts[:8, :rows] * 64 + parts[:8, rows:]).T[:, :1].astype(jnp.int32)
+        flip = ((number >> (lane // 2)) & 1) ^ (lane & 1)
+        mask_q[at, :] = jnp.where(used & (flip == 1), -BIG, 0.0).astype(BF)
+        mask_k[at, :] = jnp.where(used, (1 - flip).astype(F32).astype(BF), fixed)
+
+
+def project(blocks, rows, weight, bias, factor, bits):
     width, line = weight.shape
     args = (*blocks, weight, bias[None], factor[None])
-    shape = (sum(v.shape[0] for v in blocks), line)
+    count = rows * len(blocks)
+    shapes = [(count, line), (count, LANES), (count, LANES)]
     return pl.pallas_call(
-        functools.partial(project_kernel, blocks=len(blocks)),
+        functools.partial(project_kernel, blocks=len(blocks), rows=rows, bits=bits),
         in_specs=[whole(v.shape) for v in args],
-        out_specs=whole(shape),
-        out_shape=jax.ShapeDtypeStruct(shape, BF),
+        out_specs=[whole(v) for v in shapes],
+        out_shape=[jax.ShapeDtypeStruct(v, BF) for v in shapes],
         grid=(1,),
         compiler_params=params(),
-        cost_estimate=cost(2 * shape[0] * width * line, 2 * shape[0] * (width + line)),
+        cost_estimate=cost(2 * count * width * line, 2 * count * (width + line)),
         name="project",
     )(*args)
 
@@ -626,15 +675,17 @@
             pltpu.SemaphoreType.DMA((len(flat),)),
             pltpu.VMEM((rows, width), F32),
         ],
-        compiler_params=params(56),
+        compiler_params=params(),
         cost_estimate=cost(8 * rows * width * middle * block, 8 * width * middle * block + 16 * rows * width),
         name="feed_back",
     )(low, *weights, *slopes, du_second, normed, inverse, gain[None], *flat)
 
 
-def context_back_kernel(me, da, weight, mine, other, whole_grad, *, middle):
+def context_back_kernel(me, da, weight, *refs, middle):
+    outs, whole_grad = refs[:-1], refs[-1]
     whole_grad[...] = dot_nt(da[...], weight[...]).astype(BF)
     rows = da.shape[0]
+    mine, other = outs
     width = mine.shape[1]
     second = (me[0] & 1) == 1
     for i in range(middle):
@@ -645,17 +696,13 @@
         other[i * rows : (i + 1) * rows, :] = jnp.where(second, low, high)
 
 
-def context_back(s, me, da, weight, own_width, middle):
-    _, rows, width = da.shape
+def context_back(me, da, weight, own_width, middle):
+    rows, width = da.shape
     shape = (middle * rows, own_width)
     return pl.pallas_call(
         functools.partial(context_back_kernel, middle=middle),
         grid=(1,),
-        in_specs=[
-            pl.BlockSpec(memory_space=pltpu.SMEM),
-            pl.BlockSpec((None, rows, width), lambda i: (s, 0, 0)),
-            whole(weight.shape),
-        ],
+        in_specs=[pl.BlockSpec(memory_space=pltpu.SMEM), whole(da.shape), whole(weight.shape)],
         out_specs=[whole(shape)] * 2,
         out_shape=[jax.ShapeDtypeStruct(shape, BF)] * 2,
         scratch_shapes=[pltpu.VMEM((rows, width), BF)],
@@ -689,71 +736,161 @@
     )(act, other_act, grad, other_grad)
 
 
+EXTRA = 16
+
+
 def expand_gradient_kernel(
-    me, low, other_low, context, other_context, de, other_de, da, other_da, kept_a, sent_a, kept_b, sent_b, *, middle
+    me, low, other_low, context, other_context, de, other_de, da, other_da, small, *outs, middle, own, share
 ):
     block = de.shape[1] // middle
-    rows = kept_a.shape[1]
-    own = kept_a.shape[2] - block
+    depth = small.shape[0]
+    shard = low.shape[1] // depth
+    tall = shard + EXTRA
     first, second = low[...].T, other_low[...].T
     third, fourth = context[...].T, other_context[...].T
+    kept_a, sent_a, kept_b, sent_b = outs
     for i in range(middle):
         at = slice(i * block, (i + 1) * block)
+        target = me[0] ^ (2 * i)
         wide = (dot_nn(first, de[:, at]) + dot_nn(second, other_de[:, at])).astype(BF)
-        where = pl.ds(pl.multiple_of((me[0] ^ (2 * i)) * own, own), own)
+        where = pl.ds(pl.multiple_of(target * own, own), own)
         thin = (dot_nn(third, da[:, where]) + dot_nn(fourth, other_da[:, where])).astype(BF)
-        for target, n, part in (
-            (sent_a if i >= 2 else kept_a, i % 2, slice(0, rows)),
-            (sent_b if i % 2 else kept_b, i // 2, slice(rows, 2 * rows)),
+        for out, n, part in (
+            (sent_a if i >= 2 else kept_a, i % 2, range(depth // 2)),
+            (sent_b if i % 2 else kept_b, i // 2, range(depth // 2, depth)),
         ):
-            target[n, :, :block] = wide[part]
-            target[n, :, block:] = thin[part]
-
-
-def expand_gradient(me, low, other_low, context, other_context, de, other_de, da, other_da, own):
+            for z in part:
+                row = (z - part[0]) * tall
+                out[n, row : row + shard, :block] = wide[z * shard : (z + 1) * shard]
+                out[n, row : row + shard, block:] = thin[z * shard : (z + 1) * shard]
+                line = small[z : z + 1, pl.ds(pl.multiple_of(target * share, share), share)].astype(BF)
+                line = jnp.concatenate([line, jnp.zeros((1, block + own - share), BF)], axis=1)
+                out[n, row + shard : row + tall, :] = jnp.broadcast_to(line, (EXTRA, block + own))
+
+
+def expand_gradient(me, low, other_low, context, other_context, de, other_de, da, other_da, small, own):
     rows, width = low.shape
     middle = 4
+    depth = small.shape[0]
     block = de.shape[1] // middle
-    args = (low, other_low, context, other_context, de, other_de, da, other_da)
-    shape = (2, width // 2, block + own)
+    args = (low, other_low, context, other_context, de, other_de, da, other_da, small)
+    shape = (2, width // 2 + EXTRA * depth // 2, block + own)
+    share = small.shape[1] // (2 * middle)
     return pl.pallas_call(
-        functools.partial(expand_gradient_kernel, middle=middle),
+        functools.partial(expand_gradient_kernel, middle=middle, own=own, share=share),
         grid=(1,),
         in_specs=[pl.BlockSpec(memory_space=pltpu.SMEM)] + [whole(v.shape) for v in args],
         out_specs=[whole(shape)] * 4,
         out_shape=[jax.ShapeDtypeStruct(shape, BF)] * 4,
-        compiler_params=params(56),
+        compiler_params=params(),
         cost_estimate=cost(4 * rows * width * middle * (block + own), 4 * width * middle * block),
         name="expand_gradient",
     )(me, *args)
 
 
-def unpack_expand_kernel(me, *refs, depth):
-    wide, thin = refs[-2:]
-    count = len(refs) - 2
+def unpack_expand_kernel(blocks, wide, thin, small, *, depth):
+    count = blocks.shape[0]
+    shard = wide.shape[0]
     block = wide.shape[1] // count
     piece, own = block // depth, thin.shape[1] // count
-    for n, k in enumerate(plane_list(count)):
-        g = me[0] ^ k
+    for g in range(count):
         for z in range(depth):
-            at = pl.multiple_of(z * count * piece + g * piece, piece)
-            wide[:, pl.ds(at, piece)] = refs[n][:, z * piece : (z + 1) * piece].astype(F32)
-        thin[:, pl.ds(pl.multiple_of(g * own, own), own)] = refs[n][:, block:].astype(F32)
-
-
-def unpack_expand(me, blocks, depth, hidden, width):
-    shard = blocks[0].shape[0]
-    shapes = [(shard, hidden), (shard, width)]
+            at = (z * count + g) * piece
+            wide[:, at : at + piece] = blocks[g, :shard, z * piece : (z + 1) * piece].astype(F32)
+        thin[:, g * own : (g + 1) * own] = blocks[g, :shard, block:].astype(F32)
+        small[g : g + 1, :] = blocks[g, shard : shard + EXTRA, : small.shape[1]].astype(F32)[0:1]
+
+
+def unpack_expand(blocks, depth, hidden, width, share):
+    shard = blocks.shape[1] - EXTRA
+    shapes = [(shard, hidden), (shard, width), (blocks.shape[0], share)]
     return pl.pallas_call(
         functools.partial(unpack_expand_kernel, depth=depth),
         grid=(1,),
-        in_specs=[pl.BlockSpec(memory_space=pltpu.SMEM)] + [whole(v.shape) for v in blocks],
+        in_specs=[whole(blocks.shape)],
         out_specs=[whole(v) for v in shapes],
         out_shape=[jax.ShapeDtypeStruct(v, F32) for v in shapes],
         compiler_params=params(),
         cost_estimate=cost(0, 6 * shard * (hidden + width)),
         name="unpack_expand",
+    )(blocks)
+
+
+def unpack_reduce_kernel(me, *refs):
+    out = refs[-1]
+    rows = refs[0].shape[0]
+    for n, k in enumerate(plane_list(len(refs) - 1)):
+        out[pl.ds(pl.multiple_of((me[0] ^ k) * rows, rows), rows), :] = refs[n][...].astype(F32)
+
+
+def unpack_reduce(me, blocks):
+    rows, width = blocks[0].shape
+    shape = (rows * len(blocks), width)
+    return pl.pallas_call(
+        unpack_reduce_kernel,
+        grid=(1,),
+        in_specs=[pl.BlockSpec(memory_space=pltpu.SMEM)] + [whole(v.shape) for v in blocks],
+        out_specs=whole(shape),
+        out_shape=jax.ShapeDtypeStruct(shape, F32),
+        compiler_params=params(),
+        cost_estimate=cost(0, 6 * shape[0] * width),
+        name="unpack_reduce",
     )(me, *blocks)
+
+
+def input_part_kernel(grads, weight, *refs, with_away):
+    got = dot_nn(grads[...], weight[...])
+    if with_away:
+        got = got + refs[0][...].astype(F32)
+        outs = refs[1:]
+    else:
+        outs = refs
+    rows = outs[0].shape[0]
+    for i, out in enumerate(outs):
+        out[...] = got[i * rows : (i + 1) * rows].astype(BF)
+
+
+def input_part(grads, weight, half, away=None, pieces=1):
+    count, line = grads.shape
+    rows, width = count // 2, weight.shape[1]
+    more = () if away is None else (away,)
+    shape = (rows // pieces, width)
+    got = pl.pallas_call(
+        functools.partial(input_part_kernel, with_away=away is not None),
+        grid=(1,),
+        in_specs=[pl.BlockSpec((rows, line), lambda i: (half, 0)), whole(weight.shape)] + [whole(v.shape) for v in more],
+        out_specs=[whole(shape)] * pieces,
+        out_shape=[jax.ShapeDtypeStruct(shape, BF)] * pieces,
+        compiler_params=params(),
+        cost_estimate=cost(2 * rows * width * line, 4 * rows * width),
+        name="input_part",
+    )(grads, weight, *more)
+    return got if pieces > 1 else got[0]
+
+
+def input_kernel(before, *refs):
+    out = refs[-1]
+    rows = refs[0].shape[0]
+    half = len(refs) // 2
+    for s in range(2):
+        total = before[s * rows : (s + 1) * rows, :]
+        for ref in refs[s * half : (s + 1) * half]:
+            total = total + ref[...].astype(F32)
+        out[s] = total
+
+
+def input_sum(before, first, second):
+    rows, width = first[0].shape
+    return pl.pallas_call(
+        input_kernel,
+        grid=(1,),
+        in_specs=[whole(before.shape)] + [whole(v.shape) for v in (*first, *second)],
+        out_specs=whole((2, rows, width)),
+        out_shape=jax.ShapeDtypeStruct((2, rows, width), F32),
+        compiler_params=params(),
+        cost_estimate=cost(0, 32 * rows * width),
+        name="input_sum",
+    )(before, *first, *second)
 
 
 def unpack_heads_kernel(me, *refs):
@@ -786,21 +923,20 @@
 
 
 def heads_gradient_kernel(*refs, blocks, last):
+    grads = refs[blocks]
     if last:
-        grads, before = refs[blocks : blocks + 2]
-        out, sums, total = refs[blocks + 2 :]
-        total[...] = before[...]
+        before, out, sums, tokens = refs[blocks + 1 :]
     else:
-        grads = refs[blocks]
-        total, sums = refs[blocks + 1 :]
-        total[...] = jnp.zeros_like(total)
-    row = 0
-    for ref in refs[:blocks]:
-        total[...] += dot_tn(grads[row : row + ref.shape[0], :], ref[...])
-        row += ref.shape[0]
+        out, sums, tokens = refs[blocks + 1 :]
+    rows = grads.shape[0] // blocks
+    for i, ref in enumerate(refs[:blocks]):
+        tokens[i * rows : (i + 1) * rows, :] = ref[:rows, :]
+    total = dot_tn(grads[...], tokens[...])
     sums[...] = jnp.broadcast_to(jnp.sum(grads[...].astype(F32), axis=0, keepdims=True), sums.shape)
     if last:
-        out[...] = total[...].T.astype(BF)
+        out[...] = (total + before[...]).T.astype(BF)
+    else:
+        out[...] = total
 
 
 def heads_gradient(blocks, grads, before=None):
@@ -816,7 +952,7 @@
         in_specs=[whole(v.shape) for v in args],
         out_specs=[whole(v.shape) for v in shapes],
         out_shape=shapes,
-        scratch_shapes=[pltpu.VMEM((line, width), F32)] if last else [],
+        scratch_shapes=[pltpu.VMEM((grads.shape[0], width), BF)],
         compiler_params=params(),
         cost_estimate=cost(2 * grads.shape[0] * width * line, 2 * grads.shape[0] * width + 6 * width * line),
         name="heads_gradient",
@@ -1160,7 +1296,28 @@
     lines = -(-terms.shape[0] // (16 * line)) * 16
     terms = jnp.pad(terms, (0, lines * line - terms.shape[0])).reshape(lines, line)
     own_heads = jnp.concatenate([columns(query_weight), columns(key_weight), columns(value_weight)], axis=1)
-    own_heads = gather_shards(jnp.concatenate([own_heads, terms], axis=0))
+    shard_parts = gather_doubling(jnp.concatenate([own_heads, terms], axis=0))
+
+    def plane(value, *needed):
+        first, second = after((peer(value, 2), peer(value, 4)), *needed)
+        part = value.shape[0] // 2
+        return first, second, (peer(first[:part], 4), peer(second[part:], 2))
+
+    def chip(blocks):
+        return blocks + [jax.tree.map(lambda v: peer(v, 1), b) for b in blocks]
+
+    def direct(value):
+        return [value] + [peer(value, k) for k in evens[1:]]
+
+    low_in = []
+    for s in range(batch):
+        numbers = jnp.concatenate([segments[s] // 64, segments[s] % 64]).astype(BF)
+        numbers = jnp.pad(numbers[None], ((0, EXTRA - 1), (0, width - 2 * rows)))
+        low_in.append(jnp.concatenate([tokens[s].astype(BF), numbers], axis=0))
+
+    first_got, shard_parts, low_in = join(direct(low_in[0]), shard_parts, low_in)
+    first_blocks = chip(first_got)
+    own_heads = by_owner([shard_parts[j : j + 1] for j in range(depth)], 0, list(range(depth)), "fsdp")
     packed = own_heads[:, shard:].reshape(depth, lines * line)[:, : 3 * size]
     packed = jnp.sum(packed.reshape(depth, 3, -1).astype(F32), axis=1)
     own_heads = own_heads[:, :shard].reshape(width, line)
@@ -1184,152 +1341,184 @@
         lax.dynamic_slice_in_dim(expand_weight, (z * count + me) * piece, piece, 1).astype(BF) for z in range(depth)
     ]
     block_expand = jnp.concatenate([jnp.concatenate(block_expand, axis=1), strip], axis=0)
-    block_expand = lax.all_gather(block_expand, "fsdp", axis=0)
+    block_expand = lax.all_gather(after(block_expand, first_got[1]), "fsdp", axis=0)
 
     reduce_blocks = [lax.dynamic_slice_in_dim(reduce_weight, (me ^ k) * piece, piece, 0).astype(BF) for k in evens]
-    reduce_own = lax.all_gather(jnp.stack(reduce_blocks), "fsdp", axis=0)
-
-    def plane(value):
-        first, second = peer(value, 2), peer(value, 4)
-        part = value.shape[0] // 2
-        return first, second, (peer(first[:part], 4), peer(second[part:], 2))
-
-    def chip(blocks):
-        return blocks + [jax.tree.map(lambda v: peer(v, 1), b) for b in blocks]
-
-    low_in = [tokens[s].astype(BF) for s in range(batch)]
-    first = plane(low_in[0])
-    seg = after(segments, first[0])
-    for b in range(count.bit_length() - 1):
-        seg = jnp.concatenate([seg, peer(seg, 1 << b)], axis=1)
-    seg = seg.reshape(batch, count, rows)
-    seg = jnp.concatenate([seg[:, k] for k in order], axis=1)
-    masks = [mask_columns(seg[s], bits) for s in range(batch)]
-    second = plane(after(low_in[1], first[0], first[1]))
-    kept = []
-    for s, got in enumerate((first, second)):
-        blocks = chip([(low_in[s],), (got[0],), (got[1],), got[2]])
-        blocks = [v for b in blocks for v in b]
-        qkv = project(blocks, own_heads, head_bias, head_scale)
-        if s == 0:
-            qkv = after(qkv, second[0], second[1])
-        out, lse = attend(qkv, *masks[s], heads, rows)
-        kept.append((blocks, qkv, *masks[s], out, lse))
-    sent = [kept[s][4] for s in range(batch)]
-
-    expand_plane = plane(after(block_expand, sent[0]))
-    got_expand = chip([(block_expand,), (expand_plane[0],), (expand_plane[1],), expand_plane[2]])
+
+    halfway = count * rows // 2
+    heads_across = own_heads.T
+    first_qkv, *first_masks = project(first_blocks, rows, own_heads, head_bias, head_scale, bits)
+    first_out, first_lse, second_got = join(
+        *attend(first_qkv, *first_masks, heads, rows), direct(low_in[1])
+    )
+    second_blocks = chip(second_got)
+    (second_qkv, *second_masks), other_out = join(
+        project(second_blocks, rows, own_heads, head_bias, head_scale, bits), peer(first_out[halfway:], 1)
+    )
+
+    reduce_own = lax.all_gather(after(jnp.stack(reduce_blocks), second_got[1]), "fsdp", axis=0)
+    second_out, second_lse, first_pieces, near = join(
+        *attend(second_qkv, *second_masks, heads, rows),
+        even_pieces(first_out[:halfway], other_out),
+        (block_expand, peer(block_expand, 2), peer(block_expand, 4)),
+    )
+    part = depth // 2
+    far = peer(near[1][:part], 4), peer(near[2][part:], 2)
+    got_expand, second_pieces = join(
+        chip([*((v,) for v in near), far]), even_pieces(second_out[:halfway], peer(second_out[halfway:], 1))
+    )
     full_output = assemble_output(got_expand, shard, thin, me_array)
+    kept = [
+        (first_blocks, first_qkv, *first_masks, first_out, first_lse),
+        (second_blocks, second_qkv, *second_masks, second_out, second_lse),
+    ]
 
     earlier = None
-    for s in range(batch):
-        half = sent[s].shape[0] // 2
-        pieces = even_pieces(sent[s][:half], peer(sent[s][half:], 1))
+    for s, pieces in enumerate((first_pieces, second_pieces)):
         earlier = branch(s, me_array, pieces, full_output, tokens, bias_output, gain_first, shift_first, earlier)
     context_low, hidden_in, hidden_low, normed_first, inverse_first = (
         v.reshape(all_rows, v.shape[2]) for v in earlier
     )
 
-    act_even, act_odd, slope_even, slope_odd = expand_forward(hidden_low, bias_halves, got_expand, shard)
-    reduce_own = after(reduce_own, hidden_low)
+    act_even, act_odd, slope_even, slope_odd, other_low, other_context, reduce_own = join(
+        *expand_forward(hidden_low, bias_halves, got_expand, shard),
+        peer(hidden_low, 1),
+        peer(context_low, 1),
+        reduce_own,
+    )
     reduce_halves = [reduce_own, peer(reduce_own, 1)]
-    result, du_second, dr, sums_second = reduce_forward(
-        (act_even, act_odd),
+    result, du_second, dr, sums_second, other_act = join(
+        *reduce_forward(
+            (act_even, act_odd),
+            reduce_halves,
+            hidden_in,
+            cotangent.reshape(all_rows, width),
+            bias_reduce,
+            gain_second,
+            shift_second,
+        ),
+        peer(act_odd, 1),
+    )
+
+    sum_reduce = reduce_gradient(act_even, other_act, dr, peer(dr, 1), depth, piece)
+    sum_reduce, dr = join(sum_reduce, dr)
+    sum_reduce = lax.psum_scatter(sum_reduce, "fsdp", scatter_dimension=0, tiled=False)
+
+    de_even, de_odd, sums_even, sums_odd, grad_pre, da, sums_first = feed_back(
+        dr,
         reduce_halves,
-        hidden_in,
-        cotangent.reshape(all_rows, width),
-        bias_reduce,
-        gain_second,
-        shift_second,
-    )
-
-    de_even, de_odd, sums_even, sums_odd, grad_pre, da, sums_first = feed_back(
-        dr, reduce_halves, (slope_even, slope_odd), du_second, normed_first, inverse_first, gain_first, got_expand, shard
-    )
-    da_parts = da.reshape(batch, rows, width)
-    own_grads, other_grads = zip(
-        *(context_back(s, me_array, da_parts, full_output, own_width, middle) for s in range(batch))
-    )
-    dc = [even_pieces(own_grads[0], peer(other_grads[0], 1))]
-
-    other_low, other_context = peer(hidden_low, 1), peer(context_low, 1)
-    other_de, other_da = peer(de_odd, 1), peer(da, 1)
-    kept_a, sent_a, kept_b, sent_b = expand_gradient(
-        me_array, hidden_low, other_low, context_low, other_context, de_even, other_de, da, other_da, own_width
-    )
-    got_a, got_b = peer(sent_a, 4), peer(sent_b, 2)
-
-    other_act, other_dr = peer(act_odd, 1), peer(dr, 1)
-    sum_reduce = reduce_gradient(act_even, other_act, dr, other_dr, depth, piece)
-
-    dc[0][0] = after(dc[0][0], kept_a, sum_reduce)
-    dc.append(even_pieces(own_grads[1], peer(other_grads[1], 1)))
-    sum_reduce = lax.psum_scatter(sum_reduce, "fsdp", scatter_dimension=0, tiled=False)
-
-    add = lambda a, b: (a.astype(F32) + b.astype(F32)).astype(BF)
-    half = count * rows // 2
-    before, head_sums = None, 0.0
-    grad_in, grads = [], []
-    for s in range(batch):
-        blocks, qkv, mask_q, mask_k, out, lse = kept[s]
-        grads.append(attend_back(qkv, mask_q, mask_k, dc[s], out, lse, heads, rows))
-        if s == 0:
-            got_a, got_b = after((got_a, got_b), grads[0])
-            next_a, next_b = add(kept_a, got_a), add(kept_b, got_b)
-            got_a, got_b = peer(next_a[1], 2), peer(next_b[1], 4)
-        before, sums = heads_gradient(blocks, grads[s], before)
-        head_sums = head_sums + sums[0]
-        away = peer(dot_nt(grads[s][half:], own_heads).astype(BF), 1)
-        home = (dot_nt(grads[s][:half], own_heads) + away.astype(F32)).astype(BF)
-        if s == 0:
-            dc[1][0] = after(dc[1][0], home)
-        got = [home[:rows]] + [peer(home[i * rows : (i + 1) * rows], 2 * i) for i in range(1, middle)]
-        grad_in.append((s, got))
-    got_a, got_b = after((got_a, got_b), grads[1])
-    sum_expand = jnp.concatenate([add(next_a[0], got_a), add(next_b[0], got_b)], axis=0)
-    sum_expand = lax.psum_scatter(sum_expand, "fsdp", scatter_dimension=0, tiled=True)
-    sum_reduce = reduce_even([after(sum_reduce, grads[1])[i] for i in range(middle)], False)
-    grad_in = [
-        grad_pre[s * rows : (s + 1) * rows] + sum(v.astype(F32) for v in got) for s, got in grad_in
-    ]
-    grad_heads = before
-    grad_head_bias = jnp.pad(jnp.stack(in_terms(head_sums, 2)), ((0, 14), (0, 0)))
-    home_heads = jnp.concatenate(
-        [grad_heads.reshape(depth, shard, line), jnp.broadcast_to(grad_head_bias, (depth, 16, line))], axis=1
-    )
-    home_heads = reduce_shards(home_heads)
-    home_heads = jnp.concatenate(
-        [home_heads[:shard].astype(BF)]
-        + [v[None] for v in in_terms(home_heads[shard] + home_heads[shard + 1], 2)]
-        + [jnp.zeros((14, line), BF)],
-        axis=0,
-    )
-
-    def spread(value):
-        got = plane(value)
-        got = (value, got[0], got[1], jnp.concatenate(got[2], axis=0))
-        return [*got] + [peer(v, 1) for v in got]
-
-    grad_query_weight, grad_key_weight, grad_value_weight, wide_biases = unpack_heads(
-        me_array, spread(home_heads), shard, width
-    )
-    grad_expand_weight, grad_output_weight = unpack_expand(me_array, spread(sum_expand), depth, hidden, width)
-    grad_reduce_weight = lax.all_gather(sum_reduce, "ctx", axis=0, tiled=True).astype(F32)
-    own_shard = lambda v: lax.dynamic_slice_in_dim(v, my_shard * shard, shard, 0)
+        (slope_even, slope_odd),
+        du_second,
+        normed_first,
+        inverse_first,
+        gain_first,
+        got_expand,
+        shard,
+    )
 
     vectors = (sums_first[2], sums_first[0], sums_first[1], sums_second[2], sums_second[0], sums_second[1])
     wide_bias = by_owner(
         [sums[i, 0].reshape(depth, 1, piece) for sums in (sums_even, sums_odd) for i in range(middle)], 1
     ).reshape(depth, hidden // depth)
     small = jnp.concatenate([v.reshape(depth, shard) for v in vectors] + [wide_bias], axis=1)
-    for b in range(count.bit_length() - 1):
-        small = small + peer(small, 1 << b)
-    small = reduce_shards(small)
-    vec = [small[i * shard : (i + 1) * shard] for i in range(len(vectors))]
-    vec_expand = small[len(vectors) * shard :]
+    share = -(-small.shape[1] // (count * LANES)) * LANES
+    small = jnp.pad(small, ((0, 0), (0, share * count - small.shape[1])))
+    de_even, da, own_grads, other_grads, other_de, other_da, small, other_small = join(
+        de_even,
+        da,
+        *context_back(me_array, da, full_output, own_width, middle),
+        peer(de_odd, 1),
+        peer(da, 1),
+        small,
+        peer(small, 1),
+    )
+
+    sums, dc = join(
+        expand_gradient(
+            me_array,
+            hidden_low,
+            other_low,
+            context_low,
+            other_context,
+            de_even,
+            other_de,
+            da,
+            other_da,
+            small + other_small,
+            own_width,
+        ),
+        even_pieces(own_grads, peer(other_grads, 1)),
+    )
+    kept_a, sent_a, kept_b, sent_b = sums
+
+    add = lambda a, b: (a.astype(F32) + b.astype(F32)).astype(BF)
+    to_owner = lambda parts: [parts[0]] + [peer(parts[i], 2 * i) for i in range(1, middle)]
+
+    def back(s, dc, part=None, before=None):
+        _, qkv, mask_q, mask_k, out, lse = kept[s]
+        return attend_back(qkv, mask_q, mask_k, dc, out, lse, heads, rows, part, before, s)
+
+    first_grads, got_a, got_b = join(back(0, dc), peer(sent_a, 4), peer(sent_b, 2))
+    odd = input_part(first_grads, heads_across, 1)
+    first_grads, odd = join(first_grads, odd)
+    away, next_a, next_b, first_grads = join(peer(odd, 1), add(kept_a, got_a), add(kept_b, got_b), first_grads)
+    home = input_part(first_grads, heads_across, 0, away, middle)
+    home, first_grads, dc, sum_reduce = join(home, first_grads, dc, sum_reduce)
+    before, first_sums = heads_gradient(kept[0][0], first_grads, None)
+    before, dc = join(before, dc)
+    upper, got_a, got_b, got_reduce = join(
+        back(1, dc, 0),
+        peer(next_a[1], 2),
+        peer(next_b[1], 4),
+        to_owner(sum_reduce),
+    )
+    sum_expand = jnp.concatenate([add(next_a[0], got_a), add(next_b[0], got_b)], axis=0)
+    sum_reduce = sum(v.astype(F32) for v in got_reduce).astype(BF)
+    upper, sum_expand, sum_reduce = join(upper, sum_expand, sum_reduce)
+    sum_expand = lax.psum_scatter(sum_expand, "fsdp", scatter_dimension=0, tiled=True)
+    second_grads, from_first = join(back(1, dc, 1, upper), to_owner(home))
+
+    odd = input_part(second_grads, heads_across, 1)
+    second_grads, odd = join(second_grads, odd)
+    (grad_heads, sums), away, got_reduce, second_grads = join(
+        heads_gradient(kept[1][0], second_grads, before), peer(odd, 1), direct(sum_reduce), second_grads
+    )
+    head_sums = first_sums[0] + sums[0]
+    grad_head_bias = jnp.pad(jnp.stack(in_terms(head_sums, 2)), ((0, 14), (0, 0)))
+    home_heads = jnp.concatenate(
+        [grad_heads.reshape(depth, shard, line), jnp.broadcast_to(grad_head_bias, (depth, 16, line))], axis=1
+    )
+    shard_got = jnp.stack(
+        [lax.dynamic_index_in_dim(home_heads, my_shard ^ j, 0, keepdims=False) for j in range(depth)]
+    )
+    step = depth // 2
+    got = exchange(shard_got[step:], "fsdp", step)
+    home, sum_expand = join(input_part(second_grads, heads_across, 0, away, middle), sum_expand)
+    wide_expand = lax.all_gather(sum_expand, "ctx", axis=0)
+    got, from_second, grad_reduce_weight = join(got, to_owner(home), unpack_reduce(me_array, chip(got_reduce)))
+    shard_got = add(shard_got[:step], got)
+    while step > 1:
+        step //= 2
+        shard_got = add(shard_got[:step], exchange(shard_got[step:], "fsdp", step))
+    total = shard_got[0]
+    tail = total[shard].astype(F32) + total[shard + 1].astype(F32)
+    home_heads = jnp.concatenate(
+        [total[:shard]] + [v[None] for v in in_terms(tail, 2)] + [jnp.zeros((14, line), BF)], axis=0
+    )
+    heads_got = chip(direct(home_heads))
+    grad_in = input_sum(grad_pre, from_first, from_second)
+    grad_expand_weight, grad_output_weight, small_sum = unpack_expand(wide_expand, depth, hidden, width, share)
+    small_sum = small_sum.reshape(-1)
+    grad_query_weight, grad_key_weight, grad_value_weight, wide_biases = unpack_heads(
+        me_array, heads_got, shard, width
+    )
+    own_shard = lambda v: lax.dynamic_slice_in_dim(v, my_shard * shard, shard, 0)
+
+    vec = [small_sum[i * shard : (i + 1) * shard] for i in range(len(vectors))]
+    vec_expand = small_sum[len(vectors) * shard : len(vectors) * shard + hidden // depth]
     return (
         result.reshape(batch, rows, width),
-        jnp.stack(grad_in),
+        grad_in,
         grad_query_weight,
         own_shard(wide_biases[0]),
         grad_key_weight,

time: 511 us -> 477 us (0.933)
  waiting for transfers between devices: 155 us -> 103 us
  Pallas kernels: 180 us -> 228 us
  starting transfers between devices: 72.8 us -> 55.8 us
  matrix products: 10.9 us -> 0 us
    ppermute x95 -> x76, waiting for transfers between devices: 155 us -> 103 us  [exchange(): return lax.ppermute(value, axis, [(i, i ^ k) for i in range(count)])]
    pallas_call x5 -> x12, Pallas kernels: 71.9 us -> 106 us  [the longest x3 54.2 us: attend_back(): pl.pallas_call(functools.partial(backward_kernel, heads=heads, first=firs...]
    ppermute x95 -> x76, starting transfers between devices: 72.4 us -> 55.4 us  [exchange(): return lax.ppermute(value, axis, [(i, i ^ k) for i in range(count)])]
    unnamed x255 -> x182, local copies, waits for them, and re-layouts: 33.2 us -> 21.1 us
    dot_general x4 -> x0, matrix products: 10.9 us -> none  [dot_nt(): lax.dot_general(left, right, (((1,), (1,)), ((), ())), preferred_element_...]
    convert_element_type x6 -> x1, other arithmetic: 9.47 us -> 1.2 us  [body(): sum_reduce = sum((v.astype(F32) for v in got_reduce)).astype(BF)]
  transfers between devices with their start and end apart: 100 -> 81, of which waited for: 26 -> 28; matrix products, arithmetic and copies ran while one was open for 9% -> 9% of each run, Pallas kernels for 36% -> 46%
where the time goes in v2:
time: 477 us; the launch traced here: 469 us
  Pallas kernels  228 us (48%)
  waiting for transfers between devices  103 us (22%)
  starting transfers between devices  55.8 us (12%)
  local copies, waits for them, and re-layouts  44.8 us (9%)
  other arithmetic  21.5 us (5%)
  between operations  15.3 us (3%)
    ppermute x76, waiting for transfers between devices, exchange(): return lax.ppermute(value, axis, [(i, i ^ k) for i in range(count)])  103 us
    ppermute x76, starting transfers between devices, exchange(): return lax.ppermute(value, axis, [(i, i ^ k) for i in range(count)])  55.4 us
    pallas_call x3, Pallas kernels, attend_back(): pl.pallas_call(functools.partial(backward_kernel, heads=heads, first=firs...  54.2 us
    pallas_call x2, Pallas kernels, attend(): pl.pallas_call(functools.partial(forward_kernel, heads=heads), grid=(coun...  29.1 us
    unnamed x182, local copies, waits for them, and re-layouts  21.1 us
    pallas_call x1, Pallas kernels, feed_back(): pl.pallas_call(functools.partial(feed_back_kernel, middle=middle, depth=d...  20.6 us
    pallas_call x4, Pallas kernels, input_part(): pl.pallas_call(functools.partial(input_part_kernel, with_away=away is not...  17.1 us
    pallas_call x1, Pallas kernels, reduce_forward(): pl.pallas_call(functools.partial(reduce_kernel, steps=middle), grid=(midd...  15.1 us
  transfers between devices with their start and end apart: 81, of which 28 were waited for; matrix products, arithmetic and copies ran while one was open for 9% of the time, Pallas kernels for 46%

profile of v2, /device:TPU:0, one launch (start us, length us, event | category | flops | bytes accessed | tf_op | source)
XLA Modules:
  0.0 469.2 jit_solution(3297960684783017624)
XLA Ops:
  8.1 1.7 convert.19
  10.1 4.0 collective-permute-start.2
  16.0 2.0 collective-permute-start.3
  20.1 2.5 collective-permute-done.3
  22.7 2.8 collective-permute-start.4
  27.2 16.6 %collective-permute-done.4 = bf16[2,288,384]{2,1,0:T(8,128)(2,1)} collective-permute-done((bf16[2,288,384]{2,1,0:T(8,128)(2,1)S(1)}, bf16[2,288,384]{2,1,0:T(8,128)(2,1)}, u32[]{:S(2)}, u32[]{:S(2)}) %collective-permute-start.4) | collective-permute-done | bytes 442400 | tf_op jit(solution)/shard_map/ppermute | solution.py:37
  45.1 1.9 fusion.2
  48.1 2.3 collective-permute-start.11
  56.4 6.4 %project.2 = (bf16[2048,384]{1,0:T(8,128)(2,1)}, bf16[2048,128]{1,0:T(8,128)(2,1)}, bf16[2048,128]{1,0:T(8,128)(2,1)}) custom-call(bf16[272,1024]{1,0:T(8,128)(2,1)} %copy-done.22, bf16[272,1024]{1,0:T(8,128)(2,1)} %collective-permute-done.refs_1_, bf16[272,1024]{1,0:T(8,128)(2,1)} %copy-done.27, bf16[272,1024]{1,0:T(8,128)(2,1)} %copy-done.26, ...), custom_call_target="tpu_custom_call" | custom-call | flops 25165824 | bytes 90112 | tf_op jit(solution)/shard_map/project/pallas_call | solution.py:367
  62.8 1.4 copy-done.3
  66.3 14.5 %attend.2 = (bf16[2048,128]{1,0:T(8,128)(2,1)S(1)}, f32[2048,128]{1,0:T(8,128)S(1)}) custom-call(bf16[2048,384]{1,0:T(8,128)(2,1)S(1)} %copy-done.3, bf16[2048,384]{1,0:T(8,128)(2,1)S(1)} %copy-done.3, bf16[2048,384]{1,0:T(8,128)(2,1)S(1)} %copy-done.3, bf16[2048,128]{1,0:T(8,128)(2,1)S(1)} %copy-done.9, bf16[2048,128]{1,0:T(8,128)(2,1)S(1)} %copy-done.10), custom_call_target="tpu_custom_call" | custom-call | flops 134217728 | bytes 49152 | tf_op jit(solution)/shard_map/attend/pallas_call | solution.py:231
  82.3 1.5 collective-permute-start.21
  87.6 1.5 collective-permute-done.15.refs_7_
  89.1 6.8 %project.3 = (bf16[2048,384]{1,0:T(8,128)(2,1)}, bf16[2048,128]{1,0:T(8,128)(2,1)}, bf16[2048,128]{1,0:T(8,128)(2,1)}) custom-call(bf16[272,1024]{1,0:T(8,128)(2,1)} %pad_maximum_fusion.6.refs_0_, bf16[272,1024]{1,0:T(8,128)(2,1)} %copy-done.31, bf16[272,1024]{1,0:T(8,128)(2,1)} %collective-permute-done.10.refs_2_, ...), custom_call_target="tpu_custom_call" | custom-call | flops 25165824 | bytes 90112 | tf_op jit(solution)/shard_map/project/pallas_call | solution.py:367
  96.7 1.7 collective-permute-start.17
  98.4 1.7 collective-permute-start.18
  103.6 14.5 %attend.3 = (bf16[2048,128]{1,0:T(8,128)(2,1)S(1)}, f32[2048,128]{1,0:T(8,128)S(1)}) custom-call(bf16[2048,384]{1,0:T(8,128)(2,1)S(1)} %copy-done.2, bf16[2048,384]{1,0:T(8,128)(2,1)S(1)} %copy-done.2, bf16[2048,384]{1,0:T(8,128)(2,1)S(1)} %copy-done.2, bf16[2048,128]{1,0:T(8,128)(2,1)S(1)} %copy-done.5, bf16[2048,128]{1,0:T(8,128)(2,1)S(1)} %copy-done.6), custom_call_target="tpu_custom_call" | custom-call | flops 134217728 | bytes 49152 | tf_op jit(solution)/shard_map/attend/pallas_call | solution.py:231
  118.5 2.0 collective-permute-done.17.refs_1_
  120.7 1.5 collective-permute-done.29
  124.9 1.5 collective-permute-start.31
  132.3 13.7 %collective-permute-done.23.refs_4_.refs_7_.refs_13_ = bf16[2,320,512]{2,1,0:T(8,128)(2,1)S(1)} collective-permute-done((bf16[2,320,512]{2,1,0:T(8,128)(2,1)S(1)}, bf16[2,320,512]{2,1,0:T(8,128)(2,1)S(1)}, u32[]{:S(2)}, u32[]{:S(2)}) %collective-permute-start.23) | collective-permute-done | bytes 655392 | tf_op jit(solution)/shard_map/ppermute | solution.py:37
  150.5 3.0 assemble_output.1.refs_4_.weight
  153.5 4.8 %branch.2 = (bf16[2,256,1024]{2,1,0:T(8,128)(2,1)}, f32[2,256,1024]{2,1,0:T(8,128)}, bf16[2,256,1024]{2,1,0:T(8,128)(2,1)}, f32[2,256,1024]{2,1,0:T(8,128)}, f32[2,256,128]{2,1,0:T(8,128)}) custom-call(s32[1]{0:T(128)} %bitcast.me, bf16[256,256]{1,0:T(8,128)(2,1)} %get-tuple-element.259.refs_0_, bf16[256,256]{1,0:T(8,128)(2,1)} %copy-done.62, ...), custom_call_target="tpu_custom_call" | custom-call | flops 8388608 | bytes 106496 | tf_op jit(solution)/shard_map/branch/pallas_call | solution.py:451
  158.2 4.7 branch.3
  164.7 12.4 %expand.1 = (bf16[512,2048]{1,0:T(8,128)(2,1)}, bf16[512,2048]{1,0:T(8,128)(2,1)}, bf16[512,2048]{1,0:T(8,128)(2,1)}, bf16[512,2048]{1,0:T(8,128)(2,1)}) custom-call(bf16[512,1024]{1,0:T(8,128)(2,1)} %bitcast.154, f32[4,1,512]{2,1,0:T(1,128)} %pad_maximum_fusion.12.refs_1_, f32[4,1,512]{2,1,0:T(1,128)} %pad_maximum_fusion.13.refs_2_, ...), custom_call_target="tpu_custom_call" | custom-call | flops 67108864 | bytes 262144 | tf_op jit(solution)/shard_map/expand/pallas_call | solution.py:519
  179.5 5.2 %collective-permute-done.35.w_odd.refs_2_ = bf16[4,4,128,1024]{3,2,1,0:T(8,128)(2,1)} collective-permute-done((bf16[4,4,128,1024]{3,2,1,0:T(8,128)(2,1)}, bf16[4,4,128,1024]{3,2,1,0:T(8,128)(2,1)}, u32[]{:S(2)}, u32[]{:S(2)}) %collective-permute-start.35) | collective-permute-done | bytes 4194336 | tf_op jit(solution)/shard_map/ppermute | solution.py:37
  184.8 15.1 %reduce.25 = (f32[512,1024]{1,0:T(8,128)}, f32[512,1024]{1,0:T(8,128)}, bf16[512,1024]{1,0:T(8,128)(2,1)}, f32[8,1024]{1,0:T(8,128)}) custom-call(bf16[512,2048]{1,0:T(8,128)(2,1)} %get-tuple-element.275.act_even.act, bf16[512,2048]{1,0:T(8,128)(2,1)} %get-tuple-element.276.act_odd, bf16[4,4,128,1024]{3,2,1,0:T(8,128)(2,1)} %bitcast.142, ...), custom_call_target="tpu_custom_call" | custom-call | flops 67108864 | bytes 262144 | tf_op jit(solution)/shard_map/reduce/pallas_call | solution.py:587
  200.3 2.5 collective-permute-done.37.other_grad
  203.8 8.4 %reduce_gradient.1 = bf16[4,4,128,1024]{3,2,1,0:T(8,128)(2,1)} custom-call(bf16[512,2048]{1,0:T(8,128)(2,1)} %get-tuple-element.275.act_even.act, bf16[512,2048]{1,0:T(8,128)(2,1)} %collective-permute-done.36.other_act, bf16[512,1024]{1,0:T(8,128)(2,1)} %get-tuple-element.286.grad.refs_0_, bf16[512,1024]{1,0:T(8,128)(2,1)} %copy-done.34), custom_call_target="tpu_custom_call" | custom-call | flops 67108864 | bytes 131072 | tf_op jit(solution)/shard_map/reduce_gradient/pallas_call | solution.py:727
  213.2 20.6 %feed_back.1 = (bf16[512,2048]{1,0:T(8,128)(2,1)}, bf16[512,2048]{1,0:T(8,128)(2,1)}, f32[4,1,512]{2,1,0:T(1,128)}, f32[4,1,512]{2,1,0:T(1,128)}, f32[512,1024]{...) custom-call(bf16[512,1024]{1,0:T(8,128)(2,1)} %get-tuple-element.286.grad.refs_0_, ...), custom_call_target="tpu_custom_call" | custom-call | flops 134217728 | bytes 393216 | tf_op jit(solution)/shard_map/feed_back/pallas_call | solution.py:658
  237.5 4.5 context_back.1
  248.1 1.7 collective-permute-start.42
  250.4 12.8 %expand_gradient.1 = (bf16[2,544,640]{2,1,0:T(8,128)(2,1)}, bf16[2,544,640]{2,1,0:T(8,128)(2,1)}, bf16[2,544,640]{2,1,0:T(8,128)(2,1)}, bf16[2,544,640]{2,1,0:T(8,128)(2,1)}) custom-call(s32[1]{0:T(128)} %bitcast.me, bf16[512,1024]{1,0:T(8,128)(2,1)} %bitcast.155, bf16[512,1024]{1,0:T(8,128)(2,1)} %collective-permute-done.33.other_low, ...), custom_call_target="tpu_custom_call" | custom-call | flops 83886080 | bytes 131072 | tf_op jit(solution)/shard_map/expand_gradient/pallas_call | solution.py:779
  265.5 24.9 %attend_back.3.grads.refs_8_ = bf16[2048,384]{1,0:T(8,128)(2,1)} custom-call(bf16[2048,384]{1,0:T(8,128)(2,1)} %get-tuple-element.220.q.k.v.refs_0_.refs_1_.refs_2_, bf16[2048,384]{1,0:T(8,128)(2,1)} %get-tuple-element.220.q.k.v.refs_0_.refs_1_.refs_2_, bf16[2048,384]{1,0:T(8,128)(2,1)} %get-tuple-element.220.q.k.v.refs_0_.refs_1_.refs_2_, ...), custom_call_target="tpu_custom_call" | custom-call | flops 167772160 | bytes 65536 | tf_op jit(solution)/shard_map/attend_back/pallas_call | solution.py:328
  290.4 4.9 %collective-permute-done.45 = bf16[2,544,640]{2,1,0:T(8,128)(2,1)} collective-permute-done((bf16[2,544,640]{2,1,0:T(8,128)(2,1)}, bf16[2,544,640]{2,1,0:T(8,128)(2,1)}, u32[]{:S(2)}, u32[]{:S(2)}) %collective-permute-start.45) | collective-permute-done | bytes 1392672 | tf_op jit(solution)/shard_map/ppermute | solution.py:37
  295.4 3.9 input_part.4
  299.3 2.2 add_convert_fusion.1
  301.5 2.2 add_convert_fusion
  306.0 1.7 collective-permute-start.49
  308.2 4.5 input_part.5
  312.8 2.1 slice_bitcast_fusion.4
  316.1 1.7 collective-permute-start.51
  318.3 5.8 %heads_gradient.2 = (f32[384,1024]{1,0:T(8,128)}, f32[8,384]{1,0:T(8,128)}) custom-call(bf16[272,1024]{1,0:T(8,128)(2,1)} %copy-done.22, bf16[272,1024]{1,0:T(8,128)(2,1)} %collective-permute-done.refs_1_, bf16[272,1024]{1,0:T(8,128)(2,1)} %copy-done.27, bf16[272,1024]{1,0:T(8,128)(2,1)} %copy-done.26, bf16[272,1024]{1,0:T(8,128)(2,1)} %copy-done.28, ...), custom_call_target="tpu_custom_call" | custom-call | flops 25165824 | bytes 102400 | tf_op jit(solution)/shard_map/heads_gradient/pallas_call | solution.py:949
  324.1 14.0 %attend_back.4 = (bf16[1024,128]{1,0:T(8,128)(2,1)}, f32[128,2048]{1,0:T(8,128)}, f32[128,2048]{1,0:T(8,128)}) custom-call(bf16[2048,384]{1,0:T(8,128)(2,1)} %get-tuple-element.234.q.k.v.refs_0_.refs_1_.refs_2_, bf16[2048,384]{1,0:T(8,128)(2,1)} %get-tuple-element.234.q.k.v.refs_0_.refs_1_.refs_2_, ...), custom_call_target="tpu_custom_call" | custom-call | flops 167772160 | bytes 65536 | tf_op jit(solution)/shard_map/attend_back/pallas_call | solution.py:328
  343.0 1.6 collective-permute-start.53
  345.0 1.6 collective-permute-start.55
  346.6 15.3 %attend_back.5.grads.refs_8_ = bf16[2048,384]{1,0:T(8,128)(2,1)} custom-call(bf16[2048,384]{1,0:T(8,128)(2,1)} %get-tuple-element.234.q.k.v.refs_0_.refs_1_.refs_2_, bf16[2048,384]{1,0:T(8,128)(2,1)} %get-tuple-element.234.q.k.v.refs_0_.refs_1_.refs_2_, bf16[2048,384]{1,0:T(8,128)(2,1)} %get-tuple-element.234.q.k.v.refs_0_.refs_1_.refs_2_, ...), custom_call_target="tpu_custom_call" | custom-call | flops 167772160 | bytes 65536 | tf_op jit(solution)/shard_map/attend_back/pallas_call | solution.py:328
  362.0 6.7 %collective-permute-done.54.refs_2_ = bf16[256,1024]{1,0:T(8,128)(2,1)S(1)} collective-permute-done((bf16[256,1024]{1,0:T(8,128)(2,1)}, bf16[256,1024]{1,0:T(8,128)(2,1)S(1)}, u32[]{:S(2)}, u32[]{:S(2)}) %collective-permute-start.54) | collective-permute-done | bytes 524320 | tf_op jit(solution)/shard_map/ppermute | solution.py:37
  368.6 4.1 input_part.6
  374.8 1.5 collective-permute-start.57
  376.3 6.0 %heads_gradient.3 = (bf16[1024,384]{1,0:T(8,128)(2,1)}, f32[8,384]{1,0:T(8,128)}) custom-call(bf16[272,1024]{1,0:T(8,128)(2,1)} %pad_maximum_fusion.6.refs_0_, bf16[272,1024]{1,0:T(8,128)(2,1)} %copy-done.31, bf16[272,1024]{1,0:T(8,128)(2,1)} %collective-permute-done.10.refs_2_, bf16[272,1024]{1,0:T(8,128)(2,1)} %collective-permute-done.11.refs_3_, ...), custom_call_target="tpu_custom_call" | custom-call | flops 25165824 | bytes 102400 | tf_op jit(solution)/shard_map/heads_gradient/pallas_call | solution.py:949
  382.9 5.1 %collective-permute-done.58.refs_2_ = bf16[128,1024]{1,0:T(8,128)(2,1)} collective-permute-done((bf16[128,1024]{1,0:T(8,128)(2,1)S(1)}, bf16[128,1024]{1,0:T(8,128)(2,1)}, u32[]{:S(2)}, u32[]{:S(2)}) %collective-permute-start.58) | collective-permute-done | bytes 262176 | tf_op jit(solution)/shard_map/ppermute | solution.py:37
  388.0 4.5 input_part.7
  395.9 1.7 collective-permute-start.63
  400.3 3.9 unpack_reduce.1
  404.1 15.6 %collective-permute-done.60 = bf16[2,272,384]{2,1,0:T(8,128)(2,1)S(1)} collective-permute-done((bf16[2,272,384]{2,1,0:T(8,128)(2,1)}, bf16[2,272,384]{2,1,0:T(8,128)(2,1)S(1)}, u32[]{:S(2)}, u32[]{:S(2)}) %collective-permute-start.60) | collective-permute-done | bytes 417824 | tf_op jit(solution)/shard_map/ppermute | solution.py:37
  419.7 4.4 collective-permute-done.62.refs_6_
  425.8 6.0 %collective-permute-done.68 = bf16[1,272,384]{2,1,0:T(8,128)(2,1)S(1)} collective-permute-done((bf16[1,272,384]{2,1,0:T(8,128)(2,1)S(1)}, bf16[1,272,384]{2,1,0:T(8,128)(2,1)S(1)}, u32[]{:S(2)}, u32[]{:S(2)}) %collective-permute-start.68) | collective-permute-done | bytes 208928 | tf_op jit(solution)/shard_map/ppermute | solution.py:37
  432.1 1.5 collective-permute-start.71
  435.7 5.5 %collective-permute-done.71.refs_3_ = bf16[272,384]{1,0:T(8,128)(2,1)S(1)} collective-permute-done((bf16[272,384]{1,0:T(8,128)(2,1)S(1)}, bf16[272,384]{1,0:T(8,128)(2,1)S(1)}, u32[]{:S(2)}, u32[]{:S(2)}) %collective-permute-start.71) | collective-permute-done | bytes 208928 | tf_op jit(solution)/shard_map/ppermute | solution.py:37
  441.2 2.6 collective-permute-done.70.refs_2_
  444.3 4.7 input_sum.1
  450.4 3.6 unpack_heads.1
  456.0 4.5 unpack_expand.1
  (407 shorter events, 87.2 us)
Async XLA Ops:
  7.2 75.1 %all-gather.7.cloned.1.call-start = ((), (), s32[]{:S(2)}) async-start(), calls=%async_computation.4 | async-start | bytes 1638400 | tf_op jit(solution)/shard_map/all_gather | solution.py:1344
  10.1 34.8 %collective-permute-start.2 = (bf16[272,1024]{1,0:T(8,128)(2,1)S(1)}, bf16[272,1024]{1,0:T(8,128)(2,1)S(1)}, u32[]{:S(2)}, u32[]{:S(2)}) collective-permute-start(bf16[272,1024]{1,0:T(8,128)(2,1)S(1)} %pad_maximum_fusion.5.refs_0_), channel_id=1, source_target_pairs={{0,24},{4,28},{8,16},{12,20},{16,8},{20,12},{24,0},{28,4},{1,25},{... | collective-permute-start | bytes 1671176 | tf_op jit(solution)/shard_map/ppermute | solution.py:37
  14.0 30.9 %collective-permute-start.1 = (bf16[272,1024]{1,0:T(8,128)(2,1)S(1)}, bf16[272,1024]{1,0:T(8,128)(2,1)S(1)}, u32[]{:S(2)}, u32[]{:S(2)}) collective-permute-start(bf16[272,1024]{1,0:T(8,128)(2,1)S(1)} %pad_maximum_fusion.5.refs_0_), channel_id=1, source_target_pairs={{0,16},{4,20},{8,24},{12,28},{16,0},{20,4},{24,8},{28,12},{1,17},{... | collective-permute-start | bytes 1671176 | tf_op jit(solution)/shard_map/ppermute | solution.py:37
  14.5 30.4 %collective-permute-start = (bf16[272,1024]{1,0:T(8,128)(2,1)S(1)}, bf16[272,1024]{1,0:T(8,128)(2,1)}, u32[]{:S(2)}, u32[]{:S(2)}) collective-permute-start(bf16[272,1024]{1,0:T(8,128)(2,1)S(1)} %pad_maximum_fusion.5.refs_0_), channel_id=1, source_target_pairs={{0,8},{4,12},{8,0},{12,4},{16,24},{20,28},{24,16},{28,20},{1,9},{5... | collective-permute-start | bytes 1671176 | tf_op jit(solution)/shard_map/ppermute | solution.py:37
  16.0 6.7 %collective-permute-start.3 = (bf16[1,288,384]{2,1,0:T(8,128)(2,1)S(1)}, bf16[1,288,384]{2,1,0:T(8,128)(2,1)S(1)}, u32[]{:S(2)}, u32[]{:S(2)}) collective-permute-start(bf16[1,288,384]{2,1,0:T(8,128)(2,1)S(1)} %maximum_bitcast_fusion), channel_id=1, source_target_pairs={{0,1},{1,0},{2,3},{3,2},{4,5},{5,4},{6,7},{7,6},{8,9},{9,8},{10,11... | collective-permute-start | bytes 663560 | tf_op jit(solution)/shard_map/ppermute | solution.py:37
  22.7 21.0 %collective-permute-start.4 = (bf16[2,288,384]{2,1,0:T(8,128)(2,1)S(1)}, bf16[2,288,384]{2,1,0:T(8,128)(2,1)}, u32[]{:S(2)}, u32[]{:S(2)}) collective-permute-start(bf16[2,288,384]{2,1,0:T(8,128)(2,1)S(1)} %pad_maximum_fusion.7), channel_id=1, source_target_pairs={{0,2},{1,3},{2,0},{3,1},{4,6},{5,7},{6,4},{7,5},{8,10},{9,11},{10,... | collective-permute-start | bytes 1327112 | tf_op jit(solution)/shard_map/ppermute | solution.py:37
  45.0 132.2 %all-gather.9.cloned.1.call-start = ((), (), s32[]{:S(2)}) async-start(), calls=%async_computation.5 | async-start | bytes 5242880 | tf_op jit(solution)/shard_map/all_gather | solution.py:1359
  48.1 7.5 %collective-permute-start.6 = (bf16[272,1024]{1,0:T(8,128)(2,1)}, bf16[272,1024]{1,0:T(8,128)(2,1)}, u32[]{:S(2)}, u32[]{:S(2)}) collective-permute-start(bf16[272,1024]{1,0:T(8,128)(2,1)} %collective-permute-done.refs_1_), channel_id=1, source_target_pairs={{0,4},{4,0},{8,12},{12,8},{16,20},{20,16},{24,28},{28,24},{1,5},{5... | collective-permute-start | bytes 1671176 | tf_op jit(solution)/shard_map/ppermute | solution.py:37
  48.1 33.8 %collective-permute-start.11 = (bf16[272,1024]{1,0:T(8,128)(2,1)}, bf16[272,1024]{1,0:T(8,128)(2,1)}, u32[]{:S(2)}, u32[]{:S(2)}) collective-permute-start(bf16[272,1024]{1,0:T(8,128)(2,1)} %pad_maximum_fusion.6.refs_0_), channel_id=1, source_target_pairs={{0,24},{4,28},{8,16},{12,20},{16,8},{20,12},{24,0},{28,4},{1,25},{... | collective-permute-start | bytes 1671176 | tf_op jit(solution)/shard_map/ppermute | solution.py:37
  50.4 31.5 %collective-permute-start.10 = (bf16[272,1024]{1,0:T(8,128)(2,1)}, bf16[272,1024]{1,0:T(8,128)(2,1)}, u32[]{:S(2)}, u32[]{:S(2)}) collective-permute-start(bf16[272,1024]{1,0:T(8,128)(2,1)} %pad_maximum_fusion.6.refs_0_), channel_id=1, source_target_pairs={{0,16},{4,20},{8,24},{12,28},{16,0},{20,4},{24,8},{28,12},{1,17},{... | collective-permute-start | bytes 1671176 | tf_op jit(solution)/shard_map/ppermute | solution.py:37
  52.9 29.0 %collective-permute-start.9 = (bf16[272,1024]{1,0:T(8,128)(2,1)}, bf16[272,1024]{1,0:T(8,128)(2,1)S(1)}, u32[]{:S(2)}, u32[]{:S(2)}) collective-permute-start(bf16[272,1024]{1,0:T(8,128)(2,1)} %pad_maximum_fusion.6.refs_0_), channel_id=1, source_target_pairs={{0,8},{4,12},{8,0},{12,4},{16,24},{20,28},{24,16},{28,20},{1,9},{5... | collective-permute-start | bytes 1671176 | tf_op jit(solution)/shard_map/ppermute | solution.py:37
  81.9 230.8 %reduce-scatter.3.cloned.1.call-start = ((), (), s32[]{:S(2)}) async-start(), calls=%async_computation.2 | async-start | bytes 5242880 | tf_op jit(solution)/shard_map/reduce_scatter | solution.py:1405
  82.3 38.2 %collective-permute-start.21 = (bf16[4,320,512]{2,1,0:T(8,128)(2,1)}, bf16[4,320,512]{2,1,0:T(8,128)(2,1)}, u32[]{:S(2)}, u32[]{:S(2)}) collective-permute-start(bf16[4,320,512]{2,1,0:T(8,128)(2,1)} %bitcast.147), channel_id=1, source_target_pairs={{0,16},{4,20},{8,24},{12,28},{16,0},{20,4},{24,8},{28,12},{1,17},{... | collective-permute-start | bytes 3932168 | tf_op jit(solution)/shard_map/ppermute | solution.py:37
  83.9 36.6 %collective-permute-start.20 = (bf16[4,320,512]{2,1,0:T(8,128)(2,1)}, bf16[4,320,512]{2,1,0:T(8,128)(2,1)}, u32[]{:S(2)}, u32[]{:S(2)}) collective-permute-start(bf16[4,320,512]{2,1,0:T(8,128)(2,1)} %bitcast.148), channel_id=1, source_target_pairs={{0,8},{4,12},{8,0},{12,4},{16,24},{20,28},{24,16},{28,20},{1,9},{5... | collective-permute-start | bytes 3932168 | tf_op jit(solution)/shard_map/ppermute | solution.py:37
  87.5 8.4 %collective-permute-start.16 = (bf16[1024,128]{1,0:T(8,128)(2,1)}, bf16[1024,128]{1,0:T(8,128)(2,1)S(1)}, u32[]{:S(2)}, u32[]{:S(2)}) collective-permute-start(bf16[1024,128]{1,0:T(8,128)(2,1)} %get-tuple-element.464), channel_id=1, source_target_pairs={{0,4},{4,0},{8,12},{12,8},{16,20},{20,16},{24,28},{28,24},{1,5},{5... | collective-permute-start | bytes 786440 | tf_op jit(solution)/shard_map/ppermute | solution.py:37
  96.7 21.9 %collective-permute-start.19 = (bf16[256,256]{1,0:T(8,128)(2,1)S(1)}, bf16[256,256]{1,0:T(8,128)(2,1)S(1)}, u32[]{:S(2)}, u32[]{:S(2)}) collective-permute-start(bf16[256,256]{1,0:T(8,128)(2,1)S(1)} %get-tuple-element.459), channel_id=1, source_target_pairs={{0,24},{4,28},{8,16},{12,20},{16,8},{20,12},{24,0},{28,4},{1,25},{... | collective-permute-start | bytes 393224 | tf_op jit(solution)/shard_map/ppermute | solution.py:37
  96.7 23.8 %collective-permute-start.17 = (bf16[256,256]{1,0:T(8,128)(2,1)S(1)}, bf16[256,256]{1,0:T(8,128)(2,1)S(1)}, u32[]{:S(2)}, u32[]{:S(2)}) collective-permute-start(bf16[256,256]{1,0:T(8,128)(2,1)S(1)} %get-tuple-element.461), channel_id=1, source_target_pairs={{0,8},{4,12},{8,0},{12,4},{16,24},{20,28},{24,16},{28,20},{1,9},{5... | collective-permute-start | bytes 393224 | tf_op jit(solution)/shard_map/ppermute | solution.py:37
  98.4 22.1 %collective-permute-start.18 = (bf16[256,256]{1,0:T(8,128)(2,1)S(1)}, bf16[256,256]{1,0:T(8,128)(2,1)S(1)}, u32[]{:S(2)}, u32[]{:S(2)}) collective-permute-start(bf16[256,256]{1,0:T(8,128)(2,1)S(1)} %get-tuple-element.462), channel_id=1, source_target_pairs={{0,16},{4,20},{8,24},{12,28},{16,0},{20,4},{24,8},{28,12},{1,17},{... | collective-permute-start | bytes 393224 | tf_op jit(solution)/shard_map/ppermute | solution.py:37
  122.9 7.3 %collective-permute-start.32 = (bf16[256,256]{1,0:T(8,128)(2,1)S(1)}, bf16[256,256]{1,0:T(8,128)(2,1)S(1)}, u32[]{:S(2)}, u32[]{:S(2)}) collective-permute-start(bf16[256,256]{1,0:T(8,128)(2,1)S(1)} %get-tuple-element.453), channel_id=1, source_target_pairs={{0,24},{4,28},{8,16},{12,20},{16,8},{20,12},{24,0},{28,4},{1,25},{... | collective-permute-start | bytes 393224 | tf_op jit(solution)/shard_map/ppermute | solution.py:37
  124.2 7.0 %collective-permute-start.30 = (bf16[256,256]{1,0:T(8,128)(2,1)S(1)}, bf16[256,256]{1,0:T(8,128)(2,1)S(1)}, u32[]{:S(2)}, u32[]{:S(2)}) collective-permute-start(bf16[256,256]{1,0:T(8,128)(2,1)S(1)} %get-tuple-element.455), channel_id=1, source_target_pairs={{0,8},{4,12},{8,0},{12,4},{16,24},{20,28},{24,16},{28,20},{1,9},{5... | collective-permute-start | bytes 393224 | tf_op jit(solution)/shard_map/ppermute | solution.py:37
  124.9 7.3 %collective-permute-start.31 = (bf16[256,256]{1,0:T(8,128)(2,1)S(1)}, bf16[256,256]{1,0:T(8,128)(2,1)S(1)}, u32[]{:S(2)}, u32[]{:S(2)}) collective-permute-start(bf16[256,256]{1,0:T(8,128)(2,1)S(1)} %get-tuple-element.456), channel_id=1, source_target_pairs={{0,16},{4,20},{8,24},{12,28},{16,0},{20,4},{24,8},{28,12},{1,17},{... | collective-permute-start | bytes 393224 | tf_op jit(solution)/shard_map/ppermute | solution.py:37
  127.6 22.8 %collective-permute-start.25 = (bf16[4,320,512]{2,1,0:T(8,128)(2,1)}, bf16[4,320,512]{2,1,0:T(8,128)(2,1)}, u32[]{:S(2)}, u32[]{:S(2)}) collective-permute-start(bf16[4,320,512]{2,1,0:T(8,128)(2,1)} %collective-permute-done.20.refs_1_.refs_4_.refs_10_), channel_id=1, source_target_pairs={{0,4},{4,0},{8,12},{12,8},{16,20},{20,16},{24,28},{28,24},{1,5},{5... | collective-permute-start | bytes 3932168 | tf_op jit(solution)/shard_map/ppermute | solution.py:37
  128.8 17.2 %collective-permute-start.23 = (bf16[2,320,512]{2,1,0:T(8,128)(2,1)S(1)}, bf16[2,320,512]{2,1,0:T(8,128)(2,1)S(1)}, u32[]{:S(2)}, u32[]{:S(2)}) collective-permute-start(bf16[2,320,512]{2,1,0:T(8,128)(2,1)S(1)} %slice.269), channel_id=1, source_target_pairs={{0,8},{4,12},{8,0},{12,4},{16,24},{20,28},{24,16},{28,20},{1,9},{5... | collective-permute-start | bytes 1966088 | tf_op jit(solution)/shard_map/ppermute | solution.py:37
  130.2 16.9 %collective-permute-start.22 = (bf16[2,320,512]{2,1,0:T(8,128)(2,1)S(1)}, bf16[2,320,512]{2,1,0:T(8,128)(2,1)S(1)}, u32[]{:S(2)}, u32[]{:S(2)}) collective-permute-start(bf16[2,320,512]{2,1,0:T(8,128)(2,1)S(1)} %slice.268), channel_id=1, source_target_pairs={{0,16},{4,20},{8,24},{12,28},{16,0},{20,4},{24,8},{28,12},{1,17},{... | collective-permute-start | bytes 1966088 | tf_op jit(solution)/shard_map/ppermute | solution.py:37
  131.2 17.9 %collective-permute-start.24 = (bf16[4,320,512]{2,1,0:T(8,128)(2,1)S(1)}, bf16[4,320,512]{2,1,0:T(8,128)(2,1)S(1)}, u32[]{:S(2)}, u32[]{:S(2)}) collective-permute-start(bf16[4,320,512]{2,1,0:T(8,128)(2,1)S(1)} %bitcast.152), channel_id=1, source_target_pairs={{0,4},{4,0},{8,12},{12,8},{16,20},{20,16},{24,28},{28,24},{1,5},{5... | collective-permute-start | bytes 3932168 | tf_op jit(solution)/shard_map/ppermute | solution.py:37
  132.1 18.3 %collective-permute-start.26 = (bf16[4,320,512]{2,1,0:T(8,128)(2,1)}, bf16[4,320,512]{2,1,0:T(8,128)(2,1)}, u32[]{:S(2)}, u32[]{:S(2)}) collective-permute-start(bf16[4,320,512]{2,1,0:T(8,128)(2,1)} %collective-permute-done.21.refs_2_.refs_5_.refs_11_), channel_id=1, source_target_pairs={{0,4},{4,0},{8,12},{12,8},{16,20},{20,16},{24,28},{28,24},{1,5},{5... | collective-permute-start | bytes 3932168 | tf_op jit(solution)/shard_map/ppermute | solution.py:37
  162.9 14.2 %collective-permute-start.34 = (bf16[512,1024]{1,0:T(8,128)(2,1)}, bf16[512,1024]{1,0:T(8,128)(2,1)S(1)}, u32[]{:S(2)}, u32[]{:S(2)}) collective-permute-start(bf16[512,1024]{1,0:T(8,128)(2,1)} %bitcast.158), channel_id=1, source_target_pairs={{0,4},{4,0},{8,12},{12,8},{16,20},{20,16},{24,28},{28,24},{1,5},{5... | collective-permute-start | bytes 3145736 | tf_op jit(solution)/shard_map/ppermute | solution.py:37
  163.3 13.8 %collective-permute-start.33 = (bf16[512,1024]{1,0:T(8,128)(2,1)}, bf16[512,1024]{1,0:T(8,128)(2,1)}, u32[]{:S(2)}, u32[]{:S(2)}) collective-permute-start(bf16[512,1024]{1,0:T(8,128)(2,1)} %bitcast.153), channel_id=1, source_target_pairs={{0,4},{4,0},{8,12},{12,8},{16,20},{20,16},{24,28},{28,24},{1,5},{5... | collective-permute-start | bytes 3145736 | tf_op jit(solution)/shard_map/ppermute | solution.py:37
  177.2 7.6 %collective-permute-start.35 = (bf16[4,4,128,1024]{3,2,1,0:T(8,128)(2,1)}, bf16[4,4,128,1024]{3,2,1,0:T(8,128)(2,1)}, u32[]{:S(2)}, u32[]{:S(2)}) collective-permute-start(bf16[4,4,128,1024]{3,2,1,0:T(8,128)(2,1)} %bitcast.141), channel_id=1, source_target_pairs={{0,4},{4,0},{8,12},{12,8},{16,20},{20,16},{24,28},{28,24},{1,5},{5... | collective-permute-start | bytes 12582920 | tf_op jit(solution)/shard_map/ppermute | solution.py:37
  177.6 22.2 %collective-permute-start.36 = (bf16[512,2048]{1,0:T(8,128)(2,1)}, bf16[512,2048]{1,0:T(8,128)(2,1)}, u32[]{:S(2)}, u32[]{:S(2)}) collective-permute-start(bf16[512,2048]{1,0:T(8,128)(2,1)} %get-tuple-element.276.act_odd), channel_id=1, source_target_pairs={{0,4},{4,0},{8,12},{12,8},{16,20},{20,16},{24,28},{28,24},{1,5},{5... | collective-permute-start | bytes 6291464 | tf_op jit(solution)/shard_map/ppermute | solution.py:37
  212.2 180.4 %reduce-scatter.5.cloned.1.call-start = ((), (), s32[]{:S(2)}) async-start(), calls=%async_computation.3 | async-start | bytes 1740800 | tf_op jit(solution)/shard_map/reduce_scatter | solution.py:1478
  233.8 8.3 %collective-permute-start.38 = (bf16[512,2048]{1,0:T(8,128)(2,1)}, bf16[512,2048]{1,0:T(8,128)(2,1)}, u32[]{:S(2)}, u32[]{:S(2)}) collective-permute-start(bf16[512,2048]{1,0:T(8,128)(2,1)} %get-tuple-element.301), channel_id=1, source_target_pairs={{0,4},{4,0},{8,12},{12,8},{16,20},{20,16},{24,28},{28,24},{1,5},{5... | collective-permute-start | bytes 6291464 | tf_op jit(solution)/shard_map/ppermute | solution.py:37
  236.0 6.1 %collective-permute-start.39 = (bf16[512,1024]{1,0:T(8,128)(2,1)}, bf16[512,1024]{1,0:T(8,128)(2,1)S(1)}, u32[]{:S(2)}, u32[]{:S(2)}) collective-permute-start(bf16[512,1024]{1,0:T(8,128)(2,1)} %get-tuple-element.308.da), channel_id=1, source_target_pairs={{0,4},{4,0},{8,12},{12,8},{16,20},{20,16},{24,28},{28,24},{1,5},{5... | collective-permute-start | bytes 3145736 | tf_op jit(solution)/shard_map/ppermute | solution.py:37
  246.3 16.9 %collective-permute-start.44 = (bf16[512,256]{1,0:T(8,128)(2,1)}, bf16[512,256]{1,0:T(8,128)(2,1)S(1)}, u32[]{:S(2)}, u32[]{:S(2)}) collective-permute-start(bf16[512,256]{1,0:T(8,128)(2,1)} %get-tuple-element.435), channel_id=1, source_target_pairs={{0,24},{4,28},{8,16},{12,20},{16,8},{20,12},{24,0},{28,4},{1,25},{... | collective-permute-start | bytes 786440 | tf_op jit(solution)/shard_map/ppermute | solution.py:37
  246.8 16.3 %collective-permute-start.43 = (bf16[512,256]{1,0:T(8,128)(2,1)}, bf16[512,256]{1,0:T(8,128)(2,1)S(1)}, u32[]{:S(2)}, u32[]{:S(2)}) collective-permute-start(bf16[512,256]{1,0:T(8,128)(2,1)} %get-tuple-element.436), channel_id=1, source_target_pairs={{0,16},{4,20},{8,24},{12,28},{16,0},{20,4},{24,8},{28,12},{1,17},{... | collective-permute-start | bytes 786440 | tf_op jit(solution)/shard_map/ppermute | solution.py:37
  248.1 15.1 %collective-permute-start.42 = (bf16[512,256]{1,0:T(8,128)(2,1)}, bf16[512,256]{1,0:T(8,128)(2,1)S(1)}, u32[]{:S(2)}, u32[]{:S(2)}) collective-permute-start(bf16[512,256]{1,0:T(8,128)(2,1)} %get-tuple-element.437), channel_id=1, source_target_pairs={{0,8},{4,12},{8,0},{12,4},{16,24},{20,28},{24,16},{28,20},{1,9},{5... | collective-permute-start | bytes 786440 | tf_op jit(solution)/shard_map/ppermute | solution.py:37
  263.2 32.1 %collective-permute-start.45 = (bf16[2,544,640]{2,1,0:T(8,128)(2,1)}, bf16[2,544,640]{2,1,0:T(8,128)(2,1)}, u32[]{:S(2)}, u32[]{:S(2)}) collective-permute-start(bf16[2,544,640]{2,1,0:T(8,128)(2,1)} %get-tuple-element.322), channel_id=1, source_target_pairs={{0,16},{4,20},{8,24},{12,28},{16,0},{20,4},{24,8},{28,12},{1,17},{... | collective-permute-start | bytes 4177928 | tf_op jit(solution)/shard_map/ppermute | solution.py:37
  263.3 32.1 %collective-permute-start.46 = (bf16[2,544,640]{2,1,0:T(8,128)(2,1)}, bf16[2,544,640]{2,1,0:T(8,128)(2,1)}, u32[]{:S(2)}, u32[]{:S(2)}) collective-permute-start(bf16[2,544,640]{2,1,0:T(8,128)(2,1)} %get-tuple-element.323), channel_id=1, source_target_pairs={{0,8},{4,12},{8,0},{12,4},{16,24},{20,28},{24,16},{28,20},{1,9},{5... | collective-permute-start | bytes 4177928 | tf_op jit(solution)/shard_map/ppermute | solution.py:37
  306.0 32.1 %collective-permute-start.49 = (bf16[544,640]{1,0:T(8,128)(2,1)}, bf16[544,640]{1,0:T(8,128)(2,1)S(1)}, u32[]{:S(2)}, u32[]{:S(2)}) collective-permute-start(bf16[544,640]{1,0:T(8,128)(2,1)} %slice_bitcast_fusion), channel_id=1, source_target_pairs={{0,16},{4,20},{8,24},{12,28},{16,0},{20,4},{24,8},{28,12},{1,17},{... | collective-permute-start | bytes 2088968 | tf_op jit(solution)/shard_map/ppermute | solution.py:37
  307.7 30.4 %collective-permute-start.48 = (bf16[544,640]{1,0:T(8,128)(2,1)}, bf16[544,640]{1,0:T(8,128)(2,1)S(1)}, u32[]{:S(2)}, u32[]{:S(2)}) collective-permute-start(bf16[544,640]{1,0:T(8,128)(2,1)} %slice_bitcast_fusion.1), channel_id=1, source_target_pairs={{0,8},{4,12},{8,0},{12,4},{16,24},{20,28},{24,16},{28,20},{1,9},{5... | collective-permute-start | bytes 2088968 | tf_op jit(solution)/shard_map/ppermute | solution.py:37
  314.9 23.3 %collective-permute-start.52 = (bf16[128,1024]{1,0:T(8,128)(2,1)}, bf16[128,1024]{1,0:T(8,128)(2,1)S(1)}, u32[]{:S(2)}, u32[]{:S(2)}) collective-permute-start(bf16[128,1024]{1,0:T(8,128)(2,1)} %get-tuple-element.431), channel_id=1, source_target_pairs={{0,24},{4,28},{8,16},{12,20},{16,8},{20,12},{24,0},{28,4},{1,25},{... | collective-permute-start | bytes 786440 | tf_op jit(solution)/shard_map/ppermute | solution.py:37
  316.1 22.0 %collective-permute-start.51 = (bf16[128,1024]{1,0:T(8,128)(2,1)}, bf16[128,1024]{1,0:T(8,128)(2,1)}, u32[]{:S(2)}, u32[]{:S(2)}) collective-permute-start(bf16[128,1024]{1,0:T(8,128)(2,1)} %get-tuple-element.432), channel_id=1, source_target_pairs={{0,16},{4,20},{8,24},{12,28},{16,0},{20,4},{24,8},{28,12},{1,17},{... | collective-permute-start | bytes 786440 | tf_op jit(solution)/shard_map/ppermute | solution.py:37
  317.8 20.3 %collective-permute-start.50 = (bf16[128,1024]{1,0:T(8,128)(2,1)}, bf16[128,1024]{1,0:T(8,128)(2,1)}, u32[]{:S(2)}, u32[]{:S(2)}) collective-permute-start(bf16[128,1024]{1,0:T(8,128)(2,1)} %get-tuple-element.433), channel_id=1, source_target_pairs={{0,8},{4,12},{8,0},{12,4},{16,24},{20,28},{24,16},{28,20},{1,9},{5... | collective-permute-start | bytes 786440 | tf_op jit(solution)/shard_map/ppermute | solution.py:37
  343.0 113.0 %all-gather.11.cloned.1.call-start = ((), (), s32[]{:S(2)}) async-start(), calls=%async_computation.6 | async-start | bytes 3133440 | tf_op jit(solution)/shard_map/all_gather | solution.py:1497
  343.0 18.9 %collective-permute-start.53 = (bf16[256,1024]{1,0:T(8,128)(2,1)}, bf16[256,1024]{1,0:T(8,128)(2,1)S(1)}, u32[]{:S(2)}, u32[]{:S(2)}) collective-permute-start(bf16[256,1024]{1,0:T(8,128)(2,1)} %get-tuple-element.367), channel_id=1, source_target_pairs={{0,8},{4,12},{8,0},{12,4},{16,24},{20,28},{24,16},{28,20},{1,9},{5... | collective-permute-start | bytes 1572872 | tf_op jit(solution)/shard_map/ppermute | solution.py:37
  344.6 24.0 %collective-permute-start.54 = (bf16[256,1024]{1,0:T(8,128)(2,1)}, bf16[256,1024]{1,0:T(8,128)(2,1)S(1)}, u32[]{:S(2)}, u32[]{:S(2)}) collective-permute-start(bf16[256,1024]{1,0:T(8,128)(2,1)} %get-tuple-element.368), channel_id=1, source_target_pairs={{0,16},{4,20},{8,24},{12,28},{16,0},{20,4},{24,8},{28,12},{1,17},{... | collective-permute-start | bytes 1572872 | tf_op jit(solution)/shard_map/ppermute | solution.py:37
  345.0 23.7 %collective-permute-start.55 = (bf16[256,1024]{1,0:T(8,128)(2,1)}, bf16[256,1024]{1,0:T(8,128)(2,1)}, u32[]{:S(2)}, u32[]{:S(2)}) collective-permute-start(bf16[256,1024]{1,0:T(8,128)(2,1)} %get-tuple-element.369), channel_id=1, source_target_pairs={{0,24},{4,28},{8,16},{12,20},{16,8},{20,12},{24,0},{28,4},{1,25},{... | collective-permute-start | bytes 1572872 | tf_op jit(solution)/shard_map/ppermute | solution.py:37
  372.8 15.3 %collective-permute-start.56 = (bf16[1024,1024]{1,0:T(8,128)(2,1)}, bf16[1024,1024]{1,0:T(8,128)(2,1)}, u32[]{:S(2)}, u32[]{:S(2)}) collective-permute-start(bf16[1024,1024]{1,0:T(8,128)(2,1)} %input_part.6), channel_id=1, source_target_pairs={{0,4},{4,0},{8,12},{12,8},{16,20},{20,16},{24,28},{28,24},{1,5},{5... | collective-permute-start | bytes 6291464 | tf_op jit(solution)/shard_map/ppermute | solution.py:37
  372.8 10.1 %collective-permute-start.59 = (bf16[128,1024]{1,0:T(8,128)(2,1)S(1)}, bf16[128,1024]{1,0:T(8,128)(2,1)S(1)}, u32[]{:S(2)}, u32[]{:S(2)}) collective-permute-start(bf16[128,1024]{1,0:T(8,128)(2,1)S(1)} %add_convert_fusion.3.refs_0_), channel_id=1, source_target_pairs={{0,24},{4,28},{8,16},{12,20},{16,8},{20,12},{24,0},{28,4},{1,25},{... | collective-permute-start | bytes 786440 | tf_op jit(solution)/shard_map/ppermute | solution.py:37
  373.9 14.1 %collective-permute-start.58 = (bf16[128,1024]{1,0:T(8,128)(2,1)S(1)}, bf16[128,1024]{1,0:T(8,128)(2,1)}, u32[]{:S(2)}, u32[]{:S(2)}) collective-permute-start(bf16[128,1024]{1,0:T(8,128)(2,1)S(1)} %add_convert_fusion.3.refs_0_), channel_id=1, source_target_pairs={{0,16},{4,20},{8,24},{12,28},{16,0},{20,4},{24,8},{28,12},{1,17},{... | collective-permute-start | bytes 786440 | tf_op jit(solution)/shard_map/ppermute | solution.py:37
  374.8 13.2 %collective-permute-start.57 = (bf16[128,1024]{1,0:T(8,128)(2,1)S(1)}, bf16[128,1024]{1,0:T(8,128)(2,1)}, u32[]{:S(2)}, u32[]{:S(2)}) collective-permute-start(bf16[128,1024]{1,0:T(8,128)(2,1)S(1)} %add_convert_fusion.3.refs_0_), channel_id=1, source_target_pairs={{0,8},{4,12},{8,0},{12,4},{16,24},{20,28},{24,16},{28,20},{1,9},{5... | collective-permute-start | bytes 786440 | tf_op jit(solution)/shard_map/ppermute | solution.py:37
  392.7 5.8 %collective-permute-start.65 = (bf16[128,1024]{1,0:T(8,128)(2,1)}, bf16[128,1024]{1,0:T(8,128)(2,1)S(1)}, u32[]{:S(2)}, u32[]{:S(2)}) collective-permute-start(bf16[128,1024]{1,0:T(8,128)(2,1)} %collective-permute-done.57.refs_1_), channel_id=1, source_target_pairs={{0,4},{4,0},{8,12},{12,8},{16,20},{20,16},{24,28},{28,24},{1,5},{5... | collective-permute-start | bytes 786440 | tf_op jit(solution)/shard_map/ppermute | solution.py:37
  393.2 5.3 %collective-permute-start.66 = (bf16[128,1024]{1,0:T(8,128)(2,1)}, bf16[128,1024]{1,0:T(8,128)(2,1)S(1)}, u32[]{:S(2)}, u32[]{:S(2)}) collective-permute-start(bf16[128,1024]{1,0:T(8,128)(2,1)} %collective-permute-done.58.refs_2_), channel_id=1, source_target_pairs={{0,4},{4,0},{8,12},{12,8},{16,20},{20,16},{24,28},{28,24},{1,5},{5... | collective-permute-start | bytes 786440 | tf_op jit(solution)/shard_map/ppermute | solution.py:37
  394.1 25.6 %collective-permute-start.61 = (bf16[256,1024]{1,0:T(8,128)(2,1)}, bf16[256,1024]{1,0:T(8,128)(2,1)S(1)}, u32[]{:S(2)}, u32[]{:S(2)}) collective-permute-start(bf16[256,1024]{1,0:T(8,128)(2,1)} %get-tuple-element.392), channel_id=1, source_target_pairs={{0,8},{4,12},{8,0},{12,4},{16,24},{20,28},{24,16},{28,20},{1,9},{5... | collective-permute-start | bytes 1572872 | tf_op jit(solution)/shard_map/ppermute | solution.py:37
  394.8 29.3 %collective-permute-start.62 = (bf16[256,1024]{1,0:T(8,128)(2,1)}, bf16[256,1024]{1,0:T(8,128)(2,1)}, u32[]{:S(2)}, u32[]{:S(2)}) collective-permute-start(bf16[256,1024]{1,0:T(8,128)(2,1)} %get-tuple-element.393), channel_id=1, source_target_pairs={{0,16},{4,20},{8,24},{12,28},{16,0},{20,4},{24,8},{28,12},{1,17},{... | collective-permute-start | bytes 1572872 | tf_op jit(solution)/shard_map/ppermute | solution.py:37
  395.9 28.2 %collective-permute-start.63 = (bf16[256,1024]{1,0:T(8,128)(2,1)}, bf16[256,1024]{1,0:T(8,128)(2,1)}, u32[]{:S(2)}, u32[]{:S(2)}) collective-permute-start(bf16[256,1024]{1,0:T(8,128)(2,1)} %get-tuple-element.394), channel_id=1, source_target_pairs={{0,24},{4,28},{8,16},{12,20},{16,8},{20,12},{24,0},{28,4},{1,25},{... | collective-permute-start | bytes 1572872 | tf_op jit(solution)/shard_map/ppermute | solution.py:37
  398.5 21.2 %collective-permute-start.60 = (bf16[2,272,384]{2,1,0:T(8,128)(2,1)}, bf16[2,272,384]{2,1,0:T(8,128)(2,1)S(1)}, u32[]{:S(2)}, u32[]{:S(2)}) collective-permute-start(bf16[2,272,384]{2,1,0:T(8,128)(2,1)} %pad_maximum_fusion.8), channel_id=1, source_target_pairs={{0,2},{1,3},{2,0},{3,1},{4,6},{5,7},{6,4},{7,5},{8,10},{9,11},{10,... | collective-permute-start | bytes 1253384 | tf_op jit(solution)/shard_map/ppermute | solution.py:37
  425.2 6.6 %collective-permute-start.68 = (bf16[1,272,384]{2,1,0:T(8,128)(2,1)S(1)}, bf16[1,272,384]{2,1,0:T(8,128)(2,1)S(1)}, u32[]{:S(2)}, u32[]{:S(2)}) collective-permute-start(bf16[1,272,384]{2,1,0:T(8,128)(2,1)S(1)} %slice.358), channel_id=1, source_target_pairs={{0,1},{1,0},{2,3},{3,2},{4,5},{5,4},{6,7},{7,6},{8,9},{9,8},{10,11... | collective-permute-start | bytes 626696 | tf_op jit(solution)/shard_map/ppermute | solution.py:37
  432.1 9.1 %collective-permute-start.71 = (bf16[272,384]{1,0:T(8,128)(2,1)S(1)}, bf16[272,384]{1,0:T(8,128)(2,1)S(1)}, u32[]{:S(2)}, u32[]{:S(2)}) collective-permute-start(bf16[272,384]{1,0:T(8,128)(2,1)S(1)} %maximum_maximum_fusion.refs_0_), channel_id=1, source_target_pairs={{0,24},{4,28},{8,16},{12,20},{16,8},{20,12},{24,0},{28,4},{1,25},{... | collective-permute-start | bytes 626696 | tf_op jit(solution)/shard_map/ppermute | solution.py:37
  433.6 10.2 %collective-permute-start.70 = (bf16[272,384]{1,0:T(8,128)(2,1)S(1)}, bf16[272,384]{1,0:T(8,128)(2,1)S(1)}, u32[]{:S(2)}, u32[]{:S(2)}) collective-permute-start(bf16[272,384]{1,0:T(8,128)(2,1)S(1)} %maximum_maximum_fusion.refs_0_), channel_id=1, source_target_pairs={{0,16},{4,20},{8,24},{12,28},{16,0},{20,4},{24,8},{28,12},{1,17},{... | collective-permute-start | bytes 626696 | tf_op jit(solution)/shard_map/ppermute | solution.py:37
  434.7 9.1 %collective-permute-start.69 = (bf16[272,384]{1,0:T(8,128)(2,1)S(1)}, bf16[272,384]{1,0:T(8,128)(2,1)S(1)}, u32[]{:S(2)}, u32[]{:S(2)}) collective-permute-start(bf16[272,384]{1,0:T(8,128)(2,1)S(1)} %maximum_maximum_fusion.refs_0_), channel_id=1, source_target_pairs={{0,8},{4,12},{8,0},{12,4},{16,24},{20,28},{24,16},{28,20},{1,9},{5... | collective-permute-start | bytes 626696 | tf_op jit(solution)/shard_map/ppermute | solution.py:37
  435.7 13.3 %collective-permute-start.72 = (bf16[272,384]{1,0:T(8,128)(2,1)S(1)}, bf16[272,384]{1,0:T(8,128)(2,1)S(1)}, u32[]{:S(2)}, u32[]{:S(2)}) collective-permute-start(bf16[272,384]{1,0:T(8,128)(2,1)S(1)} %maximum_maximum_fusion.refs_0_), channel_id=1, source_target_pairs={{0,4},{4,0},{8,12},{12,8},{16,20},{20,16},{24,28},{28,24},{1,5},{5... | collective-permute-start | bytes 626696 | tf_op jit(solution)/shard_map/ppermute | solution.py:37
  441.2 7.8 %collective-permute-start.75 = (bf16[272,384]{1,0:T(8,128)(2,1)S(1)}, bf16[272,384]{1,0:T(8,128)(2,1)S(1)}, u32[]{:S(2)}, u32[]{:S(2)}) collective-permute-start(bf16[272,384]{1,0:T(8,128)(2,1)S(1)} %collective-permute-done.71.refs_3_), channel_id=1, source_target_pairs={{0,4},{4,0},{8,12},{12,8},{16,20},{20,16},{24,28},{28,24},{1,5},{5... | collective-permute-start | bytes 626696 | tf_op jit(solution)/shard_map/ppermute | solution.py:37
  443.8 6.7 %collective-permute-start.73 = (bf16[272,384]{1,0:T(8,128)(2,1)S(1)}, bf16[272,384]{1,0:T(8,128)(2,1)}, u32[]{:S(2)}, u32[]{:S(2)}) collective-permute-start(bf16[272,384]{1,0:T(8,128)(2,1)S(1)} %collective-permute-done.69.refs_1_), channel_id=1, source_target_pairs={{0,4},{4,0},{8,12},{12,8},{16,20},{20,16},{24,28},{28,24},{1,5},{5... | collective-permute-start | bytes 626696 | tf_op jit(solution)/shard_map/ppermute | solution.py:37
  (92 other events, 599.4 us)
Sparse Core Ops, SparseCore 0:
  45.1 33.6 all-gather.6
  82.0 81.7 all-gather.8
  212.3 76.8 reduce-scatter.2
  343.1 32.8 reduce-scatter.4
  392.7 44.4 all-gather.10
